TPU v7x, 256 devices: a whole 4x4x8 slice. The times are simulated.
256 devices in a mesh: row: 32 (over z, x_hi, core), col: 8 (over y, x_lo).
Axes of the slice: x: 4 (x_hi: 2, x_lo: 2; x = x_hi * 2 + x_lo), y: 4, z: 8, core: 2. Of those that a mesh axis runs over, the one named last changes fastest.
Arguments:
- tokens: bfloat16 [512, 128, 1024], P('row', 'col'), may hold values from -6 to 6
- grad_out: bfloat16 [512, 128, 1024], P('row', 'col'), may hold values from -6 to 6
- w_qkv: bfloat16 [1024, 3072], replicated, may hold values from -1 to 1
- w_proj: bfloat16 [1024, 1024], replicated, may hold values from -0.1875 to 0.1875
- norm_gain: float32 [1024], replicated, may hold values from 0.1 to 1.9
- logit_scale: float32 [32], replicated, may hold values from 5 to 128
Outputs:
- grad_tokens: bfloat16 [512, 128, 1024], P('row', 'col')
- grad_wvalue: float32 [1024, 1024], P(('row', 'col'))
- grad_wproj: float32 [1024, 1024], P(('row', 'col'))
All inputs are finite; a program needn't handle non-finite values.
Results may differ from a plain program's by a relative error of at most 0.018.
The roundings to bfloat16 on the way count: a program that leaves them out, or rounds other values in their place, can miss the bound.
Values may be sent and summed in bfloat16 or wider, within the bound.
No kernel may reach another device: no remote copies, remote signals or barrier semaphores. Data moves between devices by JAX's collectives and lax.ppermute only.
A program may use at most 128 MiB of HBM per device.

v0:
```python
import jax
import jax.numpy as jnp
from jax import lax
from jax.sharding import PartitionSpec as P

HEADS = 32
WIN = 16


EPS_NORM = 1e-06
EPS_LN = 1e-05


def passed_along(array, axis, by):
    devices = lax.axis_size(axis)
    return lax.ppermute(array, axis, [(i, (i + by) % devices) for i in range(devices)])


def mixed_einsum(form, left, right):
    return jnp.einsum(form, left, right, preferred_element_type=jnp.float32)


def unit_heads(s_win, w_qkv):
    width = w_qkv.shape[0]
    tokens_win = s_win.shape[0]
    head_dim = width // HEADS
    projected = jnp.dot(s_win, w_qkv, preferred_element_type=jnp.float32)
    query_raw = projected[:, :width].reshape(tokens_win, HEADS, head_dim)
    key_raw = projected[:, width : 2 * width].reshape(tokens_win, HEADS, head_dim)
    value_raw = projected[:, 2 * width :].reshape(tokens_win, HEADS, head_dim)
    query_scale = lax.rsqrt(jnp.sum(query_raw * query_raw, axis=-1, keepdims=True) + EPS_NORM)
    key_scale = lax.rsqrt(jnp.sum(key_raw * key_raw, axis=-1, keepdims=True) + EPS_NORM)
    return (query_raw * query_scale, key_raw * key_scale, value_raw, query_scale, key_scale)


def soft_scores(query_bf, key_bf, label, logit_scale):
    same = (label[:, None] == label[None, :])[None]
    logits = logit_scale[:, None, None] * mixed_einsum("qhd,khd->hqk", query_bf, key_bf)
    logits = jnp.where(same, logits, jnp.float32(-1000000000.0))
    top = jnp.max(logits, axis=-1, keepdims=True)
    expo = jnp.exp(logits - top)
    return expo / jnp.sum(expo, axis=-1, keepdims=True)


def output_grads(s_win, g_win, label, w_qkv, w_proj, norm_gain, logit_scale):
    width = w_qkv.shape[0]
    tokens_win = s_win.shape[0]
    query_unit, key_unit, value_raw, query_scale, key_scale = unit_heads(s_win, w_qkv)
    value_bf = value_raw.astype(jnp.bfloat16)
    probs = soft_scores(
        query_unit.astype(jnp.bfloat16), key_unit.astype(jnp.bfloat16), label, logit_scale
    )
    probs_bf = probs.astype(jnp.bfloat16)
    attended = mixed_einsum("hqk,khd->qhd", probs_bf, value_bf)
    attended_bf = attended.reshape(tokens_win, width).astype(jnp.bfloat16)
    mixed = jnp.dot(attended_bf, w_proj, preferred_element_type=jnp.float32)
    center = mixed - jnp.mean(mixed, axis=-1, keepdims=True)
    inv_std = lax.rsqrt(jnp.mean(center * center, axis=-1, keepdims=True) + EPS_LN)
    normed = center * inv_std
    grad_y = g_win.astype(jnp.float32)
    grad_norm = grad_y * norm_gain[None, :]
    grad_mix = inv_std * (
        grad_norm
        - jnp.mean(grad_norm, axis=-1, keepdims=True)
        - normed * jnp.mean(grad_norm * normed, axis=-1, keepdims=True)
    )
    grad_mix_bf = grad_mix.astype(jnp.bfloat16)
    proj_term = jnp.dot(attended_bf.T, grad_mix_bf, preferred_element_type=jnp.float32)
    grad_att_bf = jnp.dot(grad_mix_bf, w_proj.T, preferred_element_type=jnp.float32).astype(
        jnp.bfloat16
    )
    kept_parts = (
        jnp.concatenate(
            [query_unit.reshape(tokens_win, width), key_unit.reshape(tokens_win, width)], axis=1
        ),
        value_bf.reshape(tokens_win, width),
        jnp.concatenate([query_scale[:, :, 0], key_scale[:, :, 0]], axis=1),
    )
    return (grad_att_bf, kept_parts, proj_term)


def input_grads(s_win, grad_att_bf, label, kept_parts, w_qkv, logit_scale):
    width = w_qkv.shape[0]
    tokens_win = s_win.shape[0]
    head_dim = width // HEADS
    unit_pair, value_flat, scales = kept_parts
    query_unit = unit_pair[:, :width].reshape(tokens_win, HEADS, head_dim)
    key_unit = unit_pair[:, width:].reshape(tokens_win, HEADS, head_dim)
    value_bf = value_flat.reshape(tokens_win, HEADS, head_dim)
    query_scale = scales[:, :HEADS, None]
    key_scale = scales[:, HEADS:, None]
    query_bf = query_unit.astype(jnp.bfloat16)
    key_bf = key_unit.astype(jnp.bfloat16)
    probs = soft_scores(query_bf, key_bf, label, logit_scale)
    probs_bf = probs.astype(jnp.bfloat16)
    grad_att_heads = grad_att_bf.reshape(tokens_win, HEADS, head_dim)
    grad_value = mixed_einsum("hqk,qhd->khd", probs_bf, grad_att_heads)
    grad_prob = mixed_einsum("qhd,khd->hqk", grad_att_heads, value_bf)
    grad_score = probs * (grad_prob - jnp.sum(grad_prob * probs, axis=-1, keepdims=True))
    grad_score_bf = (logit_scale[:, None, None] * grad_score).astype(jnp.bfloat16)
    grad_qunit = mixed_einsum("hqk,khd->qhd", grad_score_bf, key_bf)
    grad_kunit = mixed_einsum("hqk,qhd->khd", grad_score_bf, query_bf)
    grad_query = query_scale * (
        grad_qunit - query_unit * jnp.sum(grad_qunit * query_unit, axis=-1, keepdims=True)
    )
    grad_key = key_scale * (
        grad_kunit - key_unit * jnp.sum(grad_kunit * key_unit, axis=-1, keepdims=True)
    )
    grad_qkv_bf = jnp.concatenate(
        [
            grad_query.reshape(tokens_win, width),
            grad_key.reshape(tokens_win, width),
            grad_value.reshape(tokens_win, width),
        ],
        axis=1,
    ).astype(jnp.bfloat16)
    value_term = jnp.dot(s_win.T, grad_qkv_bf[:, 2 * width :], preferred_element_type=jnp.float32)
    grad_input_bf = jnp.dot(grad_qkv_bf, w_qkv.T, preferred_element_type=jnp.float32).astype(
        jnp.bfloat16
    )
    return (grad_input_bf, value_term)


def per_device(tokens, grad_out, w_qkv, w_proj, norm_gain, logit_scale):
    half_win = WIN // 2
    tile_cols = tokens.shape[1]
    width = tokens.shape[2]
    count = tile_cols // WIN
    pair = (tokens, grad_out)
    strip = passed_along((pair[0][:half_win], pair[1][:half_win]), "row", -1)
    col_pair = (
        jnp.concatenate([pair[0][half_win:], strip[0]], axis=0),
        jnp.concatenate([pair[1][half_win:], strip[1]], axis=0),
    )
    col_strip = passed_along((col_pair[0][:, :half_win], col_pair[1][:, :half_win]), "col", -1)
    shifted = jnp.concatenate([col_pair[0][:, half_win:], col_strip[0]], axis=1)
    grad_shift = jnp.concatenate([col_pair[1][:, half_win:], col_strip[1]], axis=1)
    grid_rows = WIN * lax.axis_size("row")
    grid_cols = tile_cols * lax.axis_size("col")
    row_ids = lax.axis_index("row") * WIN + jnp.arange(WIN, dtype=jnp.int32)
    col_ids = lax.axis_index("col") * tile_cols + jnp.arange(tile_cols, dtype=jnp.int32)
    row_label = jnp.where(
        row_ids < grid_rows - WIN, 0, jnp.where(row_ids < grid_rows - half_win, 1, 2)
    )
    col_label = jnp.where(
        col_ids < grid_cols - WIN, 0, jnp.where(col_ids < grid_cols - half_win, 1, 2)
    )
    labels = (3 * row_label[:, None] + col_label[None, :]).astype(jnp.int32)

    def windows(array):
        return (
            array.reshape(WIN, count, WIN, -1).transpose(1, 0, 2, 3).reshape(count, WIN * WIN, -1)
        )

    s_stack = windows(shifted)
    g_stack = windows(grad_shift)
    label_stack = windows(labels[:, :, None])[:, :, 0]

    def first_pass(carry, item):
        s_win, g_win, label = item
        grad_att_bf, kept_parts, proj_term = output_grads(
            s_win, g_win, label, w_qkv, w_proj, norm_gain, logit_scale
        )
        return (carry + proj_term, (grad_att_bf, kept_parts[0], kept_parts[1], kept_parts[2]))

    grad_proj, (att_stack, unit_stack, value_stack, scale_stack) = lax.scan(
        first_pass, jnp.zeros((width, width), jnp.float32), (s_stack, g_stack, label_stack)
    )

    def second_pass(carry, item):
        s_win, grad_att_bf, label, unit_pair, value_flat, scales = item
        grad_input_bf, value_term = input_grads(
            s_win, grad_att_bf, label, (unit_pair, value_flat, scales), w_qkv, logit_scale
        )
        return (carry + value_term, grad_input_bf)

    grad_value_w, input_stack = lax.scan(
        second_pass,
        jnp.zeros((width, width), jnp.float32),
        (s_stack, att_stack, label_stack, unit_stack, value_stack, scale_stack),
    )
    value_part, proj_part = (
        lax.psum_scatter(grad_value_w, ("row", "col"), scatter_dimension=0, tiled=True),
        lax.psum_scatter(grad_proj, ("row", "col"), scatter_dimension=0, tiled=True),
    )
    grid = (
        input_stack.reshape(count, WIN, WIN, width)
        .transpose(1, 0, 2, 3)
        .reshape(WIN, tile_cols, width)
    )
    strip = passed_along(grid[WIN - half_win :], "row", 1)
    grid = jnp.concatenate([strip, grid[: WIN - half_win]], axis=0)
    strip = passed_along(grid[:, tile_cols - half_win :], "col", 1)
    grid = jnp.concatenate([strip, grid[:, : tile_cols - half_win]], axis=1)
    grad_tokens = (grad_out.astype(jnp.float32) + grid.astype(jnp.float32)).astype(jnp.bfloat16)
    return (grad_tokens, value_part, proj_part)


def solution(mesh):
    in_specs = (P("row", "col", None), P("row", "col", None), P(), P(), P(), P())
    out_specs = (P("row", "col", None), P(("row", "col"), None), P(("row", "col"), None))
    return jax.shard_map(
        per_device, mesh=mesh, in_specs=in_specs, out_specs=out_specs, check_vma=False
    )
```

profile of v0, /device:TPU:1, one launch (start us, length us, event | category | flops | bytes accessed | tf_op | source)
XLA Modules:
  0.0 382.4 jit_solution(5915971700402391392)
XLA Ops:
  7.2 1.9 fusion.78
  9.1 3.2 collective-permute-start
  13.5 6.1 %collective-permute-start.2 = (bf16[8,16,1024]{2,1,0:T(8,128)(2,1)S(1)}, bf16[8,16,1024]{2,1,0:T(8,128)(2,1)S(1)}, u32[]{:S(2)}, u32[]{:S(2)}) collective-permute-start(bf16[8,16,1024]{2,1,0:T(8,128)(2,1)S(1)} %get-tuple-element.62), channel_id=1, source_target_pairs={{0,248},{8,0},{16,8},{24,16},{32,24},{40,32},{48,40},{56,48},{64,5... | collective-permute-start | bytes 786440 | tf_op jit(solution)/shard_map/ppermute | solution.py:16
  21.4 2.8 collective-permute-start.1
  27.6 4.8 %fusion.88 = f32[256,3072]{1,0:T(8,128)S(1)} fusion(bf16[256,1024]{1,0:T(8,128)(2,1)S(1)} %bitcast.75, bf16[1024,3072]{1,0:T(8,128)(2,1)} %param.8), kind=kOutput, calls=%fused_computation.110 | convolution fusion | flops 1610612736 | bytes 9961472 | tf_op jit(solution)/shard_map/while/body/eval_jaxpr/dot_general | solution.py:27
  32.5 1.6 copy-done.3
  36.1 1.6 copy.34
  39.1 1.6 copy.35
  40.6 3.4 slice_multiply_fusion
  46.6 8.3 %fusion.79 = (f32[32,256]{1,0:T(8,128)}, f32[32,256,256]{1,2,0:T(8,128)}) fusion(f32[32]{0:T(128)S(1)} %copy-done.17, pred[256,256]{0,1:T(8,128)(4,1)S(1)} %broadcast_compare_fusion, bf16[256,32,32]{0,2,1:T(8,128)(2,1)} %multiply_convert_fusion.3, f32[256,32,32]{0,2,1:T(8,128)} %bitcast.65, f32[256,32]{0,1:T(8,128)S(1)} %add_rsqrt_fusion), kind=kOutput, calls=%fused_computation.107 | convolution fusion | flops 143130880 | bytes 10092672 | tf_op jit(solution)/shard_map/while/body/eval_jaxpr/sub | solution.py:41
  55.0 4.3 %fusion.46 = bf16[32,32,256]{2,1,0:T(8,128)(2,1)S(1)} fusion(bf16[256,32,32]{0,2,1:T(8,128)(2,1)} %bitcast.73, f32[32,256,256]{1,2,0:T(8,128)} %get-tuple-element.79, f32[32,256]{1,0:T(8,128)} %get-tuple-element.78), kind=kOutput, calls=%fused_computation.42 | convolution fusion | flops 138674176 | bytes 9469952 | tf_op jit(solution)/shard_map/while/body/eval_jaxpr/hqk,khd->qhd/dot_general | solution.py:20
  64.7 1.7 multiply_convert_fusion.1
  67.9 3.8 fusion.91
  73.1 7.6 %fusion.81 = (f32[32,256]{1,0:T(8,128)S(1)}, f32[32,256,256]{1,2,0:T(8,128)}) fusion(f32[32]{0:T(128)S(1)} %copy-done.18, pred[256,256]{0,1:T(8,128)(4,1)S(1)} %broadcast_compare_fusion, bf16[256,32,32]{0,2,1:T(8,128)(2,1)} %multiply_convert_fusion.3, f32[256,1024]{0,1:T(8,128)S(1)} %copy.36), kind=kOutput, calls=%fused_computation.109 | convolution fusion | flops 142606592 | bytes 10059904 | tf_op jit(solution)/shard_map/while/body/eval_jaxpr/sub | solution.py:41
  80.7 4.8 %fusion.47 = bf16[32,32,256]{2,1,0:T(8,128)(2,1)S(1)} fusion(bf16[256,32,32]{0,2,1:T(8,128)(2,1)S(1)} %bitcast.78, f32[32,256,256]{1,2,0:T(8,128)} %get-tuple-element.83, f32[32,256]{1,0:T(8,128)S(1)} %get-tuple-element.82), kind=kOutput, calls=%fused_computation.43 | convolution fusion | flops 138674176 | bytes 9469952 | tf_op jit(solution)/shard_map/while/body/eval_jaxpr/hqk,qhd->khd/dot_general | solution.py:20
  86.3 2.7 fusion.90
  89.1 5.5 %fusion.89 = f32[32,256,256]{1,2,0:T(8,128)} fusion(bf16[256,32,32]{0,2,1:T(8,128)(2,1)} %bitcast.77, bf16[256,32,32]{0,2,1:T(8,128)(2,1)S(1)} %bitcast.74), kind=kOutput, calls=%fused_computation.111 | convolution fusion | flops 134217728 | bytes 9437184 | tf_op jit(solution)/shard_map/while/body/eval_jaxpr/qhd,khd->hqk/dot_general | solution.py:20
  94.6 12.9 %fusion.34 = f32[256,32,32]{0,2,1:T(8,128)S(1)} fusion(bf16[256,32,32]{0,2,1:T(8,128)(2,1)} %multiply_convert_fusion.3, f32[32,256,256]{1,2,0:T(8,128)} %fusion.89, f32[32]{0:T(128)S(1)} %copy-done.18, f32[32,256,256]{1,2,0:T(8,128)} %get-tuple-element.83, f32[32,256]{1,0:T(8,128)S(1)} %get-tuple-element.82), kind=kOutput, calls=%fused_computation.34 | convolution fusion | flops 148906240 | bytes 18382976 | tf_op jit(solution)/shard_map/while/body/eval_jaxpr/hqk,qhd->khd/dot_general | solution.py:20
  107.5 14.3 %fusion.31 = f32[256,32,32]{0,2,1:T(8,128)} fusion(f32[32,256,256]{1,2,0:T(8,128)} %fusion.89, f32[32]{0:T(128)S(1)} %copy-done.18, f32[256,32,32]{0,2,1:T(8,128)S(1)} %bitcast.67, f32[32,256,256]{1,2,0:T(8,128)} %get-tuple-element.83, f32[32,256]{1,0:T(8,128)S(1)} %get-tuple-element.82), kind=kOutput, calls=%fused_computation.33 | convolution fusion | flops 148906240 | bytes 18907264 | tf_op jit(solution)/shard_map/while/body/eval_jaxpr/hqk,khd->qhd/dot_general | solution.py:20
  122.1 2.0 fusion.51
  124.2 5.0 %fusion.43 = bf16[256,1024]{1,0:T(8,128)(2,1)S(1)} fusion(bf16[1024,3072]{1,0:T(8,128)(2,1)} %param.8, bf16[256,1024]{0,1:T(8,128)(2,1)} %bitcast.80, bf16[256,1024]{0,1:T(8,128)(2,1)S(1)} %bitcast.81, bf16[256,1024]{0,1:T(8,128)(2,1)S(1)} %bitcast.82), kind=kOutput, calls=%fused_computation.41 | convolution fusion | flops 1615593472 | bytes 8388608 | tf_op jit(solution)/shard_map/while/body/eval_jaxpr/dot_general | solution.py:118
  129.9 7.1 %collective-permute-done.4 = bf16[8,16,1024]{2,1,0:T(8,128)(2,1)S(1)} collective-permute-done((bf16[8,16,1024]{2,1,0:T(8,128)(2,1)S(1)}, bf16[8,16,1024]{2,1,0:T(8,128)(2,1)S(1)}, u32[]{:S(2)}, u32[]{:S(2)}) %collective-permute-start.4) | collective-permute-done | bytes 262176 | tf_op jit(solution)/shard_map/ppermute | solution.py:16
  138.3 9.2 %collective-permute-done.5 = bf16[16,8,1024]{2,1,0:T(8,128)(2,1)S(1)} collective-permute-done((bf16[16,8,1024]{2,1,0:T(8,128)(2,1)}, bf16[16,8,1024]{2,1,0:T(8,128)(2,1)S(1)}, u32[]{:S(2)}, u32[]{:S(2)}) %collective-permute-start.5) | collective-permute-done | bytes 262176 | tf_op jit(solution)/shard_map/ppermute | solution.py:16
  148.5 224.3 %all-reduce.5.cloned.1.call-done = (f32[1024,1024]{1,0:T(8,128)}, f32[1024,1024]{1,0:T(8,128)}) async-done(((f32[1024,1024]{1,0:T(8,128)}, f32[1024,1024]{1,0:T(8,128)}), (f32[1024,1024]{1,0:T(8,128)}, f32[1024,1024]{1,0:T(8,128)})) %all-reduce.5.cloned.1.call-update) | async-done | bytes 8388624
  (82 shorter events, 27.5 us)
Async XLA Ops:
  7.2 52.1 %copy-start = (bf16[1024,1024]{1,0:T(8,128)(2,1)S(1)}, bf16[1024,1024]{1,0:T(8,128)(2,1)}, u32[]{:S(2)}) copy-start(bf16[1024,1024]{1,0:T(8,128)(2,1)} %param.9) | copy-start | bytes 6291460
  7.2 365.6 %all-reduce.5.cloned.1.call-start = ((), (), s32[]{:S(2)}) async-start(), calls=%async_computation | async-start | bytes 16777216
  9.1 10.6 %collective-permute-start = (bf16[8,16,1024]{2,1,0:T(8,128)(2,1)}, bf16[8,16,1024]{2,1,0:T(8,128)(2,1)S(1)}, u32[]{:S(2)}, u32[]{:S(2)}) collective-permute-start(bf16[8,16,1024]{2,1,0:T(8,128)(2,1)} %get-tuple-element.77), channel_id=1, source_target_pairs={{0,248},{8,0},{16,8},{24,16},{32,24},{40,32},{48,40},{56,48},{64,5... | collective-permute-start | bytes 786440 | tf_op jit(solution)/shard_map/ppermute | solution.py:16
  13.5 10.9 %collective-permute-start.2 = (bf16[8,16,1024]{2,1,0:T(8,128)(2,1)S(1)}, bf16[8,16,1024]{2,1,0:T(8,128)(2,1)S(1)}, u32[]{:S(2)}, u32[]{:S(2)}) collective-permute-start(bf16[8,16,1024]{2,1,0:T(8,128)(2,1)S(1)} %get-tuple-element.62), channel_id=1, source_target_pairs={{0,248},{8,0},{16,8},{24,16},{32,24},{40,32},{48,40},{56,48},{64,5... | collective-permute-start | bytes 786440 | tf_op jit(solution)/shard_map/ppermute | solution.py:16
  21.4 6.2 %collective-permute-start.1 = (bf16[16,8,1024]{2,1,0:T(8,128)(2,1)S(1)}, bf16[16,8,1024]{2,1,0:T(8,128)(2,1)S(1)}, u32[]{:S(2)}, u32[]{:S(2)}) collective-permute-start(bf16[16,8,1024]{2,1,0:T(8,128)(2,1)S(1)} %get-tuple-element.75), channel_id=1, source_target_pairs={{0,7},{1,0},{2,1},{3,2},{4,3},{5,4},{6,5},{7,6},{8,15},{9,8},{10,9... | collective-permute-start | bytes 786440 | tf_op jit(solution)/shard_map/ppermute | solution.py:16
  25.2 35.2 %collective-permute-start.3 = (bf16[16,8,1024]{2,1,0:T(8,128)(2,1)}, bf16[16,8,1024]{2,1,0:T(8,128)(2,1)}, u32[]{:S(2)}, u32[]{:S(2)}) collective-permute-start(bf16[16,8,1024]{2,1,0:T(8,128)(2,1)} %get-tuple-element.60), channel_id=1, source_target_pairs={{0,7},{1,0},{2,1},{3,2},{4,3},{5,4},{6,5},{7,6},{8,15},{9,8},{10,9... | collective-permute-start | bytes 786440 | tf_op jit(solution)/shard_map/ppermute | solution.py:16
  27.6 7.5 %copy-start.9 = (bf16[16,16,1024]{2,1,0:T(8,128)(2,1)}, bf16[16,16,1024]{2,1,0:T(8,128)(2,1)S(1)}, u32[]{:S(2)}) copy-start(bf16[16,16,1024]{2,1,0:T(8,128)(2,1)S(1)} %pad_maximum_fusion.1) | copy-start | bytes 1572868
  32.4 1.7 copy-start.3
  36.1 10.5 %copy-start.17 = (f32[32]{0:T(128)S(1)}, f32[32]{0:T(128)}, u32[]{:S(2)}) copy-start(f32[32]{0:T(128)} %param.11) | copy-start | bytes 388
  37.7 1.3 copy-start.5
  55.0 6.1 %copy-start.15 = (f32[1024]{0:T(1024)S(1)}, f32[1024]{0:T(1024)}, u32[]{:S(2)}) copy-start(f32[1024]{0:T(1024)} %param.10) | copy-start | bytes 12292
  59.2 3.1 copy-start.6
  60.1 1.0 copy-start.2
  60.4 2.6 copy-start.16
  64.7 8.4 %copy-start.18 = (f32[32]{0:T(128)S(1)}, f32[32]{0:T(128)}, u32[]{:S(2)}) copy-start(f32[32]{0:T(128)} %param.11) | copy-start | bytes 388
  67.9 3.8 copy-start.13
  67.9 4.8 %copy-start.4 = (f32[256,1024]{1,0:T(8,128)S(1)}, f32[256,1024]{1,0:T(8,128)}, u32[]{:S(2)}) copy-start(f32[256,1024]{1,0:T(8,128)} %get-tuple-element.55) | copy-start | bytes 3145732
  73.1 7.7 %copy-start.11 = (bf16[256,1024]{0,1:T(8,128)(2,1)S(1)}, bf16[256,1024]{0,1:T(8,128)(2,1)}, u32[]{:S(2)}) copy-start(bf16[256,1024]{0,1:T(8,128)(2,1)} %copy.39) | copy-start | bytes 1572868
  80.7 5.6 %copy-start.10 = (bf16[16,16,1024]{2,1,0:T(8,128)(2,1)S(1)}, bf16[16,16,1024]{2,1,0:T(8,128)(2,1)}, u32[]{:S(2)}) copy-start(bf16[16,16,1024]{2,1,0:T(8,128)(2,1)} %copy-done.9) | copy-start | bytes 1572868
  85.5 3.5 copy-start.8
  122.1 253.4 %copy-start.1 = (bf16[1024,1024]{1,0:T(8,128)(2,1)S(1)}, bf16[1024,1024]{1,0:T(8,128)(2,1)}, u32[]{:S(2)}) copy-start(bf16[1024,1024]{1,0:T(8,128)(2,1)} %param.9) | copy-start | bytes 6291460
  124.2 23.4 %copy-start.7 = (bf16[16,16,1024]{2,1,0:T(8,128)(2,1)S(1)}, bf16[16,16,1024]{2,1,0:T(8,128)(2,1)}, u32[]{:S(2)}) copy-start(bf16[16,16,1024]{2,1,0:T(8,128)(2,1)} %param.7) | copy-start | bytes 1572868
  129.3 7.7 %collective-permute-start.4 = (bf16[8,16,1024]{2,1,0:T(8,128)(2,1)S(1)}, bf16[8,16,1024]{2,1,0:T(8,128)(2,1)S(1)}, u32[]{:S(2)}, u32[]{:S(2)}) collective-permute-start(bf16[8,16,1024]{2,1,0:T(8,128)(2,1)S(1)} %bitcast.83), channel_id=1, source_target_pairs={{0,8},{8,16},{16,24},{24,32},{32,40},{40,48},{48,56},{56,64},{64,7... | collective-permute-start | bytes 786440 | tf_op jit(solution)/shard_map/ppermute | solution.py:16
  137.7 9.8 %collective-permute-start.5 = (bf16[16,8,1024]{2,1,0:T(8,128)(2,1)}, bf16[16,8,1024]{2,1,0:T(8,128)(2,1)S(1)}, u32[]{:S(2)}, u32[]{:S(2)}) collective-permute-start(bf16[16,8,1024]{2,1,0:T(8,128)(2,1)} %fusion.61), channel_id=1, source_target_pairs={{0,1},{1,2},{2,3},{3,4},{4,5},{5,6},{6,7},{7,0},{8,9},{9,10},{10,1... | collective-permute-start | bytes 786440 | tf_op jit(solution)/shard_map/ppermute | solution.py:16
  (2 other events, 1.5 us)
Sparse Core Ops, SparseCore 0:
  89.2 283.6 all-reduce.4
where the time goes:
time: 384 us; the launch traced here: 382 us
  waiting for transfers between devices  242 us (63%)
  matrix products  76.5 us (20%)
  local copies, waits for them, and re-layouts  19.6 us (5%)
  other arithmetic  15.4 us (4%)
  starting transfers between devices  14.6 us (4%)
  between operations  14.4 us (4%)
    unnamed x2, waiting for transfers between devices  224 us
    dot_general x5, matrix products, mixed_einsum(): return jnp.einsum(form, left, right, preferred_element_type=jnp.float32)  41.8 us
    ppermute x6, waiting for transfers between devices, passed_along(): lax.ppermute(array, axis, [(i, (i + by) % devices) for i in range(devices)])  17.6 us
    sub x2, matrix products, soft_scores(): expo = jnp.exp(logits - top)  16 us
    ppermute x6, starting transfers between devices, passed_along(): lax.ppermute(array, axis, [(i, (i + by) % devices) for i in range(devices)])  14.6 us
  transfers between devices with their start and end apart: 7, of which 4 were waited for; matrix products, arithmetic and copies ran while one was open for 20% of the time, Pallas kernels for 0%

commit v1 on v0

v1 whole, which is shorter than its diff:
```python
import functools
import math

import jax
import jax.numpy as jnp
from jax import lax
from jax.experimental import pallas as pl
from jax.experimental.pallas import tpu as pltpu
from jax.sharding import PartitionSpec as P

HEADS = 32
WIN = 16
HALF = WIN // 2
DIM = 32
TOK = WIN * WIN
C = 1024
EPS_NORM = 1e-06
EPS_LN = 1e-05
LOG2E = math.log2(math.e)
BLOCK = 2.0**20
BF = jnp.bfloat16
F32 = jnp.float32
MIB = 2**20


def dot(left, right, dims=((1,), (0,))):
    return lax.dot_general(left, right, (dims, ((), ())), preferred_element_type=F32)


TN = ((0,), (0,))
NT = ((1,), (1,))
TT = ((0,), (1,))
STEP = 8


def head_rows(h):
    return pl.ds(pl.multiple_of(h * DIM, DIM), DIM)


def last_window(rows, cols):
    last_row = (lax.axis_index("row") == rows - 1).astype(F32)
    last_col = (lax.axis_index("col") == cols - 1).astype(F32)
    return last_row, last_col


def mask_features(last_row, last_col):
    feature = lax.broadcasted_iota(jnp.int32, (16, TOK), 0)
    token = lax.broadcasted_iota(jnp.int32, (16, TOK), 1)
    low = (token // (TOK // 2)).astype(F32)
    far = (token // (TOK // 4) % 2).astype(F32)

    def rows(*values):
        out = jnp.zeros((16, TOK), F32)
        for n, value in enumerate(values):
            out = jnp.where(feature == n, value, out)
        return out

    key = rows(low, 1 - low, far, 1 - far)
    query = -BLOCK * rows(
        last_row * (1 - low), last_row * low, last_col * (1 - far), last_col * far
    )
    return key.astype(BF), query.astype(BF)


def attention_kernel(
    rows, cols, x0_ref, x1_ref, x2_ref, x3_ref, w_hbm_ref, scale_ref,
    att_ref, probs_ref, query_ref, key_ref, value_ref, unit_scale_ref, w_qkv_ref, sems,
):
    copies = []
    for n in range(3):
        span = pl.ds(n * C, C)
        copies.append(
            pltpu.make_async_copy(w_hbm_ref.at[:, span], w_qkv_ref.at[:, span], sems.at[n])
        )
        copies[-1].start()
    key_mask, query_mask = mask_features(*last_window(rows, cols))
    x = jnp.concatenate([x0_ref[...], x1_ref[...], x2_ref[...], x3_ref[...]], axis=0)
    for col in range(0, 3 * C, TOK):
        if col % C == 0:
            copies[col // C].wait()
        raw = dot(x, w_qkv_ref[:, col : col + TOK]).T
        if col < 2 * C:
            heads = raw.reshape(TOK // DIM, DIM, TOK)
            inv = lax.rsqrt(jnp.sum(heads * heads, axis=1, keepdims=True) + EPS_NORM)
            unit = (heads * inv).reshape(TOK, TOK)
            unit_scale_ref[col // DIM : (col + TOK) // DIM, :] = inv[:, 0, :]
            if col < C:
                query_ref[col : col + TOK, :] = unit
            else:
                key_ref[col - C : col - C + TOK, :] = unit
        else:
            value_ref[col - 2 * C : col - 2 * C + TOK, :] = raw.astype(BF)

    def head(h, carry):
        rows = head_rows(h)
        raw = dot(
            jnp.concatenate([key_ref[rows, :].astype(BF), key_mask], axis=0),
            jnp.concatenate([query_ref[rows, :].astype(BF), query_mask], axis=0),
            TN,
        )
        top = jnp.max(raw, axis=0, keepdims=True)
        expo = jnp.exp2((raw - top) * (scale_ref[h] * LOG2E))
        probs = expo * (1.0 / jnp.sum(expo, axis=0, keepdims=True))
        probs_ref[h] = probs
        att_ref[rows, :] = dot(probs.astype(BF), value_ref[rows, :], TT).T.astype(BF)
        return carry

    lax.fori_loop(0, HEADS, head, 0, unroll=8)


def norm_kernel(
    att_ref, g0_ref, g1_ref, g2_ref, g3_ref, order_ref, w_proj_ref, gain_ref,
    near_ref, far_ref, grad_att_ref,
):
    g = jnp.concatenate([g0_ref[...], g1_ref[...], g2_ref[...], g3_ref[...]], axis=0)
    mixed = dot(att_ref[...], w_proj_ref[...], TN)
    center = mixed - jnp.mean(mixed, axis=-1, keepdims=True)
    inv_std = lax.rsqrt(jnp.mean(center * center, axis=-1, keepdims=True) + EPS_LN)
    normed = center * inv_std
    grad_norm = g.astype(F32) * gain_ref[...]
    grad_mix = inv_std * (
        grad_norm
        - jnp.mean(grad_norm, axis=-1, keepdims=True)
        - normed * jnp.mean(grad_norm * normed, axis=-1, keepdims=True)
    )
    grad_mix = grad_mix.astype(BF)
    for row in range(0, C, TOK):
        att = dot(order_ref[row : row + TOK, :], att_ref[...]).astype(BF)
        out_ref = near_ref if row < C // 2 else far_ref
        out_ref[row % (C // 2) : row % (C // 2) + TOK, :] = dot(att, grad_mix).astype(BF)
    for row in range(0, C, TOK):
        grad_att_ref[row : row + TOK, :] = dot(
            w_proj_ref[row : row + TOK, :], grad_mix, NT
        ).astype(BF)


def value_kernel(
    x0_ref, x1_ref, x2_ref, x3_ref, order_ref, probs_ref, grad_att_ref,
    near_ref, far_ref, grad_value_ref,
):
    tokens = jnp.concatenate([x0_ref[...], x1_ref[...], x2_ref[...], x3_ref[...]], axis=0)

    def head(h, carry):
        rows = head_rows(h)
        grad_value_ref[rows, :] = dot(
            grad_att_ref[rows, :], probs_ref[h].astype(BF), NT
        ).astype(BF)
        return carry

    lax.fori_loop(0, HEADS, head, 0, unroll=8)
    grad_value = grad_value_ref[...]
    for row in range(0, C, TOK):
        x = dot(order_ref[row : row + TOK, :], tokens, NT).astype(BF)
        out_ref = near_ref if row < C // 2 else far_ref
        out_ref[row % (C // 2) : row % (C // 2) + TOK, :] = dot(x, grad_value, NT).astype(BF)


def score_kernel(
    probs_ref, grad_att_ref, query_ref, key_ref, value_ref, q_scale_ref, k_scale_ref,
    scale_ref, after_ref, grad_query_ref, grad_key_ref, grad_score_ref,
):
    first = pl.program_id(0) * STEP

    def scores(n, carry):
        rows = head_rows(n)
        probs = probs_ref[n]
        grad_prob = dot(value_ref[rows, :], grad_att_ref[rows, :], TN)
        mean = jnp.sum(grad_prob * probs, axis=0, keepdims=True)
        grad_score_ref[n] = (scale_ref[first + n] * (probs * (grad_prob - mean))).astype(BF)
        return carry

    def units(n, carry):
        rows = head_rows(n)
        query = query_ref[rows, :]
        key = key_ref[rows, :]
        grad_score = grad_score_ref[n]
        grad_query = dot(key.astype(BF), grad_score)
        grad_key = dot(grad_score, query.astype(BF), NT).T
        grad_query = q_scale_ref[pl.ds(n, 1), :] * (
            grad_query - query * jnp.sum(grad_query * query, axis=0, keepdims=True)
        )
        grad_key = k_scale_ref[pl.ds(n, 1), :] * (
            grad_key - key * jnp.sum(grad_key * key, axis=0, keepdims=True)
        )
        grad_query_ref[rows, :] = grad_query.astype(BF)
        grad_key_ref[rows, :] = grad_key.astype(BF)
        return carry

    lax.fori_loop(0, STEP, scores, 0, unroll=STEP)
    lax.fori_loop(0, STEP, units, 0, unroll=STEP)


def input_kernel(*refs):
    parts, w_qkv_ref, out_refs = refs[:-5], refs[-5], refs[-4:]
    for row in range(0, C, TOK):
        total, col = 0.0, 0
        for part in parts:
            size = part.shape[0]
            total += dot(w_qkv_ref[row : row + TOK, col : col + size], part[...])
            col += size
        total = total.T.astype(BF)
        for n, out_ref in enumerate(out_refs):
            out_ref[:, row : row + TOK] = total[n * 64 : n * 64 + 64]


VM = pl.BlockSpec(memory_space=pltpu.VMEM)
SM = pl.BlockSpec(memory_space=pltpu.SMEM)


def shape(dims, kind):
    return jax.ShapeDtypeStruct(dims, kind)


def call(kernel, outs, ins, micros, name, limit, scratch=()):
    return pl.pallas_call(
        kernel,
        out_shape=outs,
        in_specs=ins,
        out_specs=jax.tree.map(lambda _: VM, outs),
        scratch_shapes=scratch,
        compiler_params=pltpu.CompilerParams(vmem_limit_bytes=limit * MIB),
        cost_estimate=pl.CostEstimate(
            flops=int(micros * 11 * 10**8), bytes_accessed=MIB, transcendentals=0
        ),
        name=name,
    )


def attention(quads, w_qkv, scale, rows, cols):
    flat = shape((C, TOK), F32)
    flat_bf = shape((C, TOK), BF)
    outs = (
        flat_bf, shape((HEADS, TOK, TOK), F32), flat, flat, flat_bf, shape((2 * HEADS, TOK), F32),
    )
    kernel = functools.partial(attention_kernel, rows, cols)
    scratch = [pltpu.VMEM((C, 3 * C), BF), pltpu.SemaphoreType.DMA((3,))]
    return call(
        kernel, outs, [VM] * 4 + [pl.BlockSpec(memory_space=pltpu.HBM), SM], 14,
        "attention_part", 24, scratch,
    )(*quads, pltpu.with_memory_space_constraint(w_qkv, pltpu.HBM), scale)


def output_norm(att, quads, order, w_proj, gain):
    half = shape((C // 2, C), BF)
    return call(norm_kernel, (half, half, shape((C, TOK), BF)), [VM] * 8, 3, "norm_part", 24)(
        att, *quads, order, w_proj, gain
    )


def value_grads(quads, order, probs, grad_att):
    half = shape((C // 2, C), BF)
    return call(value_kernel, (half, half, shape((C, TOK), BF)), [VM] * 7, 4, "value_part", 24)(
        *quads, order, probs, grad_att
    )


def score_grads(probs, grad_att, query, key, value, unit_scale, scale, after):
    wide = pl.BlockSpec((STEP * DIM, TOK), lambda n: (n, 0))
    steps = HEADS // STEP
    streamed = [
        pltpu.with_memory_space_constraint(array, pltpu.HBM)
        for array in (probs, grad_att, query, key, value)
    ]
    return pl.pallas_call(
        score_kernel,
        out_shape=(shape((C, TOK), BF),) * 2,
        grid=(steps,),
        in_specs=[
            pl.BlockSpec((STEP, TOK, TOK), lambda n: (n, 0, 0)),
            wide,
            wide,
            wide,
            wide,
            pl.BlockSpec((STEP, TOK), lambda n: (n, 0)),
            pl.BlockSpec((STEP, TOK), lambda n: (n + steps, 0)),
            SM,
            pl.BlockSpec(memory_space=pl.ANY),
        ],
        out_specs=(wide, wide),
        scratch_shapes=[pltpu.VMEM((STEP, TOK, TOK), BF)],
        compiler_params=pltpu.CompilerParams(vmem_limit_bytes=24 * MIB),
        cost_estimate=pl.CostEstimate(flops=10**8, bytes_accessed=MIB, transcendentals=0),
        name="score_part",
    )(*streamed, unit_scale, unit_scale, scale, after)


def input_grad(parts, w_qkv):
    outs = (shape((TOK // 4, C), BF),) * 4
    return call(input_kernel, outs, [VM] * (len(parts) + 1), 0.2, "input_part", 24)(*parts, w_qkv)


def passed(array, d_row, d_col, rows, cols):
    pairs = [
        (r * cols + c, (r + d_row) % rows * cols + (c + d_col) % cols)
        for r in range(rows)
        for c in range(cols)
    ]
    return lax.ppermute(array, ("row", "col"), pairs)


def window(array, rows, cols):
    def quad(r, c):
        return array[r : r + HALF, c : c + HALF].reshape(TOK // 4, C)

    return (
        quad(HALF, HALF),
        passed(quad(HALF, 0), 0, -1, rows, cols),
        passed(quad(0, HALF), -1, 0, rows, cols),
        passed(quad(0, 0), -1, -1, rows, cols),
    )


def line(x, y, z, core):
    return ((z * 2 + x // 2) * 2 + core) * 8 + y * 2 + x % 2


CHIPS = [(x, y, z, core) for x in range(4) for y in range(4) for z in range(8) for core in range(2)]
BOTH = ("row", "col")


def other_core(array):
    pairs = [(line(x, y, z, core), line(x, y, z, 1 - core)) for x, y, z, core in CHIPS]
    return lax.ppermute(array, BOTH, pairs)


def row_order():
    place = jnp.arange(C, dtype=jnp.int32)
    far, x, y, z, row = place // 512, place // 128 % 4, place // 32 % 4, place // 4 % 8, place % 4
    core = (lax.axis_index("row") + far) % 2
    source = z * 128 + x // 2 * 64 + core * 32 + y * 8 + x % 2 * 4 + row
    return (source[:, None] == jnp.arange(C, dtype=jnp.int32)[None, :]).astype(BF)


def plus(*terms):
    return sum(term.astype(F32) for term in terms).astype(BF)


def group_sum(blocks, groups):
    got = lax.all_to_all(blocks, BOTH, 0, 0, axis_index_groups=groups, tiled=True)
    return jnp.sum(got.astype(F32), axis=0)


def plane_sum(blocks):
    groups = [
        [line(x, y, z, core) for x in range(4) for y in range(4)]
        for z in range(8)
        for core in range(2)
    ]
    return group_sum(blocks, groups).astype(BF)


def z_sum(blocks):
    groups = [
        [line(x, y, z, core) for z in range(8)]
        for x in range(4)
        for y in range(4)
        for core in range(2)
    ]
    return group_sum(blocks, groups)


def per_device(tokens, grad_out, w_qkv, w_proj, norm_gain, logit_scale):
    rows, cols = lax.axis_size("row"), lax.axis_size("col")
    x = window(tokens, rows, cols)
    g = window(grad_out, rows, cols)
    att, probs, query, key, value, unit_scale = attention(x, w_qkv, logit_scale, rows, cols)
    order = row_order()
    proj, far, grad_att = output_norm(att, g, order, w_proj, norm_gain.reshape(1, C))
    proj_far = other_core(far)
    val, far, grad_value = value_grads(x, order, probs, grad_att)
    terms = jnp.concatenate(
        [
            plus(proj, proj_far).reshape(16, 32, C),
            plus(val, other_core(far)).reshape(16, 32, C),
        ],
        axis=1,
    )

    grad_query, grad_key = score_grads(
        probs, grad_att, query, key, value, unit_scale, logit_scale, terms
    )
    terms = plane_sum(terms)
    grad_input = input_grad([grad_query, grad_key, grad_value], w_qkv)
    terms = jnp.concatenate(
        [terms[:32].reshape(8, 4, C), terms[32:].reshape(8, 4, C)], axis=1
    )
    terms = z_sum(terms)
    proj_part, value_part = terms[:4], terms[4:]
    back = jnp.stack(
        [
            passed(grad_input[3], 1, 1, rows, cols),
            passed(grad_input[2], 1, 0, rows, cols),
            passed(grad_input[1], 0, 1, rows, cols),
            grad_input[0],
        ]
    )
    back = back.reshape(2, 2, HALF, HALF, C).transpose(0, 2, 1, 3, 4).reshape(WIN, WIN, C)
    grad_tokens = (grad_out.astype(F32) + back.astype(F32)).astype(BF)
    return (grad_tokens, value_part, proj_part)


def solution(mesh):
    in_specs = (P("row", "col", None), P("row", "col", None), P(), P(), P(), P())
    out_specs = (P("row", "col", None), P(("row", "col"), None), P(("row", "col"), None))
    return jax.shard_map(
        per_device, mesh=mesh, in_specs=in_specs, out_specs=out_specs, check_vma=False
    )
```

time: 384 us -> 99.4 us (0.26)
  waiting for transfers between devices: 242 us -> 27.3 us
  matrix products: 76.5 us -> 0 us
  Pallas kernels: 0 us -> 25.8 us
  starting transfers between devices: 14.6 us -> 35.1 us
  local copies, waits for them, and re-layouts: 19.6 us -> 3.84 us
  between operations: 14.4 us -> 0.97 us
  other arithmetic: 15.4 us -> 6.13 us
    unnamed x2 -> x0, waiting for transfers between devices: 224 us -> none
    dot_general x11 -> x0, matrix products: 60.5 us -> none  [the longest x5 41.8 us: mixed_einsum(): return jnp.einsum(form, left, right, preferred_element_type=jnp.float32)]
    pallas_call x0 -> x5, Pallas kernels: none -> 25.8 us  [the longest x1 9.7 us: attention(): call(kernel, outs, [VM] * 4 + [pl.BlockSpec(memory_space=pltpu.HBM), SM],...]
    sub x2 -> x0, matrix products: 16 us -> none  [soft_scores(): expo = jnp.exp(logits - top)]
    all_to_all x0 -> x2, starting transfers between devices: none -> 13.3 us  [group_sum(): lax.all_to_all(blocks, BOTH, 0, 0, axis_index_groups=groups, tiled=True)]
    slice x8 -> x2, local copies, waits for them, and re-layouts: 8.26 us -> 0.63 us  [the longest x1 0.62 us: per_device(): proj_part, value_part = (terms[:4], terms[4:])]
    ppermute x6 -> x11, starting transfers between devices: 14.6 us -> 21.8 us  [the longest x9 20.7 us: passed(): return lax.ppermute(array, ('row', 'col'), pairs)]
    all_to_all x0 -> x2, waiting for transfers between devices: none -> 5.95 us  [group_sum(): lax.all_to_all(blocks, BOTH, 0, 0, axis_index_groups=groups, tiled=True)]
  transfers between devices with their start and end apart: 7 -> 13, of which waited for: 4 -> 5; matrix products, arithmetic and copies ran while one was open for 20% -> 4% of each run, Pallas kernels for 0% -> 20%
where the time goes in v1:
time: 99.4 us; the launch traced here: 99.1 us
  starting transfers between devices  35.1 us (35%)
  waiting for transfers between devices  27.3 us (27%)
  Pallas kernels  25.8 us (26%)
  other arithmetic  6.13 us (6%)
  local copies, waits for them, and re-layouts  3.84 us (4%)
    ppermute x9, starting transfers between devices, passed(): return lax.ppermute(array, ('row', 'col'), pairs)  20.7 us
    ppermute x9, waiting for transfers between devices, passed(): return lax.ppermute(array, ('row', 'col'), pairs)  18 us
    all_to_all x2, starting transfers between devices, group_sum(): lax.all_to_all(blocks, BOTH, 0, 0, axis_index_groups=groups, tiled=True)  13.3 us
    pallas_call x1, Pallas kernels, attention(): call(kernel, outs, [VM] * 4 + [pl.BlockSpec(memory_space=pltpu.HBM), SM],...  9.7 us
    pallas_call x1, Pallas kernels, score_grads(): pl.pallas_call(score_kernel, out_shape=(shape((C, TOK), BF),) * 2, grid=(...  7.79 us
    all_to_all x2, waiting for transfers between devices, group_sum(): lax.all_to_all(blocks, BOTH, 0, 0, axis_index_groups=groups, tiled=True)  5.95 us
    ppermute x2, waiting for transfers between devices, other_core(): return lax.ppermute(array, BOTH, pairs)  3.28 us
    pallas_call x1, Pallas kernels, value_grads(): call(value_kernel, (half, half, shape((C, TOK), BF)), [VM] * 7, 4, 'value...  3.25 us
  transfers between devices with their start and end apart: 13, of which 5 were waited for; matrix products, arithmetic and copies ran while one was open for 4% of the time, Pallas kernels for 20%

profile of v1, /device:TPU:1, one launch (start us, length us, event | category | flops | bytes accessed | tf_op | source)
XLA Modules:
  0.0 99.1 jit_solution(4131625250924934566)
XLA Ops:
  0.6 1.1 %slice_bitcast_fusion.4 = (bf16[64,1024]{1,0:T(8,128)(2,1)S(1)}, bf16[64,1024]{1,0:T(8,128)(2,1)S(1)}, bf16[64,1024]{1,0:T(8,128)(2,1)S(1)}, bf16[64,1024]{1,0:T(8,128)(2,1)S(1)}) fusion(bf16[16,16,1024]{2,1,0:T(8,128)(2,1)} %param.6), kind=kLoop, calls=%fused_computation.14 | loop fusion | bytes 1048576 | tf_op jit(solution)/shard_map/reshape | solution.py:303
  1.8 5.1 %collective-permute-start.2 = (bf16[64,1024]{1,0:T(8,128)(2,1)S(1)}, bf16[64,1024]{1,0:T(8,128)(2,1)S(1)}, u32[]{:S(2)}, u32[]{:S(2)}) collective-permute-start(bf16[64,1024]{1,0:T(8,128)(2,1)S(1)} %get-tuple-element.43), channel_id=1, source_target_pairs={{0,255},{1,248},{2,249},{3,250},{4,251},{5,252},{6,253},{7,254},{8... | collective-permute-start | bytes 393224 | tf_op jit(solution)/shard_map/ppermute | solution.py:298
  7.2 6.4 %collective-permute-start.1 = (bf16[64,1024]{1,0:T(8,128)(2,1)S(1)}, bf16[64,1024]{1,0:T(8,128)(2,1)S(1)}, u32[]{:S(2)}, u32[]{:S(2)}) collective-permute-start(bf16[64,1024]{1,0:T(8,128)(2,1)S(1)} %get-tuple-element.46), channel_id=1, source_target_pairs={{0,248},{1,249},{2,250},{3,251},{4,252},{5,253},{6,254},{7,255},{8... | collective-permute-start | bytes 393224 | tf_op jit(solution)/shard_map/ppermute | solution.py:298
  13.5 1.1 %slice_bitcast_fusion = (bf16[64,1024]{1,0:T(8,128)(2,1)S(1)}, bf16[64,1024]{1,0:T(8,128)(2,1)S(1)}, bf16[64,1024]{1,0:T(8,128)(2,1)S(1)}, bf16[64,1024]{1,0:T(8,128)(2,1)S(1)}) fusion(bf16[16,16,1024]{2,1,0:T(8,128)(2,1)} %param.7), kind=kLoop, calls=%fused_computation.10 | loop fusion | bytes 1048576 | tf_op jit(solution)/shard_map/reshape | solution.py:303
  14.7 2.5 %collective-permute-start.5 = (bf16[64,1024]{1,0:T(8,128)(2,1)S(1)}, bf16[64,1024]{1,0:T(8,128)(2,1)S(1)}, u32[]{:S(2)}, u32[]{:S(2)}) collective-permute-start(bf16[64,1024]{1,0:T(8,128)(2,1)S(1)} %get-tuple-element.39), channel_id=1, source_target_pairs={{0,255},{1,248},{2,249},{3,250},{4,251},{5,252},{6,253},{7,254},{8... | collective-permute-start | bytes 393224 | tf_op jit(solution)/shard_map/ppermute | solution.py:298
  17.2 1.2 %collective-permute-start.3 = (bf16[64,1024]{1,0:T(8,128)(2,1)S(1)}, bf16[64,1024]{1,0:T(8,128)(2,1)S(1)}, u32[]{:S(2)}, u32[]{:S(2)}) collective-permute-start(bf16[64,1024]{1,0:T(8,128)(2,1)S(1)} %get-tuple-element.40), channel_id=1, source_target_pairs={{0,7},{1,0},{2,1},{3,2},{4,3},{5,4},{6,5},{7,6},{8,15},{9,8},{10,9... | collective-permute-start | bytes 393224 | tf_op jit(solution)/shard_map/ppermute | solution.py:298
  19.1 9.7 %attention_part.1 = (bf16[1024,256]{1,0:T(8,128)(2,1)S(1)}, f32[32,256,256]{2,1,0:T(8,128)S(1)}, f32[1024,256]{1,0:T(8,128)S(1)}, f32[1024,256]{1,0:T(8,128)S(1)...) custom-call(bf16[64,1024]{1,0:T(8,128)(2,1)S(1)} %get-tuple-element.45.x0_ref, ...), custom_call_target="tpu_custom_call" | custom-call | flops 15399999488 | bytes 1048576 | tf_op jit(solution)/shard_map/attention_part/pallas_call | solution.py:237
  28.9 3.2 %norm_part.1 = (bf16[512,1024]{1,0:T(8,128)(2,1)S(1)}, bf16[512,1024]{1,0:T(8,128)(2,1)S(1)}, bf16[1024,256]{1,0:T(8,128)(2,1)S(1)}) custom-call(bf16[1024,256]{1,0:T(8,128)(2,1)S(1)} %get-tuple-element.22.att_ref, bf16[64,1024]{1,0:T(8,128)(2,1)S(1)} %get-tuple-element.41.g0_ref, bf16[64,1024]{1,0:T(8,128)(2,1)S(1)} %collective-permute-done.3.g1_ref, ...), custom_call_target="tpu_custom_call" | custom-call | flops 3300000000 | bytes 1048576 | tf_op jit(solution)/shard_map/norm_part/pallas_call | solution.py:245
  32.1 0.8 copy-done
  32.9 3.2 %value_part.1 = (bf16[512,1024]{1,0:T(8,128)(2,1)S(1)}, bf16[512,1024]{1,0:T(8,128)(2,1)S(1)}, bf16[1024,256]{1,0:T(8,128)(2,1)S(1)}) custom-call(bf16[64,1024]{1,0:T(8,128)(2,1)S(1)} %get-tuple-element.45.x0_ref, bf16[64,1024]{1,0:T(8,128)(2,1)S(1)} %collective-permute-done.x1_ref, bf16[64,1024]{1,0:T(8,128)(2,1)S(1)} %collective-permute-done.1.x2_ref, ...), custom_call_target="tpu_custom_call" | custom-call | flops 4400000000 | bytes 1048576 | tf_op jit(solution)/shard_map/value_part/pallas_call | solution.py:252
  36.1 1.0 %collective-permute-start.7 = (bf16[512,1024]{1,0:T(8,128)(2,1)S(1)}, bf16[512,1024]{1,0:T(8,128)(2,1)S(1)}, u32[]{:S(2)}, u32[]{:S(2)}) collective-permute-start(bf16[512,1024]{1,0:T(8,128)(2,1)S(1)} %get-tuple-element.31), channel_id=1, source_target_pairs={{0,8},{8,0},{32,40},{40,32},{64,72},{72,64},{96,104},{104,96},{128... | collective-permute-start | bytes 3145736 | tf_op jit(solution)/shard_map/ppermute | solution.py:323
  37.2 2.2 %collective-permute-done.7 = bf16[512,1024]{1,0:T(8,128)(2,1)S(1)} collective-permute-done((bf16[512,1024]{1,0:T(8,128)(2,1)S(1)}, bf16[512,1024]{1,0:T(8,128)(2,1)S(1)}, u32[]{:S(2)}, u32[]{:S(2)}) %collective-permute-start.7) | collective-permute-done | bytes 1048608 | tf_op jit(solution)/shard_map/ppermute | solution.py:323
  39.8 1.1 %collective-permute-done.6 = bf16[512,1024]{1,0:T(8,128)(2,1)S(1)} collective-permute-done((bf16[512,1024]{1,0:T(8,128)(2,1)S(1)}, bf16[512,1024]{1,0:T(8,128)(2,1)S(1)}, u32[]{:S(2)}, u32[]{:S(2)}) %collective-permute-start.6) | collective-permute-done | bytes 1048608 | tf_op jit(solution)/shard_map/ppermute | solution.py:323
  41.3 1.6 %pad_maximum_fusion.after_ref = bf16[16,64,1024]{2,1,0:T(8,128)(2,1)} fusion(bf16[16,32,1024]{2,1,0:T(8,128)(2,1)S(1)} %bitcast.33, bf16[16,32,1024]{2,1,0:T(8,128)(2,1)S(1)} %bitcast.34), kind=kLoop, calls=%fused_computation.2 | loop fusion | flops 4194304 | bytes 4194304 | tf_op jit(solution)/shard_map/concatenate | solution.py:371
  42.9 5.8 %all-to-all-start = ((bf16[16,64,1024]{2,1,0:T(8,128)(2,1)}), bf16[16,64,1024]{2,1,0:T(8,128)(2,1)S(1)}, u32[]{:S(2)}, u32[]{:S(2)}) async-start(bf16[16,64,1024]{2,1,0:T(8,128)(2,1)} %pad_maximum_fusion.after_ref), calls=%async_computation | async-start | bytes 4194304 | tf_op jit(solution)/shard_map/all_to_all | solution.py:339
  48.8 7.8 %score_part.1 = (bf16[1024,256]{1,0:T(8,128)(2,1)S(1)}, bf16[1024,256]{1,0:T(8,128)(2,1)S(1)}) custom-call(f32[32,256,256]{2,1,0:T(8,128)} %copy-done, bf16[1024,256]{1,0:T(8,128)(2,1)} %copy-done.4, f32[1024,256]{1,0:T(8,128)} %copy-done.1, f32[1024,256]{1,0:T(8,128)} %copy-done.2, bf16[1024,256]{1,0:T(8,128)(2,1)} %copy-done.3, ...), custom_call_target="tpu_custom_call" | custom-call | flops 100000000 | bytes 1048576 | tf_op jit(solution)/shard_map/score_part/pallas_call | solution.py:264
  56.6 1.9 %input_part.1 = (bf16[64,1024]{1,0:T(8,128)(2,1)S(1)}, bf16[64,1024]{1,0:T(8,128)(2,1)S(1)}, bf16[64,1024]{1,0:T(8,128)(2,1)S(1)}, bf16[64,1024]{1,0:T(8,128)(2,1)S(1)}) custom-call(bf16[1024,256]{1,0:T(8,128)(2,1)S(1)} %get-tuple-element.32.refs_0_, bf16[1024,256]{1,0:T(8,128)(2,1)S(1)} %get-tuple-element.33.refs_1_, ...), custom_call_target="tpu_custom_call" | custom-call | flops 220000000 | bytes 1048576 | tf_op jit(solution)/shard_map/input_part/pallas_call | solution.py:289
  58.5 3.5 %collective-permute-start.8 = (bf16[64,1024]{1,0:T(8,128)(2,1)S(1)}, bf16[64,1024]{1,0:T(8,128)(2,1)S(1)}, u32[]{:S(2)}, u32[]{:S(2)}) collective-permute-start(bf16[64,1024]{1,0:T(8,128)(2,1)S(1)} %get-tuple-element.35), channel_id=1, source_target_pairs={{0,9},{1,10},{2,11},{3,12},{4,13},{5,14},{6,15},{7,8},{8,17},{9,18... | collective-permute-start | bytes 393224 | tf_op jit(solution)/shard_map/ppermute | solution.py:298
  62.6 0.9 collective-permute-start.10
  63.5 16.8 %collective-permute-done.8 = bf16[64,1024]{1,0:T(8,128)(2,1)S(1)} collective-permute-done((bf16[64,1024]{1,0:T(8,128)(2,1)S(1)}, bf16[64,1024]{1,0:T(8,128)(2,1)S(1)}, u32[]{:S(2)}, u32[]{:S(2)}) %collective-permute-start.8) | collective-permute-done | bytes 131104 | tf_op jit(solution)/shard_map/ppermute | solution.py:298
  80.3 1.2 %collective-permute-done.10 = bf16[64,1024]{1,0:T(8,128)(2,1)S(1)} collective-permute-done((bf16[64,1024]{1,0:T(8,128)(2,1)S(1)}, bf16[64,1024]{1,0:T(8,128)(2,1)S(1)}, u32[]{:S(2)}, u32[]{:S(2)}) %collective-permute-start.10) | collective-permute-done | bytes 131104 | tf_op jit(solution)/shard_map/ppermute | solution.py:298
  83.0 7.5 %all-to-all-start.1 = ((bf16[8,8,1024]{2,1,0:T(8,128)(2,1)}), bf16[8,8,1024]{2,1,0:T(8,128)(2,1)S(1)}, u32[]{:S(2)}, u32[]{:S(2)}) async-start(bf16[8,8,1024]{2,1,0:T(8,128)(2,1)} %pad_maximum_fusion.2), calls=%async_computation.1 | async-start | bytes 262144 | tf_op jit(solution)/shard_map/all_to_all | solution.py:339
  90.5 2.0 %add_convert_fusion.2 = bf16[16,16,1024]{2,1,0:T(8,128)(2,1)} fusion(f32[16,16,1024]{2,1,0:T(8,128)S(1)} %bitcast.32, bf16[16,16,1024]{2,1,0:T(8,128)(2,1)} %param.7), kind=kLoop, calls=%fused_computation.6 | loop fusion | flops 786432 | bytes 2097152 | tf_op jit(solution)/shard_map/convert_element_type | solution.py:398
  92.5 5.9 %all-to-all-done.1 = bf16[8,8,1024]{2,1,0:T(8,128)(2,1)S(1)} async-done(((bf16[8,8,1024]{2,1,0:T(8,128)(2,1)}), bf16[8,8,1024]{2,1,0:T(8,128)(2,1)S(1)}, u32[]{:S(2)}, u32[]{:S(2)}) %all-to-all-start.1) | async-done | bytes 131104 | tf_op jit(solution)/shard_map/all_to_all | solution.py:339
  (46 shorter events, 4.6 us)
Async XLA Ops:
  0.6 18.4 %copy-start.5 = (f32[32]{0:T(128)S(1)}, f32[32]{0:T(128)}, u32[]{:S(2)}) copy-start(f32[32]{0:T(128)} %scale_ref.3) | copy-start | bytes 388
  1.8 17.0 %collective-permute-start.2 = (bf16[64,1024]{1,0:T(8,128)(2,1)S(1)}, bf16[64,1024]{1,0:T(8,128)(2,1)S(1)}, u32[]{:S(2)}, u32[]{:S(2)}) collective-permute-start(bf16[64,1024]{1,0:T(8,128)(2,1)S(1)} %get-tuple-element.43), channel_id=1, source_target_pairs={{0,255},{1,248},{2,249},{3,250},{4,251},{5,252},{6,253},{7,254},{8... | collective-permute-start | bytes 393224 | tf_op jit(solution)/shard_map/ppermute | solution.py:298
  6.9 12.1 %collective-permute-start = (bf16[64,1024]{1,0:T(8,128)(2,1)S(1)}, bf16[64,1024]{1,0:T(8,128)(2,1)S(1)}, u32[]{:S(2)}, u32[]{:S(2)}) collective-permute-start(bf16[64,1024]{1,0:T(8,128)(2,1)S(1)} %get-tuple-element.44), channel_id=1, source_target_pairs={{0,7},{1,0},{2,1},{3,2},{4,3},{5,4},{6,5},{7,6},{8,15},{9,8},{10,9... | collective-permute-start | bytes 393224 | tf_op jit(solution)/shard_map/ppermute | solution.py:298
  7.2 11.9 %collective-permute-start.1 = (bf16[64,1024]{1,0:T(8,128)(2,1)S(1)}, bf16[64,1024]{1,0:T(8,128)(2,1)S(1)}, u32[]{:S(2)}, u32[]{:S(2)}) collective-permute-start(bf16[64,1024]{1,0:T(8,128)(2,1)S(1)} %get-tuple-element.46), channel_id=1, source_target_pairs={{0,248},{1,249},{2,250},{3,251},{4,252},{5,253},{6,254},{7,255},{8... | collective-permute-start | bytes 393224 | tf_op jit(solution)/shard_map/ppermute | solution.py:298
  14.7 14.2 %collective-permute-start.5 = (bf16[64,1024]{1,0:T(8,128)(2,1)S(1)}, bf16[64,1024]{1,0:T(8,128)(2,1)S(1)}, u32[]{:S(2)}, u32[]{:S(2)}) collective-permute-start(bf16[64,1024]{1,0:T(8,128)(2,1)S(1)} %get-tuple-element.39), channel_id=1, source_target_pairs={{0,255},{1,248},{2,249},{3,250},{4,251},{5,252},{6,253},{7,254},{8... | collective-permute-start | bytes 393224 | tf_op jit(solution)/shard_map/ppermute | solution.py:298
  17.2 11.7 %collective-permute-start.3 = (bf16[64,1024]{1,0:T(8,128)(2,1)S(1)}, bf16[64,1024]{1,0:T(8,128)(2,1)S(1)}, u32[]{:S(2)}, u32[]{:S(2)}) collective-permute-start(bf16[64,1024]{1,0:T(8,128)(2,1)S(1)} %get-tuple-element.40), channel_id=1, source_target_pairs={{0,7},{1,0},{2,1},{3,2},{4,3},{5,4},{6,5},{7,6},{8,15},{9,8},{10,9... | collective-permute-start | bytes 393224 | tf_op jit(solution)/shard_map/ppermute | solution.py:298
  18.8 10.1 %collective-permute-start.4 = (bf16[64,1024]{1,0:T(8,128)(2,1)S(1)}, bf16[64,1024]{1,0:T(8,128)(2,1)S(1)}, u32[]{:S(2)}, u32[]{:S(2)}) collective-permute-start(bf16[64,1024]{1,0:T(8,128)(2,1)S(1)} %get-tuple-element.42), channel_id=1, source_target_pairs={{0,248},{1,249},{2,250},{3,251},{4,252},{5,253},{6,254},{7,255},{8... | collective-permute-start | bytes 393224 | tf_op jit(solution)/shard_map/ppermute | solution.py:298
  19.1 9.8 %copy-start.6 = (bf16[1024,1024]{1,0:T(8,128)(2,1)S(1)}, bf16[1024,1024]{1,0:T(8,128)(2,1)}, u32[]{:S(2)}) copy-start(bf16[1024,1024]{1,0:T(8,128)(2,1)} %w_proj_ref.1) | copy-start | bytes 6291460
  19.1 9.8 %copy-start.7 = (f32[1024]{0:T(1024)S(1)}, f32[1024]{0:T(1024)}, u32[]{:S(2)}) copy-start(f32[1024]{0:T(1024)} %param.10) | copy-start | bytes 12292
  28.8 3.3 %copy-start.1 = (f32[1024,256]{1,0:T(8,128)}, f32[1024,256]{1,0:T(8,128)S(1)}, u32[]{:S(2)}) copy-start(f32[1024,256]{1,0:T(8,128)S(1)} %get-tuple-element.24.query_ref) | copy-start | bytes 3145732
  28.8 3.3 %copy-start.2 = (f32[1024,256]{1,0:T(8,128)}, f32[1024,256]{1,0:T(8,128)S(1)}, u32[]{:S(2)}) copy-start(f32[1024,256]{1,0:T(8,128)S(1)} %get-tuple-element.25.key_ref) | copy-start | bytes 3145732
  28.8 3.3 %copy-start.3 = (bf16[1024,256]{1,0:T(8,128)(2,1)}, bf16[1024,256]{1,0:T(8,128)(2,1)S(1)}, u32[]{:S(2)}) copy-start(bf16[1024,256]{1,0:T(8,128)(2,1)S(1)} %get-tuple-element.26.value_ref) | copy-start | bytes 1572868
  28.8 4.0 %copy-start = (f32[32,256,256]{2,1,0:T(8,128)}, f32[32,256,256]{2,1,0:T(8,128)S(1)}, u32[]{:S(2)}) copy-start(f32[32,256,256]{2,1,0:T(8,128)S(1)} %get-tuple-element.21.probs_ref) | copy-start | bytes 25165828
  32.1 4.0 %copy-start.4 = (bf16[1024,256]{1,0:T(8,128)(2,1)}, bf16[1024,256]{1,0:T(8,128)(2,1)S(1)}, u32[]{:S(2)}) copy-start(bf16[1024,256]{1,0:T(8,128)(2,1)S(1)} %get-tuple-element.23.grad_att_ref) | copy-start | bytes 1572868
  36.1 3.3 %collective-permute-start.7 = (bf16[512,1024]{1,0:T(8,128)(2,1)S(1)}, bf16[512,1024]{1,0:T(8,128)(2,1)S(1)}, u32[]{:S(2)}, u32[]{:S(2)}) collective-permute-start(bf16[512,1024]{1,0:T(8,128)(2,1)S(1)} %get-tuple-element.31), channel_id=1, source_target_pairs={{0,8},{8,0},{32,40},{40,32},{64,72},{72,64},{96,104},{104,96},{128... | collective-permute-start | bytes 3145736 | tf_op jit(solution)/shard_map/ppermute | solution.py:323
  37.1 3.8 %collective-permute-start.6 = (bf16[512,1024]{1,0:T(8,128)(2,1)S(1)}, bf16[512,1024]{1,0:T(8,128)(2,1)S(1)}, u32[]{:S(2)}, u32[]{:S(2)}) collective-permute-start(bf16[512,1024]{1,0:T(8,128)(2,1)S(1)} %get-tuple-element.29), channel_id=1, source_target_pairs={{0,8},{8,0},{32,40},{40,32},{64,72},{72,64},{96,104},{104,96},{128... | collective-permute-start | bytes 3145736 | tf_op jit(solution)/shard_map/ppermute | solution.py:323
  42.9 38.9 %all-to-all-start = ((bf16[16,64,1024]{2,1,0:T(8,128)(2,1)}), bf16[16,64,1024]{2,1,0:T(8,128)(2,1)S(1)}, u32[]{:S(2)}, u32[]{:S(2)}) async-start(bf16[16,64,1024]{2,1,0:T(8,128)(2,1)} %pad_maximum_fusion.after_ref), calls=%async_computation | async-start | bytes 4194304 | tf_op jit(solution)/shard_map/all_to_all | solution.py:339
  48.8 7.8 %slice-start = ((s8[6291456]{0:T(1024)(128)(4,1)}), s8[4194304]{0:T(1024)(128)(4,1)S(1)}, s32[]{:S(2)}) async-start(s8[6291456]{0:T(1024)(128)(4,1)} %bitcast.28), calls=%async_computation.2 | async-start | bytes 8388608
  48.8 7.8 %slice-start.1 = ((s8[6291456]{0:T(1024)(128)(4,1)}), s8[2097152]{0:T(1024)(128)(4,1)S(1)}, s32[]{:S(2)}) async-start(s8[6291456]{0:T(1024)(128)(4,1)} %bitcast.28), calls=%async_computation.3 | async-start | bytes 4194304
  58.5 21.8 %collective-permute-start.8 = (bf16[64,1024]{1,0:T(8,128)(2,1)S(1)}, bf16[64,1024]{1,0:T(8,128)(2,1)S(1)}, u32[]{:S(2)}, u32[]{:S(2)}) collective-permute-start(bf16[64,1024]{1,0:T(8,128)(2,1)S(1)} %get-tuple-element.35), channel_id=1, source_target_pairs={{0,9},{1,10},{2,11},{3,12},{4,13},{5,14},{6,15},{7,8},{8,17},{9,18... | collective-permute-start | bytes 393224 | tf_op jit(solution)/shard_map/ppermute | solution.py:298
  62.0 18.3 %collective-permute-start.9 = (bf16[64,1024]{1,0:T(8,128)(2,1)S(1)}, bf16[64,1024]{1,0:T(8,128)(2,1)S(1)}, u32[]{:S(2)}, u32[]{:S(2)}) collective-permute-start(bf16[64,1024]{1,0:T(8,128)(2,1)S(1)} %get-tuple-element.36), channel_id=1, source_target_pairs={{0,8},{1,9},{2,10},{3,11},{4,12},{5,13},{6,14},{7,15},{8,16},{9,17... | collective-permute-start | bytes 393224 | tf_op jit(solution)/shard_map/ppermute | solution.py:298
  62.6 18.9 %collective-permute-start.10 = (bf16[64,1024]{1,0:T(8,128)(2,1)S(1)}, bf16[64,1024]{1,0:T(8,128)(2,1)S(1)}, u32[]{:S(2)}, u32[]{:S(2)}) collective-permute-start(bf16[64,1024]{1,0:T(8,128)(2,1)S(1)} %get-tuple-element.37), channel_id=1, source_target_pairs={{0,1},{1,2},{2,3},{3,4},{4,5},{5,6},{6,7},{7,0},{8,9},{9,10},{10,1... | collective-permute-start | bytes 393224 | tf_op jit(solution)/shard_map/ppermute | solution.py:298
  83.0 15.5 %all-to-all-start.1 = ((bf16[8,8,1024]{2,1,0:T(8,128)(2,1)}), bf16[8,8,1024]{2,1,0:T(8,128)(2,1)S(1)}, u32[]{:S(2)}, u32[]{:S(2)}) async-start(bf16[8,8,1024]{2,1,0:T(8,128)(2,1)} %pad_maximum_fusion.2), calls=%async_computation.1 | async-start | bytes 262144 | tf_op jit(solution)/shard_map/all_to_all | solution.py:339

commit v2 on v1

--- a/solution.py
+++ b/solution.py
@@ -30,7 +30,6 @@
 TN = ((0,), (0,))
 NT = ((1,), (1,))
 TT = ((0,), (1,))
-STEP = 8
 
 
 def head_rows(h):
@@ -64,7 +63,8 @@
 
 def attention_kernel(
     rows, cols, x0_ref, x1_ref, x2_ref, x3_ref, w_hbm_ref, scale_ref,
-    att_ref, probs_ref, query_ref, key_ref, value_ref, unit_scale_ref, w_qkv_ref, sems,
+    att_ref, probs_ref, query_ref, key_ref, value_ref, unit_scale_ref, window_ref,
+    w_qkv_ref, sems,
 ):
     copies = []
     for n in range(3):
@@ -75,6 +75,7 @@
         copies[-1].start()
     key_mask, query_mask = mask_features(*last_window(rows, cols))
     x = jnp.concatenate([x0_ref[...], x1_ref[...], x2_ref[...], x3_ref[...]], axis=0)
+    window_ref[...] = x
     for col in range(0, 3 * C, TOK):
         if col % C == 0:
             copies[col // C].wait()
@@ -109,8 +110,7 @@
 
 
 def norm_kernel(
-    att_ref, g0_ref, g1_ref, g2_ref, g3_ref, order_ref, w_proj_ref, gain_ref,
-    near_ref, far_ref, grad_att_ref,
+    att_ref, g0_ref, g1_ref, g2_ref, g3_ref, w_proj_ref, gain_ref, grad_mix_ref, grad_att_ref
 ):
     g = jnp.concatenate([g0_ref[...], g1_ref[...], g2_ref[...], g3_ref[...]], axis=0)
     mixed = dot(att_ref[...], w_proj_ref[...], TN)
@@ -124,22 +124,14 @@
         - normed * jnp.mean(grad_norm * normed, axis=-1, keepdims=True)
     )
     grad_mix = grad_mix.astype(BF)
-    for row in range(0, C, TOK):
-        att = dot(order_ref[row : row + TOK, :], att_ref[...]).astype(BF)
-        out_ref = near_ref if row < C // 2 else far_ref
-        out_ref[row % (C // 2) : row % (C // 2) + TOK, :] = dot(att, grad_mix).astype(BF)
+    grad_mix_ref[...] = grad_mix
     for row in range(0, C, TOK):
         grad_att_ref[row : row + TOK, :] = dot(
             w_proj_ref[row : row + TOK, :], grad_mix, NT
         ).astype(BF)
 
 
-def value_kernel(
-    x0_ref, x1_ref, x2_ref, x3_ref, order_ref, probs_ref, grad_att_ref,
-    near_ref, far_ref, grad_value_ref,
-):
-    tokens = jnp.concatenate([x0_ref[...], x1_ref[...], x2_ref[...], x3_ref[...]], axis=0)
-
+def value_kernel(probs_ref, grad_att_ref, grad_value_ref):
     def head(h, carry):
         rows = head_rows(h)
         grad_value_ref[rows, :] = dot(
@@ -148,46 +140,74 @@
         return carry
 
     lax.fori_loop(0, HEADS, head, 0, unroll=8)
-    grad_value = grad_value_ref[...]
-    for row in range(0, C, TOK):
-        x = dot(order_ref[row : row + TOK, :], tokens, NT).astype(BF)
-        out_ref = near_ref if row < C // 2 else far_ref
-        out_ref[row % (C // 2) : row % (C // 2) + TOK, :] = dot(x, grad_value, NT).astype(BF)
+
+
+def write_blocks(out_refs, col, term):
+    for n, out_ref in enumerate(out_refs):
+        out_ref[:, col : col + TOK] = term[n * 128 : n * 128 + 128].astype(BF)
+
+
+def proj_term_kernel(order_ref, att_ref, att2_ref, grad_mix_ref, grad_mix2_ref, *out_refs):
+    att = jnp.concatenate([att_ref[...], att2_ref[...]], axis=1)
+    grad_mix = jnp.concatenate([grad_mix_ref[...], grad_mix2_ref[...]], axis=0)
+    left = dot(order_ref[...], att).astype(BF)
+    for col in range(0, C, TOK):
+        write_blocks(out_refs, col, dot(left, grad_mix[:, col : col + TOK]))
+
+
+def value_term_kernel(order_ref, x_ref, x2_ref, grad_value_ref, grad_value2_ref, *out_refs):
+    x = jnp.concatenate([x_ref[...], x2_ref[...]], axis=0)
+    grad_value = jnp.concatenate([grad_value_ref[...], grad_value2_ref[...]], axis=1)
+    left = dot(order_ref[...], x, NT).astype(BF)
+    for col in range(0, C, TOK):
+        write_blocks(out_refs, col, dot(left, grad_value[col : col + TOK, :], NT))
+
+
+def sum_kernel(*refs):
+    ins, out_refs = refs[:8], refs[8:]
+    for group in range(2):
+        own, *others = ins[group * 4 : group * 4 + 4]
+        total = own[...].astype(F32)
+        for other in others:
+            total += other[...].astype(F32)
+        total = total.astype(BF)
+        for n in range(4):
+            out_refs[group * 4 + n][...] = total[n * 32 : n * 32 + 32]
 
 
 def score_kernel(
-    probs_ref, grad_att_ref, query_ref, key_ref, value_ref, q_scale_ref, k_scale_ref,
+    first, count, probs_ref, grad_att_ref, query_ref, key_ref, value_ref, unit_scale_ref,
     scale_ref, after_ref, grad_query_ref, grad_key_ref, grad_score_ref,
 ):
-    first = pl.program_id(0) * STEP
-
     def scores(n, carry):
-        rows = head_rows(n)
-        probs = probs_ref[n]
+        h = n + first
+        rows = head_rows(h)
+        probs = probs_ref[h]
         grad_prob = dot(value_ref[rows, :], grad_att_ref[rows, :], TN)
         mean = jnp.sum(grad_prob * probs, axis=0, keepdims=True)
-        grad_score_ref[n] = (scale_ref[first + n] * (probs * (grad_prob - mean))).astype(BF)
+        grad_score_ref[n] = (scale_ref[h] * (probs * (grad_prob - mean))).astype(BF)
         return carry
 
     def units(n, carry):
-        rows = head_rows(n)
+        h = n + first
+        rows, out_rows = head_rows(h), head_rows(n)
         query = query_ref[rows, :]
         key = key_ref[rows, :]
         grad_score = grad_score_ref[n]
         grad_query = dot(key.astype(BF), grad_score)
         grad_key = dot(grad_score, query.astype(BF), NT).T
-        grad_query = q_scale_ref[pl.ds(n, 1), :] * (
+        grad_query = unit_scale_ref[pl.ds(h, 1), :] * (
             grad_query - query * jnp.sum(grad_query * query, axis=0, keepdims=True)
         )
-        grad_key = k_scale_ref[pl.ds(n, 1), :] * (
+        grad_key = unit_scale_ref[pl.ds(h + HEADS, 1), :] * (
             grad_key - key * jnp.sum(grad_key * key, axis=0, keepdims=True)
         )
-        grad_query_ref[rows, :] = grad_query.astype(BF)
-        grad_key_ref[rows, :] = grad_key.astype(BF)
+        grad_query_ref[out_rows, :] = grad_query.astype(BF)
+        grad_key_ref[out_rows, :] = grad_key.astype(BF)
         return carry
 
-    lax.fori_loop(0, STEP, scores, 0, unroll=STEP)
-    lax.fori_loop(0, STEP, units, 0, unroll=STEP)
+    lax.fori_loop(0, count, scores, 0, unroll=8)
+    lax.fori_loop(0, count, units, 0, unroll=16)
 
 
 def input_kernel(*refs):
@@ -231,6 +251,7 @@
     flat_bf = shape((C, TOK), BF)
     outs = (
         flat_bf, shape((HEADS, TOK, TOK), F32), flat, flat, flat_bf, shape((2 * HEADS, TOK), F32),
+        shape((TOK, C), BF),
     )
     kernel = functools.partial(attention_kernel, rows, cols)
     scratch = [pltpu.VMEM((C, 3 * C), BF), pltpu.SemaphoreType.DMA((3,))]
@@ -240,48 +261,33 @@
     )(*quads, pltpu.with_memory_space_constraint(w_qkv, pltpu.HBM), scale)
 
 
-def output_norm(att, quads, order, w_proj, gain):
-    half = shape((C // 2, C), BF)
-    return call(norm_kernel, (half, half, shape((C, TOK), BF)), [VM] * 8, 3, "norm_part", 24)(
-        att, *quads, order, w_proj, gain
-    )
-
-
-def value_grads(quads, order, probs, grad_att):
-    half = shape((C // 2, C), BF)
-    return call(value_kernel, (half, half, shape((C, TOK), BF)), [VM] * 7, 4, "value_part", 24)(
-        *quads, order, probs, grad_att
-    )
-
-
-def score_grads(probs, grad_att, query, key, value, unit_scale, scale, after):
-    wide = pl.BlockSpec((STEP * DIM, TOK), lambda n: (n, 0))
-    steps = HEADS // STEP
-    streamed = [
-        pltpu.with_memory_space_constraint(array, pltpu.HBM)
-        for array in (probs, grad_att, query, key, value)
-    ]
-    return pl.pallas_call(
-        score_kernel,
-        out_shape=(shape((C, TOK), BF),) * 2,
-        grid=(steps,),
-        in_specs=[
-            pl.BlockSpec((STEP, TOK, TOK), lambda n: (n, 0, 0)),
-            wide,
-            wide,
-            wide,
-            wide,
-            pl.BlockSpec((STEP, TOK), lambda n: (n, 0)),
-            pl.BlockSpec((STEP, TOK), lambda n: (n + steps, 0)),
-            SM,
-            pl.BlockSpec(memory_space=pl.ANY),
-        ],
-        out_specs=(wide, wide),
-        scratch_shapes=[pltpu.VMEM((STEP, TOK, TOK), BF)],
-        compiler_params=pltpu.CompilerParams(vmem_limit_bytes=24 * MIB),
-        cost_estimate=pl.CostEstimate(flops=10**8, bytes_accessed=MIB, transcendentals=0),
-        name="score_part",
-    )(*streamed, unit_scale, unit_scale, scale, after)
+def output_norm(att, quads, w_proj, gain):
+    outs = (shape((TOK, C), BF), shape((C, TOK), BF))
+    return call(norm_kernel, outs, [VM] * 7, 2, "norm_part", 24)(att, *quads, w_proj, gain)
+
+
+def value_grads(probs, grad_att):
+    return call(value_kernel, shape((C, TOK), BF), [VM] * 2, 2, "value_part", 24)(probs, grad_att)
+
+
+def proj_terms(*args):
+    return call(proj_term_kernel, (shape((128, C), BF),) * 4, [VM] * 5, 1.3, "proj_term", 24)(*args)
+
+
+def value_terms(*args):
+    return call(value_term_kernel, (shape((128, C), BF),) * 4, [VM] * 5, 1.3, "value_term", 24)(*args)
+
+
+def score_grads(first, count, *args):
+    outs = (shape((count * DIM, TOK), BF),) * 2
+    scratch = [pltpu.VMEM((count, TOK, TOK), BF)]
+    kernel = functools.partial(score_kernel, first, count)
+    ins = [VM] * 6 + [SM, pl.BlockSpec(memory_space=pl.ANY)]
+    return call(kernel, outs, ins, 0.3, "score_part", 32, scratch)(*args)
+
+
+def block_sums(blocks):
+    return call(sum_kernel, (shape((32, C), BF),) * 8, [VM] * 8, 0.5, "block_sums", 24)(*blocks)
 
 
 def input_grad(parts, w_qkv):
@@ -323,30 +329,33 @@
     return lax.ppermute(array, BOTH, pairs)
 
 
-def row_order():
-    place = jnp.arange(C, dtype=jnp.int32)
-    far, x, y, z, row = place // 512, place // 128 % 4, place // 32 % 4, place // 4 % 8, place % 4
-    core = (lax.axis_index("row") + far) % 2
-    source = z * 128 + x // 2 * 64 + core * 32 + y * 8 + x % 2 * 4 + row
+def moved(array, axis, by):
+    pairs = []
+    for x, y, z, core in CHIPS:
+        to = ((x + by) % 4, y) if axis == "x" else (x, (y + by) % 4)
+        pairs.append((line(x, y, z, core), line(*to, z, core)))
+    return lax.ppermute(array, BOTH, pairs)
+
+
+def gathered(blocks, axis):
+    far = moved(blocks[2], axis, 2)
+    return far, moved(blocks[1], axis, 1), moved(blocks[3], axis, -1)
+
+
+def row_order(axis):
+    place = jnp.arange(C // 2, dtype=jnp.int32)
+    a, b, z, row = place // 128, place // 32 % 4, place // 4 % 8, place % 4
+    r, c = lax.axis_index("row"), lax.axis_index("col")
+    dx, dy = (a, b) if axis == "x" else (b, a)
+    x = (r // 2 % 2 * 2 + c % 2 + dx) % 4
+    y = (c // 2 + dy) % 4
+    source = z * 128 + x // 2 * 64 + r % 2 * 32 + y * 8 + x % 2 * 4 + row
     return (source[:, None] == jnp.arange(C, dtype=jnp.int32)[None, :]).astype(BF)
-
-
-def plus(*terms):
-    return sum(term.astype(F32) for term in terms).astype(BF)
 
 
 def group_sum(blocks, groups):
     got = lax.all_to_all(blocks, BOTH, 0, 0, axis_index_groups=groups, tiled=True)
     return jnp.sum(got.astype(F32), axis=0)
-
-
-def plane_sum(blocks):
-    groups = [
-        [line(x, y, z, core) for x in range(4) for y in range(4)]
-        for z in range(8)
-        for core in range(2)
-    ]
-    return group_sum(blocks, groups).astype(BF)
 
 
 def z_sum(blocks):
@@ -363,26 +372,32 @@
     rows, cols = lax.axis_size("row"), lax.axis_size("col")
     x = window(tokens, rows, cols)
     g = window(grad_out, rows, cols)
-    att, probs, query, key, value, unit_scale = attention(x, w_qkv, logit_scale, rows, cols)
-    order = row_order()
-    proj, far, grad_att = output_norm(att, g, order, w_proj, norm_gain.reshape(1, C))
-    proj_far = other_core(far)
-    val, far, grad_value = value_grads(x, order, probs, grad_att)
+    att, probs, query, key, value, unit_scale, tokens_win = attention(
+        x, w_qkv, logit_scale, rows, cols
+    )
+    grad_mix, grad_att = output_norm(att, g, w_proj, norm_gain.reshape(1, C))
+    grad_value = value_grads(probs, grad_att)
+    proj = proj_terms(row_order("x"), att, other_core(att), grad_mix, other_core(grad_mix))
+    val = value_terms(
+        row_order("y"), tokens_win, other_core(tokens_win), grad_value, other_core(grad_value)
+    )
+    proj_got, val_got = gathered(proj, "x"), gathered(val, "y")
+    args = (probs, grad_att, query, key, value, unit_scale, logit_scale)
+    half = HEADS // 2
+    early = score_grads(0, half, *args, val[0])
+    late = score_grads(half, half, *args, proj_got[0])
+    parts = [early[0], late[0], early[1], late[1], grad_value]
+    grad_input = input_grad(parts, w_qkv)
+    grad_input, proj_got, val_got = lax.optimization_barrier((grad_input, proj_got, val_got))
+    blocks = block_sums((proj[0], *proj_got, val[0], *val_got))
+    proj, val = blocks[:4], blocks[4:]
+    proj_got, val_got = gathered(proj, "y"), gathered(val, "x")
+    proj, val, grad_input = lax.optimization_barrier(
+        ((proj[0], *proj_got), (val[0], *val_got), grad_input)
+    )
     terms = jnp.concatenate(
-        [
-            plus(proj, proj_far).reshape(16, 32, C),
-            plus(val, other_core(far)).reshape(16, 32, C),
-        ],
+        [sum(a.astype(F32) for a in part).reshape(8, 4, C).astype(BF) for part in (proj, val)],
         axis=1,
-    )
-
-    grad_query, grad_key = score_grads(
-        probs, grad_att, query, key, value, unit_scale, logit_scale, terms
-    )
-    terms = plane_sum(terms)
-    grad_input = input_grad([grad_query, grad_key, grad_value], w_qkv)
-    terms = jnp.concatenate(
-        [terms[:32].reshape(8, 4, C), terms[32:].reshape(8, 4, C)], axis=1
     )
     terms = z_sum(terms)
     proj_part, value_part = terms[:4], terms[4:]

time: 99.4 us -> 89.1 us (0.90)
  waiting for transfers between devices: 27.3 us -> 16 us
  starting transfers between devices: 35.1 us -> 41.3 us
  other arithmetic: 6.13 us -> 2.46 us
  Pallas kernels: 25.8 us -> 24.3 us
    ppermute x9, waiting for transfers between devices: 18 us -> 1.74 us  [passed(): return lax.ppermute(array, ('row', 'col'), pairs)]
    ppermute x0 -> x12, starting transfers between devices: none -> 12.1 us  [moved(): return lax.ppermute(array, BOTH, pairs)]
    all_to_all x2 -> x1, starting transfers between devices: 13.3 us -> 3.89 us  [group_sum(): lax.all_to_all(blocks, BOTH, 0, 0, axis_index_groups=groups, tiled=True)]
    ppermute x0 -> x12, waiting for transfers between devices: none -> 8.44 us  [moved(): return lax.ppermute(array, BOTH, pairs)]
    ppermute x2 -> x4, waiting for transfers between devices: 3.28 us -> 0.01 us  [other_core(): return lax.ppermute(array, BOTH, pairs)]
    ppermute x9, starting transfers between devices: 20.7 us -> 22.9 us  [passed(): return lax.ppermute(array, ('row', 'col'), pairs)]
    concatenate x2 -> x1, other arithmetic: 2.31 us -> 0.72 us  [per_device(): jnp.concatenate([sum((a.astype(F32) for a in part)).reshape(8, 4, C).asty...]
    pallas_call x3 -> x7, Pallas kernels: 14.2 us -> 12.7 us  [the longest x2 6.24 us: score_grads(): return call(kernel, outs, ins, 0.3, 'score_part', 32, scratch)(*args)]
  transfers between devices with their start and end apart: 13 -> 26, of which waited for: 5 -> 7; matrix products, arithmetic and copies ran while one was open for 4% -> 4% of each run, Pallas kernels for 20% -> 27%
where the time goes in v2:
time: 89.1 us; the launch traced here: 88.8 us
  starting transfers between devices  41.3 us (46%)
  Pallas kernels  24.3 us (27%)
  waiting for transfers between devices  16 us (18%)
  local copies, waits for them, and re-layouts  3.89 us (4%)
  other arithmetic  2.46 us (3%)
  between operations  0.9 us (1%)
    ppermute x9, starting transfers between devices, passed(): return lax.ppermute(array, ('row', 'col'), pairs)  22.9 us
    ppermute x12, starting transfers between devices, moved(): return lax.ppermute(array, BOTH, pairs)  12.1 us
    pallas_call x1, Pallas kernels, attention(): call(kernel, outs, [VM] * 4 + [pl.BlockSpec(memory_space=pltpu.HBM), SM],...  9.7 us
    ppermute x12, waiting for transfers between devices, moved(): return lax.ppermute(array, BOTH, pairs)  8.44 us
    pallas_call x2, Pallas kernels, score_grads(): return call(kernel, outs, ins, 0.3, 'score_part', 32, scratch)(*args)  6.24 us
    all_to_all x1, waiting for transfers between devices, group_sum(): lax.all_to_all(blocks, BOTH, 0, 0, axis_index_groups=groups, tiled=True)  5.81 us
    all_to_all x1, starting transfers between devices, group_sum(): lax.all_to_all(blocks, BOTH, 0, 0, axis_index_groups=groups, tiled=True)  3.89 us
    ppermute x4, starting transfers between devices, other_core(): return lax.ppermute(array, BOTH, pairs)  2.42 us
  transfers between devices with their start and end apart: 26, of which 7 were waited for; matrix products, arithmetic and copies ran while one was open for 4% of the time, Pallas kernels for 27%

profile of v2, /device:TPU:1, one launch (start us, length us, event | category | flops | bytes accessed | tf_op | source)
XLA Modules:
  0.0 88.8 jit_solution(5634766065101900745)
XLA Ops:
  1.8 4.6 %collective-permute-start = (bf16[64,1024]{1,0:T(8,128)(2,1)S(1)}, bf16[64,1024]{1,0:T(8,128)(2,1)S(1)}, u32[]{:S(2)}, u32[]{:S(2)}) collective-permute-start(bf16[64,1024]{1,0:T(8,128)(2,1)S(1)} %get-tuple-element.118), channel_id=1, source_target_pairs={{0,7},{1,0},{2,1},{3,2},{4,3},{5,4},{6,5},{7,6},{8,15},{9,8},{10,9... | collective-permute-start | bytes 393224 | tf_op jit(solution)/shard_map/ppermute | solution.py:304
  7.3 7.0 %collective-permute-start.2 = (bf16[64,1024]{1,0:T(8,128)(2,1)S(1)}, bf16[64,1024]{1,0:T(8,128)(2,1)S(1)}, u32[]{:S(2)}, u32[]{:S(2)}) collective-permute-start(bf16[64,1024]{1,0:T(8,128)(2,1)S(1)} %get-tuple-element.117), channel_id=1, source_target_pairs={{0,255},{1,248},{2,249},{3,250},{4,251},{5,252},{6,253},{7,254},{8... | collective-permute-start | bytes 393224 | tf_op jit(solution)/shard_map/ppermute | solution.py:304
  15.4 1.8 %collective-permute-start.4 = (bf16[64,1024]{1,0:T(8,128)(2,1)S(1)}, bf16[64,1024]{1,0:T(8,128)(2,1)S(1)}, u32[]{:S(2)}, u32[]{:S(2)}) collective-permute-start(bf16[64,1024]{1,0:T(8,128)(2,1)S(1)} %get-tuple-element.114), channel_id=1, source_target_pairs={{0,7},{1,0},{2,1},{3,2},{4,3},{5,4},{6,5},{7,6},{8,15},{9,8},{10,9... | collective-permute-start | bytes 393224 | tf_op jit(solution)/shard_map/ppermute | solution.py:304
  18.4 9.7 %attention_part.1 = (bf16[1024,256]{1,0:T(8,128)(2,1)S(1)}, f32[32,256,256]{2,1,0:T(8,128)S(1)}, f32[1024,256]{1,0:T(8,128)S(1)}, f32[1024,256]{1,0:T(8,128)S(1)...) custom-call(bf16[64,1024]{1,0:T(8,128)(2,1)S(1)} %get-tuple-element.119.x0_ref, ...), custom_call_target="tpu_custom_call" | custom-call | flops 15399999488 | bytes 1048576 | tf_op jit(solution)/shard_map/attention_part/pallas_call | solution.py:258
  28.1 1.5 %collective-permute-start.3 = (bf16[1024,256]{1,0:T(8,128)(2,1)S(1)}, bf16[1024,256]{1,0:T(8,128)(2,1)S(1)}, u32[]{:S(2)}, u32[]{:S(2)}) collective-permute-start(bf16[1024,256]{1,0:T(8,128)(2,1)S(1)} %get-tuple-element.58.att_ref), channel_id=1, source_target_pairs={{0,8},{8,0},{32,40},{40,32},{64,72},{72,64},{96,104},{104,96},{128... | collective-permute-start | bytes 1572872 | tf_op jit(solution)/shard_map/ppermute | solution.py:329
  29.6 2.0 %norm_part.1 = (bf16[256,1024]{1,0:T(8,128)(2,1)S(1)}, bf16[1024,256]{1,0:T(8,128)(2,1)S(1)}) custom-call(bf16[1024,256]{1,0:T(8,128)(2,1)S(1)} %get-tuple-element.58.att_ref, bf16[64,1024]{1,0:T(8,128)(2,1)S(1)} %get-tuple-element.115.g0_ref, bf16[64,1024]{1,0:T(8,128)(2,1)S(1)} %collective-permute-done.4.g1_ref, ...), custom_call_target="tpu_custom_call" | custom-call | flops 2200000000 | bytes 1048576 | tf_op jit(solution)/shard_map/norm_part/pallas_call | solution.py:266
  32.2 1.7 %value_part.1.grad_value_ref.refs_4_ = bf16[1024,256]{1,0:T(8,128)(2,1)S(1)} custom-call(f32[32,256,256]{2,1,0:T(8,128)S(1)} %get-tuple-element.61.probs_ref, bf16[1024,256]{1,0:T(8,128)(2,1)S(1)} %get-tuple-element.62.grad_att_ref), custom_call_target="tpu_custom_call" | custom-call | flops 2200000000 | bytes 1048576 | tf_op jit(solution)/shard_map/value_part/pallas_call | solution.py:270
  34.5 1.3 %proj_term.1 = (bf16[128,1024]{1,0:T(8,128)(2,1)S(1)}, bf16[128,1024]{1,0:T(8,128)(2,1)S(1)}, bf16[128,1024]{1,0:T(8,128)(2,1)S(1)}, bf16[128,1024]{1,0:T(8,128)(2,1)S(1)}) custom-call(bf16[512,1024]{1,0:T(8,128)(2,1)S(1)} %fusion.order_ref, bf16[1024,256]{1,0:T(8,128)(2,1)S(1)} %get-tuple-element.58.att_ref, ...), custom_call_target="tpu_custom_call" | custom-call | flops 1430000000 | bytes 1048576 | tf_op jit(solution)/shard_map/proj_term/pallas_call | solution.py:274
  35.8 2.0 %collective-permute-start.10 = (bf16[128,1024]{1,0:T(8,128)(2,1)S(1)}, bf16[128,1024]{1,0:T(8,128)(2,1)S(1)}, u32[]{:S(2)}, u32[]{:S(2)}) collective-permute-start(bf16[128,1024]{1,0:T(8,128)(2,1)S(1)} %get-tuple-element.70), channel_id=1, source_target_pairs={{0,16},{8,24},{32,48},{40,56},{64,80},{72,88},{96,112},{104,120},{... | collective-permute-start | bytes 786440 | tf_op jit(solution)/shard_map/ppermute | solution.py:337
  38.3 2.5 %collective-permute-start.12 = (bf16[128,1024]{1,0:T(8,128)(2,1)S(1)}, bf16[128,1024]{1,0:T(8,128)(2,1)S(1)}, u32[]{:S(2)}, u32[]{:S(2)}) collective-permute-start(bf16[128,1024]{1,0:T(8,128)(2,1)S(1)} %get-tuple-element.79), channel_id=1, source_target_pairs={{0,17},{8,25},{32,49},{40,57},{64,81},{72,89},{96,113},{104,121},{... | collective-permute-start | bytes 786440 | tf_op jit(solution)/shard_map/ppermute | solution.py:337
  40.8 1.3 %value_term.1 = (bf16[128,1024]{1,0:T(8,128)(2,1)S(1)}, bf16[128,1024]{1,0:T(8,128)(2,1)S(1)}, bf16[128,1024]{1,0:T(8,128)(2,1)S(1)}, bf16[128,1024]{1,0:T(8,128)(2,1)S(1)}) custom-call(bf16[512,1024]{1,0:T(8,128)(2,1)S(1)} %fusion.1.order_ref, bf16[256,1024]{1,0:T(8,128)(2,1)S(1)} %get-tuple-element.67.x_ref, ...), custom_call_target="tpu_custom_call" | custom-call | flops 1430000000 | bytes 1048576 | tf_op jit(solution)/shard_map/value_term/pallas_call | solution.py:278
  43.3 1.6 %collective-permute-done.10.after_ref.refs_1_ = bf16[128,1024]{1,0:T(8,128)(2,1)S(1)} collective-permute-done((bf16[128,1024]{1,0:T(8,128)(2,1)S(1)}, bf16[128,1024]{1,0:T(8,128)(2,1)S(1)}, u32[]{:S(2)}, u32[]{:S(2)}) %collective-permute-start.10) | collective-permute-done | bytes 262176 | tf_op jit(solution)/shard_map/ppermute | solution.py:337
  45.6 3.1 %score_part.2 = (bf16[512,256]{1,0:T(8,128)(2,1)S(1)}, bf16[512,256]{1,0:T(8,128)(2,1)S(1)}) custom-call(f32[32,256,256]{2,1,0:T(8,128)S(1)} %get-tuple-element.61.probs_ref, bf16[1024,256]{1,0:T(8,128)(2,1)S(1)} %get-tuple-element.62.grad_att_ref, f32[1024,256]{1,0:T(8,128)S(1)} %get-tuple-element.63.query_ref, f32[1024,256]{1,0:T(8,128)S(1)} %get-tuple-element.64.key_ref, ...), custom_call_target="tpu_custom_call" | custom-call | flops 330000000 | bytes 1048576 | tf_op jit(solution)/shard_map/score_part/pallas_call | solution.py:286
  48.7 3.1 %score_part.3 = (bf16[512,256]{1,0:T(8,128)(2,1)S(1)}, bf16[512,256]{1,0:T(8,128)(2,1)S(1)}) custom-call(f32[32,256,256]{2,1,0:T(8,128)S(1)} %get-tuple-element.61.probs_ref, bf16[1024,256]{1,0:T(8,128)(2,1)S(1)} %get-tuple-element.62.grad_att_ref, f32[1024,256]{1,0:T(8,128)S(1)} %get-tuple-element.63.query_ref, f32[1024,256]{1,0:T(8,128)S(1)} %get-tuple-element.64.key_ref, ...), custom_call_target="tpu_custom_call" | custom-call | flops 330000000 | bytes 1048576 | tf_op jit(solution)/shard_map/score_part/pallas_call | solution.py:286
  51.9 1.9 %input_part.1 = (bf16[64,1024]{1,0:T(8,128)(2,1)S(1)}, bf16[64,1024]{1,0:T(8,128)(2,1)S(1)}, bf16[64,1024]{1,0:T(8,128)(2,1)S(1)}, bf16[64,1024]{1,0:T(8,128)(2,1)S(1)}) custom-call(bf16[512,256]{1,0:T(8,128)(2,1)S(1)} %get-tuple-element.69.refs_0_, bf16[512,256]{1,0:T(8,128)(2,1)S(1)} %get-tuple-element.71.refs_1_, ...), custom_call_target="tpu_custom_call" | custom-call | flops 220000000 | bytes 1048576 | tf_op jit(solution)/shard_map/input_part/pallas_call | solution.py:295
  53.8 3.7 %collective-permute-done.14.refs_6_ = bf16[128,1024]{1,0:T(8,128)(2,1)S(1)} collective-permute-done((bf16[128,1024]{1,0:T(8,128)(2,1)S(1)}, bf16[128,1024]{1,0:T(8,128)(2,1)S(1)}, u32[]{:S(2)}, u32[]{:S(2)}) %collective-permute-start.14) | collective-permute-done | bytes 262176 | tf_op jit(solution)/shard_map/ppermute | solution.py:337
  59.2 2.1 %collective-permute-start.18 = (bf16[32,1024]{1,0:T(8,128)(2,1)S(1)}, bf16[32,1024]{1,0:T(8,128)(2,1)S(1)}, u32[]{:S(2)}, u32[]{:S(2)}) collective-permute-start(bf16[32,1024]{1,0:T(8,128)(2,1)S(1)} %get-tuple-element.92), channel_id=1, source_target_pairs={{0,6},{8,14},{32,38},{40,46},{64,70},{72,78},{96,102},{104,110},{1... | collective-permute-start | bytes 196616 | tf_op jit(solution)/shard_map/ppermute | solution.py:337
  62.6 1.4 %collective-permute-start.21 = (bf16[32,1024]{1,0:T(8,128)(2,1)S(1)}, bf16[32,1024]{1,0:T(8,128)(2,1)S(1)}, u32[]{:S(2)}, u32[]{:S(2)}) collective-permute-start(bf16[32,1024]{1,0:T(8,128)(2,1)S(1)} %get-tuple-element.96), channel_id=1, source_target_pairs={{0,17},{8,25},{32,49},{40,57},{64,81},{72,89},{96,113},{104,121},{... | collective-permute-start | bytes 196616 | tf_op jit(solution)/shard_map/ppermute | solution.py:337
  64.0 2.0 %collective-permute-done.19 = bf16[32,1024]{1,0:T(8,128)(2,1)S(1)} collective-permute-done((bf16[32,1024]{1,0:T(8,128)(2,1)S(1)}, bf16[32,1024]{1,0:T(8,128)(2,1)S(1)}, u32[]{:S(2)}, u32[]{:S(2)}) %collective-permute-start.19) | collective-permute-done | bytes 65568 | tf_op jit(solution)/shard_map/ppermute | solution.py:337
  66.3 1.7 %collective-permute-start.24 = (bf16[64,1024]{1,0:T(8,128)(2,1)S(1)}, bf16[64,1024]{1,0:T(8,128)(2,1)S(1)}, u32[]{:S(2)}, u32[]{:S(2)}) collective-permute-start(bf16[64,1024]{1,0:T(8,128)(2,1)S(1)} %get-tuple-element.103), channel_id=1, source_target_pairs={{0,1},{1,2},{2,3},{3,4},{4,5},{5,6},{6,7},{7,0},{8,9},{9,10},{10,1... | collective-permute-start | bytes 393224 | tf_op jit(solution)/shard_map/ppermute | solution.py:304
  68.1 5.8 %collective-permute-start.23 = (bf16[64,1024]{1,0:T(8,128)(2,1)S(1)}, bf16[64,1024]{1,0:T(8,128)(2,1)S(1)}, u32[]{:S(2)}, u32[]{:S(2)}) collective-permute-start(bf16[64,1024]{1,0:T(8,128)(2,1)S(1)} %get-tuple-element.102), channel_id=1, source_target_pairs={{0,8},{1,9},{2,10},{3,11},{4,12},{5,13},{6,14},{7,15},{8,16},{9,17... | collective-permute-start | bytes 393224 | tf_op jit(solution)/shard_map/ppermute | solution.py:304
  74.7 3.9 %all-to-all-start = ((bf16[8,8,1024]{2,1,0:T(8,128)(2,1)}), bf16[8,8,1024]{2,1,0:T(8,128)(2,1)S(1)}, u32[]{:S(2)}, u32[]{:S(2)}) async-start(bf16[8,8,1024]{2,1,0:T(8,128)(2,1)} %pad_maximum_fusion.1), calls=%async_computation | async-start | bytes 262144 | tf_op jit(solution)/shard_map/all_to_all | solution.py:357
  78.6 1.7 %collective-permute-done.22 = bf16[64,1024]{1,0:T(8,128)(2,1)S(1)} collective-permute-done((bf16[64,1024]{1,0:T(8,128)(2,1)S(1)}, bf16[64,1024]{1,0:T(8,128)(2,1)S(1)}, u32[]{:S(2)}, u32[]{:S(2)}) %collective-permute-start.22) | collective-permute-done | bytes 131104 | tf_op jit(solution)/shard_map/ppermute | solution.py:304
  82.4 5.8 %all-to-all-done = bf16[8,8,1024]{2,1,0:T(8,128)(2,1)S(1)} async-done(((bf16[8,8,1024]{2,1,0:T(8,128)(2,1)}), bf16[8,8,1024]{2,1,0:T(8,128)(2,1)S(1)}, u32[]{:S(2)}, u32[]{:S(2)}) %all-to-all-start) | async-done | bytes 131104 | tf_op jit(solution)/shard_map/all_to_all | solution.py:357
  (66 shorter events, 14.8 us)
Async XLA Ops:
  1.8 15.5 %collective-permute-start = (bf16[64,1024]{1,0:T(8,128)(2,1)S(1)}, bf16[64,1024]{1,0:T(8,128)(2,1)S(1)}, u32[]{:S(2)}, u32[]{:S(2)}) collective-permute-start(bf16[64,1024]{1,0:T(8,128)(2,1)S(1)} %get-tuple-element.118), channel_id=1, source_target_pairs={{0,7},{1,0},{2,1},{3,2},{4,3},{5,4},{6,5},{7,6},{8,15},{9,8},{10,9... | collective-permute-start | bytes 393224 | tf_op jit(solution)/shard_map/ppermute | solution.py:304
  6.3 12.0 %collective-permute-start.1 = (bf16[64,1024]{1,0:T(8,128)(2,1)S(1)}, bf16[64,1024]{1,0:T(8,128)(2,1)S(1)}, u32[]{:S(2)}, u32[]{:S(2)}) collective-permute-start(bf16[64,1024]{1,0:T(8,128)(2,1)S(1)} %get-tuple-element.120), channel_id=1, source_target_pairs={{0,248},{1,249},{2,250},{3,251},{4,252},{5,253},{6,254},{7,255},{8... | collective-permute-start | bytes 393224 | tf_op jit(solution)/shard_map/ppermute | solution.py:304
  7.3 11.1 %collective-permute-start.2 = (bf16[64,1024]{1,0:T(8,128)(2,1)S(1)}, bf16[64,1024]{1,0:T(8,128)(2,1)S(1)}, u32[]{:S(2)}, u32[]{:S(2)}) collective-permute-start(bf16[64,1024]{1,0:T(8,128)(2,1)S(1)} %get-tuple-element.117), channel_id=1, source_target_pairs={{0,255},{1,248},{2,249},{3,250},{4,251},{5,252},{6,253},{7,254},{8... | collective-permute-start | bytes 393224 | tf_op jit(solution)/shard_map/ppermute | solution.py:304
  15.4 14.2 %collective-permute-start.4 = (bf16[64,1024]{1,0:T(8,128)(2,1)S(1)}, bf16[64,1024]{1,0:T(8,128)(2,1)S(1)}, u32[]{:S(2)}, u32[]{:S(2)}) collective-permute-start(bf16[64,1024]{1,0:T(8,128)(2,1)S(1)} %get-tuple-element.114), channel_id=1, source_target_pairs={{0,7},{1,0},{2,1},{3,2},{4,3},{5,4},{6,5},{7,6},{8,15},{9,8},{10,9... | collective-permute-start | bytes 393224 | tf_op jit(solution)/shard_map/ppermute | solution.py:304
  17.2 12.4 %collective-permute-start.5 = (bf16[64,1024]{1,0:T(8,128)(2,1)S(1)}, bf16[64,1024]{1,0:T(8,128)(2,1)S(1)}, u32[]{:S(2)}, u32[]{:S(2)}) collective-permute-start(bf16[64,1024]{1,0:T(8,128)(2,1)S(1)} %get-tuple-element.116), channel_id=1, source_target_pairs={{0,248},{1,249},{2,250},{3,251},{4,252},{5,253},{6,254},{7,255},{8... | collective-permute-start | bytes 393224 | tf_op jit(solution)/shard_map/ppermute | solution.py:304
  17.3 12.4 %collective-permute-start.6 = (bf16[64,1024]{1,0:T(8,128)(2,1)S(1)}, bf16[64,1024]{1,0:T(8,128)(2,1)S(1)}, u32[]{:S(2)}, u32[]{:S(2)}) collective-permute-start(bf16[64,1024]{1,0:T(8,128)(2,1)S(1)} %get-tuple-element.113), channel_id=1, source_target_pairs={{0,255},{1,248},{2,249},{3,250},{4,251},{5,252},{6,253},{7,254},{8... | collective-permute-start | bytes 393224 | tf_op jit(solution)/shard_map/ppermute | solution.py:304
  28.1 6.4 %collective-permute-start.3 = (bf16[1024,256]{1,0:T(8,128)(2,1)S(1)}, bf16[1024,256]{1,0:T(8,128)(2,1)S(1)}, u32[]{:S(2)}, u32[]{:S(2)}) collective-permute-start(bf16[1024,256]{1,0:T(8,128)(2,1)S(1)} %get-tuple-element.58.att_ref), channel_id=1, source_target_pairs={{0,8},{8,0},{32,40},{40,32},{64,72},{72,64},{96,104},{104,96},{128... | collective-permute-start | bytes 1572872 | tf_op jit(solution)/shard_map/ppermute | solution.py:329
  31.7 9.1 %collective-permute-start.8 = (bf16[256,1024]{1,0:T(8,128)(2,1)S(1)}, bf16[256,1024]{1,0:T(8,128)(2,1)S(1)}, u32[]{:S(2)}, u32[]{:S(2)}) collective-permute-start(bf16[256,1024]{1,0:T(8,128)(2,1)S(1)} %get-tuple-element.67.x_ref), channel_id=1, source_target_pairs={{0,8},{8,0},{32,40},{40,32},{64,72},{72,64},{96,104},{104,96},{128... | collective-permute-start | bytes 1572872 | tf_op jit(solution)/shard_map/ppermute | solution.py:329
  33.9 7.0 %collective-permute-start.9 = (bf16[1024,256]{1,0:T(8,128)(2,1)S(1)}, bf16[1024,256]{1,0:T(8,128)(2,1)S(1)}, u32[]{:S(2)}, u32[]{:S(2)}) collective-permute-start(bf16[1024,256]{1,0:T(8,128)(2,1)S(1)} %value_part.1.grad_value_ref.refs_4_), channel_id=1, source_target_pairs={{0,8},{8,0},{32,40},{40,32},{64,72},{72,64},{96,104},{104,96},{128... | collective-permute-start | bytes 1572872 | tf_op jit(solution)/shard_map/ppermute | solution.py:329
  35.8 9.1 %collective-permute-start.10 = (bf16[128,1024]{1,0:T(8,128)(2,1)S(1)}, bf16[128,1024]{1,0:T(8,128)(2,1)S(1)}, u32[]{:S(2)}, u32[]{:S(2)}) collective-permute-start(bf16[128,1024]{1,0:T(8,128)(2,1)S(1)} %get-tuple-element.70), channel_id=1, source_target_pairs={{0,16},{8,24},{32,48},{40,56},{64,80},{72,88},{96,112},{104,120},{... | collective-permute-start | bytes 786440 | tf_op jit(solution)/shard_map/ppermute | solution.py:337
  38.1 15.7 %collective-permute-start.11 = (bf16[128,1024]{1,0:T(8,128)(2,1)S(1)}, bf16[128,1024]{1,0:T(8,128)(2,1)S(1)}, u32[]{:S(2)}, u32[]{:S(2)}) collective-permute-start(bf16[128,1024]{1,0:T(8,128)(2,1)S(1)} %get-tuple-element.78), channel_id=1, source_target_pairs={{0,1},{8,9},{32,33},{40,41},{64,65},{72,73},{96,97},{104,105},{128... | collective-permute-start | bytes 786440 | tf_op jit(solution)/shard_map/ppermute | solution.py:337
  38.3 15.5 %collective-permute-start.12 = (bf16[128,1024]{1,0:T(8,128)(2,1)S(1)}, bf16[128,1024]{1,0:T(8,128)(2,1)S(1)}, u32[]{:S(2)}, u32[]{:S(2)}) collective-permute-start(bf16[128,1024]{1,0:T(8,128)(2,1)S(1)} %get-tuple-element.79), channel_id=1, source_target_pairs={{0,17},{8,25},{32,49},{40,57},{64,81},{72,89},{96,113},{104,121},{... | collective-permute-start | bytes 786440 | tf_op jit(solution)/shard_map/ppermute | solution.py:337
  42.1 11.7 %collective-permute-start.13 = (bf16[128,1024]{1,0:T(8,128)(2,1)S(1)}, bf16[128,1024]{1,0:T(8,128)(2,1)S(1)}, u32[]{:S(2)}, u32[]{:S(2)}) collective-permute-start(bf16[128,1024]{1,0:T(8,128)(2,1)S(1)} %get-tuple-element.80), channel_id=1, source_target_pairs={{0,4},{8,12},{32,36},{40,44},{64,68},{72,76},{96,100},{104,108},{1... | collective-permute-start | bytes 786440 | tf_op jit(solution)/shard_map/ppermute | solution.py:337
  42.3 15.3 %collective-permute-start.14 = (bf16[128,1024]{1,0:T(8,128)(2,1)S(1)}, bf16[128,1024]{1,0:T(8,128)(2,1)S(1)}, u32[]{:S(2)}, u32[]{:S(2)}) collective-permute-start(bf16[128,1024]{1,0:T(8,128)(2,1)S(1)} %get-tuple-element.81), channel_id=1, source_target_pairs={{0,2},{8,10},{32,34},{40,42},{64,66},{72,74},{96,98},{104,106},{12... | collective-permute-start | bytes 786440 | tf_op jit(solution)/shard_map/ppermute | solution.py:337
  44.9 12.7 %collective-permute-start.15 = (bf16[128,1024]{1,0:T(8,128)(2,1)S(1)}, bf16[128,1024]{1,0:T(8,128)(2,1)S(1)}, u32[]{:S(2)}, u32[]{:S(2)}) collective-permute-start(bf16[128,1024]{1,0:T(8,128)(2,1)S(1)} %get-tuple-element.82), channel_id=1, source_target_pairs={{0,6},{8,14},{32,38},{40,46},{64,70},{72,78},{96,102},{104,110},{1... | collective-permute-start | bytes 786440 | tf_op jit(solution)/shard_map/ppermute | solution.py:337
  57.8 4.7 %collective-permute-start.16 = (bf16[32,1024]{1,0:T(8,128)(2,1)S(1)}, bf16[32,1024]{1,0:T(8,128)(2,1)S(1)}, u32[]{:S(2)}, u32[]{:S(2)}) collective-permute-start(bf16[32,1024]{1,0:T(8,128)(2,1)S(1)} %get-tuple-element.90), channel_id=1, source_target_pairs={{0,4},{8,12},{32,36},{40,44},{64,68},{72,76},{96,100},{104,108},{1... | collective-permute-start | bytes 196616 | tf_op jit(solution)/shard_map/ppermute | solution.py:337
  58.5 5.5 %collective-permute-start.17 = (bf16[32,1024]{1,0:T(8,128)(2,1)S(1)}, bf16[32,1024]{1,0:T(8,128)(2,1)S(1)}, u32[]{:S(2)}, u32[]{:S(2)}) collective-permute-start(bf16[32,1024]{1,0:T(8,128)(2,1)S(1)} %get-tuple-element.91), channel_id=1, source_target_pairs={{0,2},{8,10},{32,34},{40,42},{64,66},{72,74},{96,98},{104,106},{12... | collective-permute-start | bytes 196616 | tf_op jit(solution)/shard_map/ppermute | solution.py:337
  59.2 4.8 %collective-permute-start.18 = (bf16[32,1024]{1,0:T(8,128)(2,1)S(1)}, bf16[32,1024]{1,0:T(8,128)(2,1)S(1)}, u32[]{:S(2)}, u32[]{:S(2)}) collective-permute-start(bf16[32,1024]{1,0:T(8,128)(2,1)S(1)} %get-tuple-element.92), channel_id=1, source_target_pairs={{0,6},{8,14},{32,38},{40,46},{64,70},{72,78},{96,102},{104,110},{1... | collective-permute-start | bytes 196616 | tf_op jit(solution)/shard_map/ppermute | solution.py:337
  61.3 4.7 %collective-permute-start.19 = (bf16[32,1024]{1,0:T(8,128)(2,1)S(1)}, bf16[32,1024]{1,0:T(8,128)(2,1)S(1)}, u32[]{:S(2)}, u32[]{:S(2)}) collective-permute-start(bf16[32,1024]{1,0:T(8,128)(2,1)S(1)} %get-tuple-element.94), channel_id=1, source_target_pairs={{0,16},{8,24},{32,48},{40,56},{64,80},{72,88},{96,112},{104,120},{... | collective-permute-start | bytes 196616 | tf_op jit(solution)/shard_map/ppermute | solution.py:337
  61.3 5.0 %collective-permute-start.20 = (bf16[32,1024]{1,0:T(8,128)(2,1)S(1)}, bf16[32,1024]{1,0:T(8,128)(2,1)S(1)}, u32[]{:S(2)}, u32[]{:S(2)}) collective-permute-start(bf16[32,1024]{1,0:T(8,128)(2,1)S(1)} %get-tuple-element.95), channel_id=1, source_target_pairs={{0,1},{8,9},{32,33},{40,41},{64,65},{72,73},{96,97},{104,105},{128... | collective-permute-start | bytes 196616 | tf_op jit(solution)/shard_map/ppermute | solution.py:337
  66.3 12.3 %collective-permute-start.24 = (bf16[64,1024]{1,0:T(8,128)(2,1)S(1)}, bf16[64,1024]{1,0:T(8,128)(2,1)S(1)}, u32[]{:S(2)}, u32[]{:S(2)}) collective-permute-start(bf16[64,1024]{1,0:T(8,128)(2,1)S(1)} %get-tuple-element.103), channel_id=1, source_target_pairs={{0,1},{1,2},{2,3},{3,4},{4,5},{5,6},{6,7},{7,0},{8,9},{9,10},{10,1... | collective-permute-start | bytes 393224 | tf_op jit(solution)/shard_map/ppermute | solution.py:304
  68.1 10.5 %collective-permute-start.23 = (bf16[64,1024]{1,0:T(8,128)(2,1)S(1)}, bf16[64,1024]{1,0:T(8,128)(2,1)S(1)}, u32[]{:S(2)}, u32[]{:S(2)}) collective-permute-start(bf16[64,1024]{1,0:T(8,128)(2,1)S(1)} %get-tuple-element.102), channel_id=1, source_target_pairs={{0,8},{1,9},{2,10},{3,11},{4,12},{5,13},{6,14},{7,15},{8,16},{9,17... | collective-permute-start | bytes 393224 | tf_op jit(solution)/shard_map/ppermute | solution.py:304
  73.8 6.5 %collective-permute-start.22 = (bf16[64,1024]{1,0:T(8,128)(2,1)S(1)}, bf16[64,1024]{1,0:T(8,128)(2,1)S(1)}, u32[]{:S(2)}, u32[]{:S(2)}) collective-permute-start(bf16[64,1024]{1,0:T(8,128)(2,1)S(1)} %get-tuple-element.101), channel_id=1, source_target_pairs={{0,9},{1,10},{2,11},{3,12},{4,13},{5,14},{6,15},{7,8},{8,17},{9,18... | collective-permute-start | bytes 393224 | tf_op jit(solution)/shard_map/ppermute | solution.py:304
  74.7 13.5 %all-to-all-start = ((bf16[8,8,1024]{2,1,0:T(8,128)(2,1)}), bf16[8,8,1024]{2,1,0:T(8,128)(2,1)S(1)}, u32[]{:S(2)}, u32[]{:S(2)}) async-start(bf16[8,8,1024]{2,1,0:T(8,128)(2,1)} %pad_maximum_fusion.1), calls=%async_computation | async-start | bytes 262144 | tf_op jit(solution)/shard_map/all_to_all | solution.py:357
  (8 other events, 57.4 us)

commit v3 on v2

--- a/solution.py
+++ b/solution.py
@@ -30,10 +30,15 @@
 TN = ((0,), (0,))
 NT = ((1,), (1,))
 TT = ((0,), (1,))
+EARLY = 8
 
 
 def head_rows(h):
     return pl.ds(pl.multiple_of(h * DIM, DIM), DIM)
+
+
+def core_index():
+    return lax.rem(lax.axis_index("row"), 2)
 
 
 def last_window(rows, cols):
@@ -62,7 +67,7 @@
 
 
 def attention_kernel(
-    rows, cols, x0_ref, x1_ref, x2_ref, x3_ref, w_hbm_ref, scale_ref,
+    rows, cols, x0_ref, x1_ref, x2_ref, x3_ref, w_hbm_ref, scale_ref, after_ref,
     att_ref, probs_ref, query_ref, key_ref, value_ref, unit_scale_ref, window_ref,
     w_qkv_ref, sems,
 ):
@@ -142,37 +147,39 @@
     lax.fori_loop(0, HEADS, head, 0, unroll=8)
 
 
-def write_blocks(out_refs, col, term):
-    for n, out_ref in enumerate(out_refs):
-        out_ref[:, col : col + TOK] = term[n * 128 : n * 128 + 128].astype(BF)
-
-
-def proj_term_kernel(order_ref, att_ref, att2_ref, grad_mix_ref, grad_mix2_ref, *out_refs):
-    att = jnp.concatenate([att_ref[...], att2_ref[...]], axis=1)
-    grad_mix = jnp.concatenate([grad_mix_ref[...], grad_mix2_ref[...]], axis=0)
-    left = dot(order_ref[...], att).astype(BF)
-    for col in range(0, C, TOK):
-        write_blocks(out_refs, col, dot(left, grad_mix[:, col : col + TOK]))
-
-
-def value_term_kernel(order_ref, x_ref, x2_ref, grad_value_ref, grad_value2_ref, *out_refs):
-    x = jnp.concatenate([x_ref[...], x2_ref[...]], axis=0)
-    grad_value = jnp.concatenate([grad_value_ref[...], grad_value2_ref[...]], axis=1)
-    left = dot(order_ref[...], x, NT).astype(BF)
-    for col in range(0, C, TOK):
-        write_blocks(out_refs, col, dot(left, grad_value[col : col + TOK, :], NT))
-
-
-def sum_kernel(*refs):
-    ins, out_refs = refs[:8], refs[8:]
-    for group in range(2):
-        own, *others = ins[group * 4 : group * 4 + 4]
-        total = own[...].astype(F32)
-        for other in others:
-            total += other[...].astype(F32)
-        total = total.astype(BF)
-        for n in range(4):
-            out_refs[group * 4 + n][...] = total[n * 32 : n * 32 + 32]
+def term_kernel(
+    order_ref, att_ref, x_ref, grad_mix_ref, grad_value_ref,
+    att2_ref, x2_ref, grad_mix2_ref, grad_value2_ref, after_ref, *out_refs,
+):
+    def write(col, term):
+        for n, out_ref in enumerate(out_refs):
+            out_ref[:, col : col + TOK] = term[n * TOK : n * TOK + TOK].astype(BF)
+
+    @pl.when(core_index() == 0)
+    def _():
+        att = jnp.concatenate([att_ref[...], att2_ref[...]], axis=1)
+        grad_mix = jnp.concatenate([grad_mix_ref[...], grad_mix2_ref[...]], axis=0)
+        left = dot(order_ref[...], att).astype(BF)
+        for col in range(0, C, TOK):
+            write(col, dot(left, grad_mix[:, col : col + TOK]))
+
+    @pl.when(core_index() == 1)
+    def _():
+        x = jnp.concatenate([x_ref[...], x2_ref[...]], axis=0)
+        grad_value = jnp.concatenate([grad_value_ref[...], grad_value2_ref[...]], axis=1)
+        left = dot(order_ref[...], x, NT).astype(BF)
+        for col in range(0, C, TOK):
+            write(col, dot(left, grad_value[col : col + TOK, :], NT))
+
+
+def sum_kernel(own_ref, *refs):
+    total = own_ref[...].astype(F32)
+    for other in refs[:3]:
+        total += other[...].astype(F32)
+    total = total.astype(BF)
+    size = total.shape[0] // len(refs[3:])
+    for n, out_ref in enumerate(refs[3:]):
+        out_ref[...] = total[n * size : n * size + size]
 
 
 def score_kernel(
@@ -207,7 +214,7 @@
         return carry
 
     lax.fori_loop(0, count, scores, 0, unroll=8)
-    lax.fori_loop(0, count, units, 0, unroll=16)
+    lax.fori_loop(0, count, units, 0, unroll=8)
 
 
 def input_kernel(*refs):
@@ -246,7 +253,7 @@
     )
 
 
-def attention(quads, w_qkv, scale, rows, cols):
+def attention(quads, w_qkv, scale, rows, cols, after):
     flat = shape((C, TOK), F32)
     flat_bf = shape((C, TOK), BF)
     outs = (
@@ -256,26 +263,23 @@
     kernel = functools.partial(attention_kernel, rows, cols)
     scratch = [pltpu.VMEM((C, 3 * C), BF), pltpu.SemaphoreType.DMA((3,))]
     return call(
-        kernel, outs, [VM] * 4 + [pl.BlockSpec(memory_space=pltpu.HBM), SM], 14,
+        kernel, outs, [VM] * 4 + [pl.BlockSpec(memory_space=pltpu.HBM), SM, pl.BlockSpec(memory_space=pl.ANY)], 14,
         "attention_part", 24, scratch,
-    )(*quads, pltpu.with_memory_space_constraint(w_qkv, pltpu.HBM), scale)
+    )(*quads, pltpu.with_memory_space_constraint(w_qkv, pltpu.HBM), scale, after)
 
 
 def output_norm(att, quads, w_proj, gain):
     outs = (shape((TOK, C), BF), shape((C, TOK), BF))
-    return call(norm_kernel, outs, [VM] * 7, 2, "norm_part", 24)(att, *quads, w_proj, gain)
+    return call(norm_kernel, outs, [VM] * 7, 2, "norm_part", 16)(att, *quads, w_proj, gain)
 
 
 def value_grads(probs, grad_att):
-    return call(value_kernel, shape((C, TOK), BF), [VM] * 2, 2, "value_part", 24)(probs, grad_att)
-
-
-def proj_terms(*args):
-    return call(proj_term_kernel, (shape((128, C), BF),) * 4, [VM] * 5, 1.3, "proj_term", 24)(*args)
-
-
-def value_terms(*args):
-    return call(value_term_kernel, (shape((128, C), BF),) * 4, [VM] * 5, 1.3, "value_term", 24)(*args)
+    return call(value_kernel, shape((C, TOK), BF), [VM] * 2, 2, "value_part", 16)(probs, grad_att)
+
+
+def weight_terms(*args):
+    ins = [VM] * 9 + [pl.BlockSpec(memory_space=pl.ANY)]
+    return call(term_kernel, (shape((TOK, C), BF),) * 4, ins, 2.6, "weight_terms", 24)(*args)
 
 
 def score_grads(first, count, *args):
@@ -283,11 +287,12 @@
     scratch = [pltpu.VMEM((count, TOK, TOK), BF)]
     kernel = functools.partial(score_kernel, first, count)
     ins = [VM] * 6 + [SM, pl.BlockSpec(memory_space=pl.ANY)]
-    return call(kernel, outs, ins, 0.3, "score_part", 32, scratch)(*args)
-
-
-def block_sums(blocks):
-    return call(sum_kernel, (shape((32, C), BF),) * 8, [VM] * 8, 0.5, "block_sums", 24)(*blocks)
+    return call(kernel, outs, ins, 0.3, "score_part", 16, scratch)(*args)
+
+
+def block_sums(count, *blocks):
+    outs = (shape((64, C), BF),) * count
+    return call(sum_kernel, outs, [VM] * 4, 0.5, "block_sums", 16)(*blocks)
 
 
 def input_grad(parts, w_qkv):
@@ -329,27 +334,28 @@
     return lax.ppermute(array, BOTH, pairs)
 
 
-def moved(array, axis, by):
+def moved(array, stage, by):
     pairs = []
     for x, y, z, core in CHIPS:
-        to = ((x + by) % 4, y) if axis == "x" else (x, (y + by) % 4)
+        to = ((x + by) % 4, y) if core == stage else (x, (y + by) % 4)
         pairs.append((line(x, y, z, core), line(*to, z, core)))
     return lax.ppermute(array, BOTH, pairs)
 
 
-def gathered(blocks, axis):
-    far = moved(blocks[2], axis, 2)
-    return far, moved(blocks[1], axis, 1), moved(blocks[3], axis, -1)
-
-
-def row_order(axis):
-    place = jnp.arange(C // 2, dtype=jnp.int32)
-    a, b, z, row = place // 128, place // 32 % 4, place // 4 % 8, place % 4
+def gathered(blocks, stage):
+    far = moved(blocks[2], stage, 2)
+    return far, moved(blocks[1], stage, 1), moved(blocks[3], stage, -1)
+
+
+def row_order():
+    place = jnp.arange(C, dtype=jnp.int32)
+    a, b, z, far, row = place // 256, place // 64 % 4, place // 8 % 8, place // 4 % 2, place % 4
     r, c = lax.axis_index("row"), lax.axis_index("col")
-    dx, dy = (a, b) if axis == "x" else (b, a)
+    core = r % 2
+    dx, dy = jnp.where(core == 0, a, b), jnp.where(core == 0, b, a)
     x = (r // 2 % 2 * 2 + c % 2 + dx) % 4
     y = (c // 2 + dy) % 4
-    source = z * 128 + x // 2 * 64 + r % 2 * 32 + y * 8 + x % 2 * 4 + row
+    source = z * 128 + x // 2 * 64 + (core + far) % 2 * 32 + y * 8 + x % 2 * 4 + row
     return (source[:, None] == jnp.arange(C, dtype=jnp.int32)[None, :]).astype(BF)
 
 
@@ -372,35 +378,29 @@
     rows, cols = lax.axis_size("row"), lax.axis_size("col")
     x = window(tokens, rows, cols)
     g = window(grad_out, rows, cols)
+    order = row_order()
     att, probs, query, key, value, unit_scale, tokens_win = attention(
-        x, w_qkv, logit_scale, rows, cols
+        x, w_qkv, logit_scale, rows, cols, order
     )
     grad_mix, grad_att = output_norm(att, g, w_proj, norm_gain.reshape(1, C))
     grad_value = value_grads(probs, grad_att)
-    proj = proj_terms(row_order("x"), att, other_core(att), grad_mix, other_core(grad_mix))
-    val = value_terms(
-        row_order("y"), tokens_win, other_core(tokens_win), grad_value, other_core(grad_value)
-    )
-    proj_got, val_got = gathered(proj, "x"), gathered(val, "y")
+    mine = (att, tokens_win, grad_mix, grad_value)
     args = (probs, grad_att, query, key, value, unit_scale, logit_scale)
-    half = HEADS // 2
-    early = score_grads(0, half, *args, val[0])
-    late = score_grads(half, half, *args, proj_got[0])
+    early = score_grads(0, EARLY, *args, grad_value)
+    blocks = weight_terms(order, *mine, *[other_core(a) for a in mine], early[0])
+    others = gathered(blocks, 0)
+    late = score_grads(EARLY, HEADS - EARLY, *args, blocks[0])
     parts = [early[0], late[0], early[1], late[1], grad_value]
     grad_input = input_grad(parts, w_qkv)
-    grad_input, proj_got, val_got = lax.optimization_barrier((grad_input, proj_got, val_got))
-    blocks = block_sums((proj[0], *proj_got, val[0], *val_got))
-    proj, val = blocks[:4], blocks[4:]
-    proj_got, val_got = gathered(proj, "y"), gathered(val, "x")
-    proj, val, grad_input = lax.optimization_barrier(
-        ((proj[0], *proj_got), (val[0], *val_got), grad_input)
-    )
-    terms = jnp.concatenate(
-        [sum(a.astype(F32) for a in part).reshape(8, 4, C).astype(BF) for part in (proj, val)],
-        axis=1,
-    )
-    terms = z_sum(terms)
-    proj_part, value_part = terms[:4], terms[4:]
+    grad_input, others = lax.optimization_barrier((grad_input, others))
+    blocks = block_sums(4, blocks[0], *others)
+    others = gathered(blocks, 1)
+    terms, grad_input = lax.optimization_barrier(((blocks[0], *others), grad_input))
+    (terms,) = block_sums(1, *terms)
+    terms = z_sum(terms.reshape(8, 8, C))
+    kept, got = terms[:4], other_core(terms[4:])
+    first = lax.axis_index("row") % 2 == 0
+    proj_part, value_part = jnp.where(first, kept, got), jnp.where(first, got, kept)
     back = jnp.stack(
         [
             passed(grad_input[3], 1, 1, rows, cols),

time: 89.1 us -> 84.3 us (0.946)
  starting transfers between devices: 41.3 us -> 35.6 us
  waiting for transfers between devices: 16 us -> 17.6 us
  local copies, waits for them, and re-layouts: 3.89 us -> 2.37 us
  Pallas kernels: 24.3 us -> 25.2 us
    ppermute x12 -> x6, starting transfers between devices: 12.1 us -> 8.33 us  [moved(): return lax.ppermute(array, BOTH, pairs)]
    ppermute x9, waiting for transfers between devices: 1.74 us -> 4.87 us  [passed(): return lax.ppermute(array, ('row', 'col'), pairs)]
    all_to_all x1, waiting for transfers between devices: 5.81 us -> 3.44 us  [group_sum(): lax.all_to_all(blocks, BOTH, 0, 0, axis_index_groups=groups, tiled=True)]
    ppermute x9, starting transfers between devices: 22.9 us -> 20.8 us  [passed(): return lax.ppermute(array, ('row', 'col'), pairs)]
    ppermute x4 -> x5, waiting for transfers between devices: 0.01 us -> 1.35 us  [other_core(): return lax.ppermute(array, BOTH, pairs)]
    ppermute x4 -> x5, starting transfers between devices: 2.42 us -> 3.07 us  [other_core(): return lax.ppermute(array, BOTH, pairs)]
    ppermute x12 -> x6, waiting for transfers between devices: 8.44 us -> 7.95 us  [moved(): return lax.ppermute(array, BOTH, pairs)]
  transfers between devices with their start and end apart: 26 -> 21, of which waited for: 7 -> 8; matrix products, arithmetic and copies ran while one was open for 4% -> 3% of each run, Pallas kernels for 27% -> 23%
where the time goes in v3:
time: 84.3 us; the launch traced here: 83.8 us
  starting transfers between devices  35.6 us (42%)
  Pallas kernels  25.2 us (30%)
  waiting for transfers between devices  17.6 us (21%)
  local copies, waits for them, and re-layouts  2.37 us (3%)
  other arithmetic  2.19 us (3%)
  between operations  0.9 us (1%)
    ppermute x9, starting transfers between devices, passed(): return lax.ppermute(array, ('row', 'col'), pairs)  20.8 us
    pallas_call x1, Pallas kernels, attention(): call(kernel, outs, [VM] * 4 + [pl.BlockSpec(memory_space=pltpu.HBM), SM,...  9.7 us
    ppermute x6, starting transfers between devices, moved(): return lax.ppermute(array, BOTH, pairs)  8.33 us
    ppermute x6, waiting for transfers between devices, moved(): return lax.ppermute(array, BOTH, pairs)  7.95 us
    pallas_call x2, Pallas kernels, score_grads(): return call(kernel, outs, ins, 0.3, 'score_part', 16, scratch)(*args)  6.6 us
    ppermute x9, waiting for transfers between devices, passed(): return lax.ppermute(array, ('row', 'col'), pairs)  4.87 us
    all_to_all x1, waiting for transfers between devices, group_sum(): lax.all_to_all(blocks, BOTH, 0, 0, axis_index_groups=groups, tiled=True)  3.44 us
    all_to_all x1, starting transfers between devices, group_sum(): lax.all_to_all(blocks, BOTH, 0, 0, axis_index_groups=groups, tiled=True)  3.37 us
  transfers between devices with their start and end apart: 21, of which 8 were waited for; matrix products, arithmetic and copies ran while one was open for 3% of the time, Pallas kernels for 23%

profile of v3, /device:TPU:1, one launch (start us, length us, event | category | flops | bytes accessed | tf_op | source)
XLA Modules:
  0.0 83.8 jit_solution(13333569778966663091)
XLA Ops:
  0.6 1.1 %slice_bitcast_fusion.4 = (bf16[64,1024]{1,0:T(8,128)(2,1)S(1)}, bf16[64,1024]{1,0:T(8,128)(2,1)S(1)}, bf16[64,1024]{1,0:T(8,128)(2,1)S(1)}, bf16[64,1024]{1,0:T(8,128)(2,1)S(1)}) fusion(bf16[16,16,1024]{2,1,0:T(8,128)(2,1)} %param.6), kind=kLoop, calls=%fused_computation.10 | loop fusion | bytes 1048576 | tf_op jit(solution)/shard_map/reshape | solution.py:314
  1.8 5.1 %collective-permute-start.2 = (bf16[64,1024]{1,0:T(8,128)(2,1)S(1)}, bf16[64,1024]{1,0:T(8,128)(2,1)S(1)}, u32[]{:S(2)}, u32[]{:S(2)}) collective-permute-start(bf16[64,1024]{1,0:T(8,128)(2,1)S(1)} %get-tuple-element.87), channel_id=1, source_target_pairs={{0,255},{1,248},{2,249},{3,250},{4,251},{5,252},{6,253},{7,254},{8... | collective-permute-start | bytes 393224 | tf_op jit(solution)/shard_map/ppermute | solution.py:309
  7.2 6.4 %collective-permute-start.1 = (bf16[64,1024]{1,0:T(8,128)(2,1)S(1)}, bf16[64,1024]{1,0:T(8,128)(2,1)S(1)}, u32[]{:S(2)}, u32[]{:S(2)}) collective-permute-start(bf16[64,1024]{1,0:T(8,128)(2,1)S(1)} %get-tuple-element.90), channel_id=1, source_target_pairs={{0,248},{1,249},{2,250},{3,251},{4,252},{5,253},{6,254},{7,255},{8... | collective-permute-start | bytes 393224 | tf_op jit(solution)/shard_map/ppermute | solution.py:309
  14.7 2.5 %collective-permute-start.5 = (bf16[64,1024]{1,0:T(8,128)(2,1)S(1)}, bf16[64,1024]{1,0:T(8,128)(2,1)S(1)}, u32[]{:S(2)}, u32[]{:S(2)}) collective-permute-start(bf16[64,1024]{1,0:T(8,128)(2,1)S(1)} %get-tuple-element.83), channel_id=1, source_target_pairs={{0,255},{1,248},{2,249},{3,250},{4,251},{5,252},{6,253},{7,254},{8... | collective-permute-start | bytes 393224 | tf_op jit(solution)/shard_map/ppermute | solution.py:309
  17.2 1.2 %collective-permute-start.3 = (bf16[64,1024]{1,0:T(8,128)(2,1)S(1)}, bf16[64,1024]{1,0:T(8,128)(2,1)S(1)}, u32[]{:S(2)}, u32[]{:S(2)}) collective-permute-start(bf16[64,1024]{1,0:T(8,128)(2,1)S(1)} %get-tuple-element.84), channel_id=1, source_target_pairs={{0,7},{1,0},{2,1},{3,2},{4,3},{5,4},{6,5},{7,6},{8,15},{9,8},{10,9... | collective-permute-start | bytes 393224 | tf_op jit(solution)/shard_map/ppermute | solution.py:309
  18.9 9.7 %attention_part.1 = (bf16[1024,256]{1,0:T(8,128)(2,1)S(1)}, f32[32,256,256]{2,1,0:T(8,128)S(1)}, f32[1024,256]{1,0:T(8,128)S(1)}, f32[1024,256]{1,0:T(8,128)S(1)...) custom-call(bf16[64,1024]{1,0:T(8,128)(2,1)S(1)} %get-tuple-element.89.x0_ref, ...), custom_call_target="tpu_custom_call" | custom-call | flops 15399999488 | bytes 1048576 | tf_op jit(solution)/shard_map/attention_part/pallas_call | solution.py:265
  28.7 1.9 %norm_part.1 = (bf16[256,1024]{1,0:T(8,128)(2,1)S(1)}, bf16[1024,256]{1,0:T(8,128)(2,1)S(1)}) custom-call(bf16[1024,256]{1,0:T(8,128)(2,1)S(1)} %get-tuple-element.43.att_ref, bf16[64,1024]{1,0:T(8,128)(2,1)S(1)} %get-tuple-element.85.g0_ref, bf16[64,1024]{1,0:T(8,128)(2,1)S(1)} %collective-permute-done.3.g1_ref, ...), custom_call_target="tpu_custom_call" | custom-call | flops 2200000000 | bytes 1048576 | tf_op jit(solution)/shard_map/norm_part/pallas_call | solution.py:273
  30.6 1.7 %value_part.1.after_ref.grad_value_ref.refs_4_ = bf16[1024,256]{1,0:T(8,128)(2,1)S(1)} custom-call(f32[32,256,256]{2,1,0:T(8,128)S(1)} %get-tuple-element.46.probs_ref, bf16[1024,256]{1,0:T(8,128)(2,1)S(1)} %get-tuple-element.47.grad_att_ref), custom_call_target="tpu_custom_call" | custom-call | flops 2200000000 | bytes 1048576 | tf_op jit(solution)/shard_map/value_part/pallas_call | solution.py:277
  33.9 1.8 %score_part.2 = (bf16[256,256]{1,0:T(8,128)(2,1)S(1)}, bf16[256,256]{1,0:T(8,128)(2,1)S(1)}) custom-call(f32[32,256,256]{2,1,0:T(8,128)S(1)} %get-tuple-element.46.probs_ref, bf16[1024,256]{1,0:T(8,128)(2,1)S(1)} %get-tuple-element.47.grad_att_ref, f32[1024,256]{1,0:T(8,128)S(1)} %get-tuple-element.48.query_ref, f32[1024,256]{1,0:T(8,128)S(1)} %get-tuple-element.49.key_ref, ...), custom_call_target="tpu_custom_call" | custom-call | flops 330000000 | bytes 1048576 | tf_op jit(solution)/shard_map/score_part/pallas_call | solution.py:290
  37.1 2.4 %weight_terms.1 = (bf16[256,1024]{1,0:T(8,128)(2,1)S(1)}, bf16[256,1024]{1,0:T(8,128)(2,1)S(1)}, bf16[256,1024]{1,0:T(8,128)(2,1)S(1)}, bf16[256,1024]{1,0:T(8,128)(2,1)S(1)}) custom-call(bf16[1024,1024]{1,0:T(8,128)(2,1)S(1)} %fusion.after_ref.order_ref, bf16[1024,256]{1,0:T(8,128)(2,1)S(1)} %get-tuple-element.43.att_ref, ...), custom_call_target="tpu_custom_call" | custom-call | flops 2860000000 | bytes 1048576 | tf_op jit(solution)/shard_map/weight_terms/pallas_call | solution.py:282
  40.7 2.3 %collective-permute-start.12 = (bf16[256,1024]{1,0:T(8,128)(2,1)S(1)}, bf16[256,1024]{1,0:T(8,128)(2,1)S(1)}, u32[]{:S(2)}, u32[]{:S(2)}) collective-permute-start(bf16[256,1024]{1,0:T(8,128)(2,1)S(1)} %get-tuple-element.63), channel_id=1, source_target_pairs={{0,17},{8,14},{32,49},{40,46},{64,81},{72,78},{96,113},{104,110},{... | collective-permute-start | bytes 1572872 | tf_op jit(solution)/shard_map/ppermute | solution.py:342
  43.0 4.8 %score_part.3 = (bf16[768,256]{1,0:T(8,128)(2,1)S(1)}, bf16[768,256]{1,0:T(8,128)(2,1)S(1)}) custom-call(f32[32,256,256]{2,1,0:T(8,128)S(1)} %get-tuple-element.46.probs_ref, bf16[1024,256]{1,0:T(8,128)(2,1)S(1)} %get-tuple-element.47.grad_att_ref, f32[1024,256]{1,0:T(8,128)S(1)} %get-tuple-element.48.query_ref, f32[1024,256]{1,0:T(8,128)S(1)} %get-tuple-element.49.key_ref, ...), custom_call_target="tpu_custom_call" | custom-call | flops 330000000 | bytes 1048576 | tf_op jit(solution)/shard_map/score_part/pallas_call | solution.py:290
  47.8 1.9 %input_part.1 = (bf16[64,1024]{1,0:T(8,128)(2,1)S(1)}, bf16[64,1024]{1,0:T(8,128)(2,1)S(1)}, bf16[64,1024]{1,0:T(8,128)(2,1)S(1)}, bf16[64,1024]{1,0:T(8,128)(2,1)S(1)}) custom-call(bf16[256,256]{1,0:T(8,128)(2,1)S(1)} %get-tuple-element.52.after_ref.refs_0_, bf16[768,256]{1,0:T(8,128)(2,1)S(1)} %get-tuple-element.54.refs_1_, ...), custom_call_target="tpu_custom_call" | custom-call | flops 220000000 | bytes 1048576 | tf_op jit(solution)/shard_map/input_part/pallas_call | solution.py:300
  49.7 5.3 %collective-permute-done.11.refs_1_ = bf16[256,1024]{1,0:T(8,128)(2,1)S(1)} collective-permute-done((bf16[256,1024]{1,0:T(8,128)(2,1)S(1)}, bf16[256,1024]{1,0:T(8,128)(2,1)S(1)}, u32[]{:S(2)}, u32[]{:S(2)}) %collective-permute-start.11) | collective-permute-done | bytes 524320 | tf_op jit(solution)/shard_map/ppermute | solution.py:342
  55.3 2.2 %collective-permute-start.13 = (bf16[64,1024]{1,0:T(8,128)(2,1)S(1)}, bf16[64,1024]{1,0:T(8,128)(2,1)S(1)}, u32[]{:S(2)}, u32[]{:S(2)}) collective-permute-start(bf16[64,1024]{1,0:T(8,128)(2,1)S(1)} %get-tuple-element.68), channel_id=1, source_target_pairs={{0,4},{8,24},{32,36},{40,56},{64,68},{72,88},{96,100},{104,120},{1... | collective-permute-start | bytes 393224 | tf_op jit(solution)/shard_map/ppermute | solution.py:342
  58.1 2.1 %collective-permute-start.15 = (bf16[64,1024]{1,0:T(8,128)(2,1)S(1)}, bf16[64,1024]{1,0:T(8,128)(2,1)S(1)}, u32[]{:S(2)}, u32[]{:S(2)}) collective-permute-start(bf16[64,1024]{1,0:T(8,128)(2,1)S(1)} %get-tuple-element.70), channel_id=1, source_target_pairs={{0,6},{8,25},{32,38},{40,57},{64,70},{72,89},{96,102},{104,121},{1... | collective-permute-start | bytes 393224 | tf_op jit(solution)/shard_map/ppermute | solution.py:342
  60.7 2.1 %collective-permute-done.14.refs_1_ = bf16[64,1024]{1,0:T(8,128)(2,1)S(1)} collective-permute-done((bf16[64,1024]{1,0:T(8,128)(2,1)S(1)}, bf16[64,1024]{1,0:T(8,128)(2,1)S(1)}, u32[]{:S(2)}, u32[]{:S(2)}) %collective-permute-start.14) | collective-permute-done | bytes 131104 | tf_op jit(solution)/shard_map/ppermute | solution.py:342
  62.8 3.8 %collective-permute-start.16 = (bf16[64,1024]{1,0:T(8,128)(2,1)S(1)}, bf16[64,1024]{1,0:T(8,128)(2,1)S(1)}, u32[]{:S(2)}, u32[]{:S(2)}) collective-permute-start(bf16[64,1024]{1,0:T(8,128)(2,1)S(1)} %get-tuple-element.75), channel_id=1, source_target_pairs={{0,9},{1,10},{2,11},{3,12},{4,13},{5,14},{6,15},{7,8},{8,17},{9,18... | collective-permute-start | bytes 393224 | tf_op jit(solution)/shard_map/ppermute | solution.py:309
  66.6 1.5 %collective-permute-start.17 = (bf16[64,1024]{1,0:T(8,128)(2,1)S(1)}, bf16[64,1024]{1,0:T(8,128)(2,1)S(1)}, u32[]{:S(2)}, u32[]{:S(2)}) collective-permute-start(bf16[64,1024]{1,0:T(8,128)(2,1)S(1)} %get-tuple-element.76), channel_id=1, source_target_pairs={{0,8},{1,9},{2,10},{3,11},{4,12},{5,13},{6,14},{7,15},{8,16},{9,17... | collective-permute-start | bytes 393224 | tf_op jit(solution)/shard_map/ppermute | solution.py:309
  68.8 3.4 %all-to-all-start = ((bf16[8,8,1024]{2,1,0:T(8,128)(2,1)}), bf16[8,8,1024]{2,1,0:T(8,128)(2,1)S(1)}, u32[]{:S(2)}, u32[]{:S(2)}) async-start(bf16[8,8,1024]{2,1,0:T(8,128)(2,1)} %bitcast.16), calls=%async_computation | async-start | bytes 262144 | tf_op jit(solution)/shard_map/all_to_all | solution.py:363
  72.2 1.7 %collective-permute-done.16 = bf16[64,1024]{1,0:T(8,128)(2,1)S(1)} collective-permute-done((bf16[64,1024]{1,0:T(8,128)(2,1)S(1)}, bf16[64,1024]{1,0:T(8,128)(2,1)S(1)}, u32[]{:S(2)}, u32[]{:S(2)}) %collective-permute-start.16) | collective-permute-done | bytes 131104 | tf_op jit(solution)/shard_map/ppermute | solution.py:309
  74.0 3.1 %collective-permute-done.18 = bf16[64,1024]{1,0:T(8,128)(2,1)S(1)} collective-permute-done((bf16[64,1024]{1,0:T(8,128)(2,1)S(1)}, bf16[64,1024]{1,0:T(8,128)(2,1)S(1)}, u32[]{:S(2)}, u32[]{:S(2)}) %collective-permute-start.18) | collective-permute-done | bytes 131104 | tf_op jit(solution)/shard_map/ppermute | solution.py:309
  77.3 3.4 %all-to-all-done = bf16[8,8,1024]{2,1,0:T(8,128)(2,1)S(1)} async-done(((bf16[8,8,1024]{2,1,0:T(8,128)(2,1)}), bf16[8,8,1024]{2,1,0:T(8,128)(2,1)S(1)}, u32[]{:S(2)}, u32[]{:S(2)}) %all-to-all-start) | async-done | bytes 131104 | tf_op jit(solution)/shard_map/all_to_all | solution.py:363
  80.8 1.4 %collective-permute-start.19 = (f32[4,1024]{1,0:T(4,128)S(1)}, f32[4,1024]{1,0:T(4,128)S(1)}, u32[]{:S(2)}, u32[]{:S(2)}) collective-permute-start(f32[4,1024]{1,0:T(4,128)S(1)} %slice.40), channel_id=1, source_target_pairs={{0,8},{8,0},{32,40},{40,32},{64,72},{72,64},{96,104},{104,96},{128... | collective-permute-start | bytes 49160 | tf_op jit(solution)/shard_map/ppermute | solution.py:334
  (51 shorter events, 10.1 us)
Async XLA Ops:
  0.6 18.3 %copy-start = (f32[32]{0:T(128)S(1)}, f32[32]{0:T(128)}, u32[]{:S(2)}) copy-start(f32[32]{0:T(128)} %scale_ref.5) | copy-start | bytes 388
  1.8 17.0 %collective-permute-start.2 = (bf16[64,1024]{1,0:T(8,128)(2,1)S(1)}, bf16[64,1024]{1,0:T(8,128)(2,1)S(1)}, u32[]{:S(2)}, u32[]{:S(2)}) collective-permute-start(bf16[64,1024]{1,0:T(8,128)(2,1)S(1)} %get-tuple-element.87), channel_id=1, source_target_pairs={{0,255},{1,248},{2,249},{3,250},{4,251},{5,252},{6,253},{7,254},{8... | collective-permute-start | bytes 393224 | tf_op jit(solution)/shard_map/ppermute | solution.py:309
  6.9 12.0 %collective-permute-start = (bf16[64,1024]{1,0:T(8,128)(2,1)S(1)}, bf16[64,1024]{1,0:T(8,128)(2,1)S(1)}, u32[]{:S(2)}, u32[]{:S(2)}) collective-permute-start(bf16[64,1024]{1,0:T(8,128)(2,1)S(1)} %get-tuple-element.88), channel_id=1, source_target_pairs={{0,7},{1,0},{2,1},{3,2},{4,3},{5,4},{6,5},{7,6},{8,15},{9,8},{10,9... | collective-permute-start | bytes 393224 | tf_op jit(solution)/shard_map/ppermute | solution.py:309
  7.2 11.7 %collective-permute-start.1 = (bf16[64,1024]{1,0:T(8,128)(2,1)S(1)}, bf16[64,1024]{1,0:T(8,128)(2,1)S(1)}, u32[]{:S(2)}, u32[]{:S(2)}) collective-permute-start(bf16[64,1024]{1,0:T(8,128)(2,1)S(1)} %get-tuple-element.90), channel_id=1, source_target_pairs={{0,248},{1,249},{2,250},{3,251},{4,252},{5,253},{6,254},{7,255},{8... | collective-permute-start | bytes 393224 | tf_op jit(solution)/shard_map/ppermute | solution.py:309
  14.7 14.0 %collective-permute-start.5 = (bf16[64,1024]{1,0:T(8,128)(2,1)S(1)}, bf16[64,1024]{1,0:T(8,128)(2,1)S(1)}, u32[]{:S(2)}, u32[]{:S(2)}) collective-permute-start(bf16[64,1024]{1,0:T(8,128)(2,1)S(1)} %get-tuple-element.83), channel_id=1, source_target_pairs={{0,255},{1,248},{2,249},{3,250},{4,251},{5,252},{6,253},{7,254},{8... | collective-permute-start | bytes 393224 | tf_op jit(solution)/shard_map/ppermute | solution.py:309
  17.2 11.5 %collective-permute-start.3 = (bf16[64,1024]{1,0:T(8,128)(2,1)S(1)}, bf16[64,1024]{1,0:T(8,128)(2,1)S(1)}, u32[]{:S(2)}, u32[]{:S(2)}) collective-permute-start(bf16[64,1024]{1,0:T(8,128)(2,1)S(1)} %get-tuple-element.84), channel_id=1, source_target_pairs={{0,7},{1,0},{2,1},{3,2},{4,3},{5,4},{6,5},{7,6},{8,15},{9,8},{10,9... | collective-permute-start | bytes 393224 | tf_op jit(solution)/shard_map/ppermute | solution.py:309
  18.8 9.9 %collective-permute-start.4 = (bf16[64,1024]{1,0:T(8,128)(2,1)S(1)}, bf16[64,1024]{1,0:T(8,128)(2,1)S(1)}, u32[]{:S(2)}, u32[]{:S(2)}) collective-permute-start(bf16[64,1024]{1,0:T(8,128)(2,1)S(1)} %get-tuple-element.86), channel_id=1, source_target_pairs={{0,248},{1,249},{2,250},{3,251},{4,252},{5,253},{6,254},{7,255},{8... | collective-permute-start | bytes 393224 | tf_op jit(solution)/shard_map/ppermute | solution.py:309
  18.9 9.8 %copy-start.1 = (bf16[1024,1024]{1,0:T(8,128)(2,1)S(1)}, bf16[1024,1024]{1,0:T(8,128)(2,1)}, u32[]{:S(2)}) copy-start(bf16[1024,1024]{1,0:T(8,128)(2,1)} %w_proj_ref.1) | copy-start | bytes 6291460
  32.3 3.4 %collective-permute-start.9 = (bf16[1024,256]{1,0:T(8,128)(2,1)S(1)}, bf16[1024,256]{1,0:T(8,128)(2,1)S(1)}, u32[]{:S(2)}, u32[]{:S(2)}) collective-permute-start(bf16[1024,256]{1,0:T(8,128)(2,1)S(1)} %value_part.1.after_ref.grad_value_ref.refs_4_), channel_id=1, source_target_pairs={{0,8},{8,0},{32,40},{40,32},{64,72},{72,64},{96,104},{104,96},{128... | collective-permute-start | bytes 1572872 | tf_op jit(solution)/shard_map/ppermute | solution.py:334
  33.3 2.4 %collective-permute-start.8 = (bf16[256,1024]{1,0:T(8,128)(2,1)S(1)}, bf16[256,1024]{1,0:T(8,128)(2,1)S(1)}, u32[]{:S(2)}, u32[]{:S(2)}) collective-permute-start(bf16[256,1024]{1,0:T(8,128)(2,1)S(1)} %get-tuple-element.45.grad_mix_ref), channel_id=1, source_target_pairs={{0,8},{8,0},{32,40},{40,32},{64,72},{72,64},{96,104},{104,96},{128... | collective-permute-start | bytes 1572872 | tf_op jit(solution)/shard_map/ppermute | solution.py:334
  33.4 2.9 %collective-permute-start.7 = (bf16[256,1024]{1,0:T(8,128)(2,1)S(1)}, bf16[256,1024]{1,0:T(8,128)(2,1)S(1)}, u32[]{:S(2)}, u32[]{:S(2)}) collective-permute-start(bf16[256,1024]{1,0:T(8,128)(2,1)S(1)} %get-tuple-element.44.x_ref), channel_id=1, source_target_pairs={{0,8},{8,0},{32,40},{40,32},{64,72},{72,64},{96,104},{104,96},{128... | collective-permute-start | bytes 1572872 | tf_op jit(solution)/shard_map/ppermute | solution.py:334
  33.8 3.3 %collective-permute-start.6 = (bf16[1024,256]{1,0:T(8,128)(2,1)S(1)}, bf16[1024,256]{1,0:T(8,128)(2,1)S(1)}, u32[]{:S(2)}, u32[]{:S(2)}) collective-permute-start(bf16[1024,256]{1,0:T(8,128)(2,1)S(1)} %get-tuple-element.43.att_ref), channel_id=1, source_target_pairs={{0,8},{8,0},{32,40},{40,32},{64,72},{72,64},{96,104},{104,96},{128... | collective-permute-start | bytes 1572872 | tf_op jit(solution)/shard_map/ppermute | solution.py:334
  39.5 10.2 %collective-permute-start.10 = (bf16[256,1024]{1,0:T(8,128)(2,1)S(1)}, bf16[256,1024]{1,0:T(8,128)(2,1)S(1)}, u32[]{:S(2)}, u32[]{:S(2)}) collective-permute-start(bf16[256,1024]{1,0:T(8,128)(2,1)S(1)} %get-tuple-element.61), channel_id=1, source_target_pairs={{0,16},{8,12},{32,48},{40,44},{64,80},{72,76},{96,112},{104,108},{... | collective-permute-start | bytes 1572872 | tf_op jit(solution)/shard_map/ppermute | solution.py:342
  40.3 14.8 %collective-permute-start.11 = (bf16[256,1024]{1,0:T(8,128)(2,1)S(1)}, bf16[256,1024]{1,0:T(8,128)(2,1)S(1)}, u32[]{:S(2)}, u32[]{:S(2)}) collective-permute-start(bf16[256,1024]{1,0:T(8,128)(2,1)S(1)} %get-tuple-element.62), channel_id=1, source_target_pairs={{0,1},{8,10},{32,33},{40,42},{64,65},{72,74},{96,97},{104,106},{12... | collective-permute-start | bytes 1572872 | tf_op jit(solution)/shard_map/ppermute | solution.py:342
  40.7 14.4 %collective-permute-start.12 = (bf16[256,1024]{1,0:T(8,128)(2,1)S(1)}, bf16[256,1024]{1,0:T(8,128)(2,1)S(1)}, u32[]{:S(2)}, u32[]{:S(2)}) collective-permute-start(bf16[256,1024]{1,0:T(8,128)(2,1)S(1)} %get-tuple-element.63), channel_id=1, source_target_pairs={{0,17},{8,14},{32,49},{40,46},{64,81},{72,78},{96,113},{104,110},{... | collective-permute-start | bytes 1572872 | tf_op jit(solution)/shard_map/ppermute | solution.py:342
  55.0 27.2 %copy-start.3 = (bf16[16,16,1024]{2,1,0:T(8,128)(2,1)S(1)}, bf16[16,16,1024]{2,1,0:T(8,128)(2,1)}, u32[]{:S(2)}) copy-start(bf16[16,16,1024]{2,1,0:T(8,128)(2,1)} %param.7) | copy-start | bytes 1572868
  55.3 5.4 %collective-permute-start.13 = (bf16[64,1024]{1,0:T(8,128)(2,1)S(1)}, bf16[64,1024]{1,0:T(8,128)(2,1)S(1)}, u32[]{:S(2)}, u32[]{:S(2)}) collective-permute-start(bf16[64,1024]{1,0:T(8,128)(2,1)S(1)} %get-tuple-element.68), channel_id=1, source_target_pairs={{0,4},{8,24},{32,36},{40,56},{64,68},{72,88},{96,100},{104,120},{1... | collective-permute-start | bytes 393224 | tf_op jit(solution)/shard_map/ppermute | solution.py:342
  57.5 5.3 %collective-permute-start.14 = (bf16[64,1024]{1,0:T(8,128)(2,1)S(1)}, bf16[64,1024]{1,0:T(8,128)(2,1)S(1)}, u32[]{:S(2)}, u32[]{:S(2)}) collective-permute-start(bf16[64,1024]{1,0:T(8,128)(2,1)S(1)} %get-tuple-element.69), channel_id=1, source_target_pairs={{0,2},{8,9},{32,34},{40,41},{64,66},{72,73},{96,98},{104,105},{128... | collective-permute-start | bytes 393224 | tf_op jit(solution)/shard_map/ppermute | solution.py:342
  58.1 4.7 %collective-permute-start.15 = (bf16[64,1024]{1,0:T(8,128)(2,1)S(1)}, bf16[64,1024]{1,0:T(8,128)(2,1)S(1)}, u32[]{:S(2)}, u32[]{:S(2)}) collective-permute-start(bf16[64,1024]{1,0:T(8,128)(2,1)S(1)} %get-tuple-element.70), channel_id=1, source_target_pairs={{0,6},{8,25},{32,38},{40,57},{64,70},{72,89},{96,102},{104,121},{1... | collective-permute-start | bytes 393224 | tf_op jit(solution)/shard_map/ppermute | solution.py:342
  62.8 11.2 %collective-permute-start.16 = (bf16[64,1024]{1,0:T(8,128)(2,1)S(1)}, bf16[64,1024]{1,0:T(8,128)(2,1)S(1)}, u32[]{:S(2)}, u32[]{:S(2)}) collective-permute-start(bf16[64,1024]{1,0:T(8,128)(2,1)S(1)} %get-tuple-element.75), channel_id=1, source_target_pairs={{0,9},{1,10},{2,11},{3,12},{4,13},{5,14},{6,15},{7,8},{8,17},{9,18... | collective-permute-start | bytes 393224 | tf_op jit(solution)/shard_map/ppermute | solution.py:309
  66.6 7.3 %collective-permute-start.17 = (bf16[64,1024]{1,0:T(8,128)(2,1)S(1)}, bf16[64,1024]{1,0:T(8,128)(2,1)S(1)}, u32[]{:S(2)}, u32[]{:S(2)}) collective-permute-start(bf16[64,1024]{1,0:T(8,128)(2,1)S(1)} %get-tuple-element.76), channel_id=1, source_target_pairs={{0,8},{1,9},{2,10},{3,11},{4,12},{5,13},{6,14},{7,15},{8,16},{9,17... | collective-permute-start | bytes 393224 | tf_op jit(solution)/shard_map/ppermute | solution.py:309
  68.1 9.0 %collective-permute-start.18 = (bf16[64,1024]{1,0:T(8,128)(2,1)S(1)}, bf16[64,1024]{1,0:T(8,128)(2,1)S(1)}, u32[]{:S(2)}, u32[]{:S(2)}) collective-permute-start(bf16[64,1024]{1,0:T(8,128)(2,1)S(1)} %get-tuple-element.77), channel_id=1, source_target_pairs={{0,1},{1,2},{2,3},{3,4},{4,5},{5,6},{6,7},{7,0},{8,9},{9,10},{10,1... | collective-permute-start | bytes 393224 | tf_op jit(solution)/shard_map/ppermute | solution.py:309
  68.8 11.9 %all-to-all-start = ((bf16[8,8,1024]{2,1,0:T(8,128)(2,1)}), bf16[8,8,1024]{2,1,0:T(8,128)(2,1)S(1)}, u32[]{:S(2)}, u32[]{:S(2)}) async-start(bf16[8,8,1024]{2,1,0:T(8,128)(2,1)} %bitcast.16), calls=%async_computation | async-start | bytes 262144 | tf_op jit(solution)/shard_map/all_to_all | solution.py:363
  80.8 2.4 %collective-permute-start.19 = (f32[4,1024]{1,0:T(4,128)S(1)}, f32[4,1024]{1,0:T(4,128)S(1)}, u32[]{:S(2)}, u32[]{:S(2)}) collective-permute-start(f32[4,1024]{1,0:T(4,128)S(1)} %slice.40), channel_id=1, source_target_pairs={{0,8},{8,0},{32,40},{40,32},{64,72},{72,64},{96,104},{104,96},{128... | collective-permute-start | bytes 49160 | tf_op jit(solution)/shard_map/ppermute | solution.py:334
  (3 other events, 19.4 us)

commit v4 on v3

--- a/solution.py
+++ b/solution.py
@@ -30,7 +30,6 @@
 TN = ((0,), (0,))
 NT = ((1,), (1,))
 TT = ((0,), (1,))
-EARLY = 8
 
 
 def head_rows(h):
@@ -66,10 +65,9 @@
     return key.astype(BF), query.astype(BF)
 
 
-def attention_kernel(
-    rows, cols, x0_ref, x1_ref, x2_ref, x3_ref, w_hbm_ref, scale_ref, after_ref,
-    att_ref, probs_ref, query_ref, key_ref, value_ref, unit_scale_ref, window_ref,
-    w_qkv_ref, sems,
+def project_kernel(
+    x0_ref, x1_ref, x2_ref, x3_ref, w_hbm_ref, after_ref,
+    query_ref, key_ref, value_ref, unit_scale_ref, window_ref, w_qkv_ref, sems,
 ):
     copies = []
     for n in range(3):
@@ -78,7 +76,6 @@
             pltpu.make_async_copy(w_hbm_ref.at[:, span], w_qkv_ref.at[:, span], sems.at[n])
         )
         copies[-1].start()
-    key_mask, query_mask = mask_features(*last_window(rows, cols))
     x = jnp.concatenate([x0_ref[...], x1_ref[...], x2_ref[...], x3_ref[...]], axis=0)
     window_ref[...] = x
     for col in range(0, 3 * C, TOK):
@@ -97,6 +94,13 @@
         else:
             value_ref[col - 2 * C : col - 2 * C + TOK, :] = raw.astype(BF)
 
+
+def attention_kernel(
+    rows, cols, query_ref, key_ref, value_ref, scale_ref, after_ref, after2_ref, after3_ref,
+    att_ref, probs_ref,
+):
+    key_mask, query_mask = mask_features(*last_window(rows, cols))
+
     def head(h, carry):
         rows = head_rows(h)
         raw = dot(
@@ -115,7 +119,8 @@
 
 
 def norm_kernel(
-    att_ref, g0_ref, g1_ref, g2_ref, g3_ref, w_proj_ref, gain_ref, grad_mix_ref, grad_att_ref
+    att_ref, g0_ref, g1_ref, g2_ref, g3_ref, w_proj_ref, gain_ref, after_ref,
+    grad_mix_ref, grad_att_ref,
 ):
     g = jnp.concatenate([g0_ref[...], g1_ref[...], g2_ref[...], g3_ref[...]], axis=0)
     mixed = dot(att_ref[...], w_proj_ref[...], TN)
@@ -136,7 +141,7 @@
         ).astype(BF)
 
 
-def value_kernel(probs_ref, grad_att_ref, grad_value_ref):
+def value_kernel(probs_ref, grad_att_ref, after_ref, grad_value_ref):
     def head(h, carry):
         rows = head_rows(h)
         grad_value_ref[rows, :] = dot(
@@ -147,27 +152,36 @@
     lax.fori_loop(0, HEADS, head, 0, unroll=8)
 
 
+def left_kernel(order_ref, att_ref, att2_ref, x_ref, x2_ref, after_ref, left_ref):
+    @pl.when(core_index() == 0)
+    def _():
+        att = jnp.concatenate([att_ref[...], att2_ref[...]], axis=1)
+        left_ref[...] = dot(order_ref[...], att).astype(BF)
+
+    @pl.when(core_index() == 1)
+    def _():
+        x = jnp.concatenate([x_ref[...], x2_ref[...]], axis=0)
+        left_ref[...] = dot(order_ref[...], x, NT).astype(BF)
+
+
 def term_kernel(
-    order_ref, att_ref, x_ref, grad_mix_ref, grad_value_ref,
-    att2_ref, x2_ref, grad_mix2_ref, grad_value2_ref, after_ref, *out_refs,
+    left_ref, grad_mix_ref, grad_mix2_ref, grad_value_ref, grad_value2_ref, *out_refs
 ):
     def write(col, term):
         for n, out_ref in enumerate(out_refs):
             out_ref[:, col : col + TOK] = term[n * TOK : n * TOK + TOK].astype(BF)
 
+    left = left_ref[...]
+
     @pl.when(core_index() == 0)
     def _():
-        att = jnp.concatenate([att_ref[...], att2_ref[...]], axis=1)
         grad_mix = jnp.concatenate([grad_mix_ref[...], grad_mix2_ref[...]], axis=0)
-        left = dot(order_ref[...], att).astype(BF)
         for col in range(0, C, TOK):
             write(col, dot(left, grad_mix[:, col : col + TOK]))
 
     @pl.when(core_index() == 1)
     def _():
-        x = jnp.concatenate([x_ref[...], x2_ref[...]], axis=0)
         grad_value = jnp.concatenate([grad_value_ref[...], grad_value2_ref[...]], axis=1)
-        left = dot(order_ref[...], x, NT).astype(BF)
         for col in range(0, C, TOK):
             write(col, dot(left, grad_value[col : col + TOK, :], NT))
 
@@ -214,7 +228,7 @@
         return carry
 
     lax.fori_loop(0, count, scores, 0, unroll=8)
-    lax.fori_loop(0, count, units, 0, unroll=8)
+    lax.fori_loop(0, count, units, 0, unroll=16)
 
 
 def input_kernel(*refs):
@@ -231,6 +245,7 @@
 
 
 VM = pl.BlockSpec(memory_space=pltpu.VMEM)
+ANY = pl.BlockSpec(memory_space=pl.ANY)
 SM = pl.BlockSpec(memory_space=pltpu.SMEM)
 
 
@@ -253,40 +268,51 @@
     )
 
 
-def attention(quads, w_qkv, scale, rows, cols, after):
+def project(quads, w_qkv, after):
     flat = shape((C, TOK), F32)
-    flat_bf = shape((C, TOK), BF)
     outs = (
-        flat_bf, shape((HEADS, TOK, TOK), F32), flat, flat, flat_bf, shape((2 * HEADS, TOK), F32),
-        shape((TOK, C), BF),
-    )
+        flat, flat, shape((C, TOK), BF), shape((2 * HEADS, TOK), F32), shape((TOK, C), BF),
+    )
+    scratch = [pltpu.VMEM((C, 3 * C), BF), pltpu.SemaphoreType.DMA((3,))]
+    ins = [VM] * 4 + [pl.BlockSpec(memory_space=pltpu.HBM), ANY]
+    return call(project_kernel, outs, ins, 4, "project_part", 24, scratch)(
+        *quads, pltpu.with_memory_space_constraint(w_qkv, pltpu.HBM), after
+    )
+
+
+def attention(rows, cols, *args):
+    outs = (shape((C, TOK), BF), shape((HEADS, TOK, TOK), F32))
     kernel = functools.partial(attention_kernel, rows, cols)
-    scratch = [pltpu.VMEM((C, 3 * C), BF), pltpu.SemaphoreType.DMA((3,))]
-    return call(
-        kernel, outs, [VM] * 4 + [pl.BlockSpec(memory_space=pltpu.HBM), SM, pl.BlockSpec(memory_space=pl.ANY)], 14,
-        "attention_part", 24, scratch,
-    )(*quads, pltpu.with_memory_space_constraint(w_qkv, pltpu.HBM), scale, after)
-
-
-def output_norm(att, quads, w_proj, gain):
+    return call(kernel, outs, [VM] * 3 + [SM] + [ANY] * 3, 6, "attention_part", 16)(*args)
+
+
+def output_norm(att, quads, w_proj, gain, after):
     outs = (shape((TOK, C), BF), shape((C, TOK), BF))
-    return call(norm_kernel, outs, [VM] * 7, 2, "norm_part", 16)(att, *quads, w_proj, gain)
-
-
-def value_grads(probs, grad_att):
-    return call(value_kernel, shape((C, TOK), BF), [VM] * 2, 2, "value_part", 16)(probs, grad_att)
+    return call(norm_kernel, outs, [VM] * 7 + [ANY], 2, "norm_part", 16)(
+        att, *quads, w_proj, gain, after
+    )
+
+
+def value_grads(*args):
+    ins = [VM] * 2 + [ANY]
+    return call(value_kernel, shape((C, TOK), BF), ins, 2, "value_part", 16)(*args)
+
+
+def left_rows(*args):
+    ins = [VM] * 5 + [ANY]
+    return call(left_kernel, shape((C, 2 * TOK), BF), ins, 1.2, "left_rows", 24)(*args)
 
 
 def weight_terms(*args):
-    ins = [VM] * 9 + [pl.BlockSpec(memory_space=pl.ANY)]
-    return call(term_kernel, (shape((TOK, C), BF),) * 4, ins, 2.6, "weight_terms", 24)(*args)
+    outs = (shape((TOK, C), BF),) * 4
+    return call(term_kernel, outs, [VM] * 5, 1.3, "weight_terms", 24)(*args)
 
 
 def score_grads(first, count, *args):
     outs = (shape((count * DIM, TOK), BF),) * 2
     scratch = [pltpu.VMEM((count, TOK, TOK), BF)]
     kernel = functools.partial(score_kernel, first, count)
-    ins = [VM] * 6 + [SM, pl.BlockSpec(memory_space=pl.ANY)]
+    ins = [VM] * 6 + [SM, ANY]
     return call(kernel, outs, ins, 0.3, "score_part", 16, scratch)(*args)
 
 
@@ -379,18 +405,19 @@
     x = window(tokens, rows, cols)
     g = window(grad_out, rows, cols)
     order = row_order()
-    att, probs, query, key, value, unit_scale, tokens_win = attention(
-        x, w_qkv, logit_scale, rows, cols, order
-    )
-    grad_mix, grad_att = output_norm(att, g, w_proj, norm_gain.reshape(1, C))
-    grad_value = value_grads(probs, grad_att)
-    mine = (att, tokens_win, grad_mix, grad_value)
-    args = (probs, grad_att, query, key, value, unit_scale, logit_scale)
-    early = score_grads(0, EARLY, *args, grad_value)
-    blocks = weight_terms(order, *mine, *[other_core(a) for a in mine], early[0])
+    query, key, value, unit_scale, tokens_win = project(x, w_qkv, order)
+    att, probs = attention(rows, cols, query, key, value, logit_scale, *g[1:])
+    tokens_win2, att2 = other_core(tokens_win), other_core(att)
+    grad_mix, grad_att = output_norm(att, g, w_proj, norm_gain.reshape(1, C), tokens_win2)
+    grad_value = value_grads(probs, grad_att, att2)
+    grad_mix2, grad_value2 = other_core(grad_mix), other_core(grad_value)
+    left = left_rows(order, att, att2, tokens_win, tokens_win2, grad_value)
+    blocks = weight_terms(left, grad_mix, grad_mix2, grad_value, grad_value2)
     others = gathered(blocks, 0)
-    late = score_grads(EARLY, HEADS - EARLY, *args, blocks[0])
-    parts = [early[0], late[0], early[1], late[1], grad_value]
+    grads = score_grads(
+        0, HEADS, probs, grad_att, query, key, value, unit_scale, logit_scale, blocks[0]
+    )
+    parts = [*grads, grad_value]
     grad_input = input_grad(parts, w_qkv)
     grad_input, others = lax.optimization_barrier((grad_input, others))
     blocks = block_sums(4, blocks[0], *others)

time: 84.3 us -> 82.6 us (0.980)
  waiting for transfers between devices: 17.6 us -> 16.2 us
  starting transfers between devices: 35.6 us -> 36.7 us
  Pallas kernels: 25.2 us -> 24.1 us
    ppermute x9, waiting for transfers between devices: 4.87 us -> 3.07 us  [passed(): return lax.ppermute(array, ('row', 'col'), pairs)]
    all_to_all x1, waiting for transfers between devices: 3.44 us -> 4.9 us  [group_sum(): lax.all_to_all(blocks, BOTH, 0, 0, axis_index_groups=groups, tiled=True)]
    ppermute x5, starting transfers between devices: 3.07 us -> 4.33 us  [other_core(): return lax.ppermute(array, BOTH, pairs)]
    pallas_call x2 -> x1, Pallas kernels: 6.6 us -> 5.37 us  [score_grads(): return call(kernel, outs, ins, 0.3, 'score_part', 16, scratch)(*args)]
    all_to_all x1, starting transfers between devices: 3.37 us -> 4.22 us  [group_sum(): lax.all_to_all(blocks, BOTH, 0, 0, axis_index_groups=groups, tiled=True)]
    pallas_call x4 -> x6, Pallas kernels: 15.7 us -> 15.9 us  [the longest x1 5.43 us: attention(): call(kernel, outs, [VM] * 3 + [SM] + [ANY] * 3, 6, 'attention_part', 16)]
  transfers between devices with their start and end apart: 21 -> 21, of which waited for: 8 -> 8; matrix products, arithmetic and copies ran while one was open for 3% -> 3% of each run, Pallas kernels for 23% -> 25%
where the time goes in v4:
time: 82.6 us; the launch traced here: 82.4 us
  starting transfers between devices  36.7 us (44%)
  Pallas kernels  24.1 us (29%)
  waiting for transfers between devices  16.2 us (20%)
  local copies, waits for them, and re-layouts  2.36 us (3%)
  other arithmetic  2.2 us (3%)
  between operations  0.84 us (1%)
    ppermute x9, starting transfers between devices, passed(): return lax.ppermute(array, ('row', 'col'), pairs)  20.3 us
    ppermute x6, starting transfers between devices, moved(): return lax.ppermute(array, BOTH, pairs)  7.83 us
    ppermute x6, waiting for transfers between devices, moved(): return lax.ppermute(array, BOTH, pairs)  7.51 us
    pallas_call x1, Pallas kernels, attention(): call(kernel, outs, [VM] * 3 + [SM] + [ANY] * 3, 6, 'attention_part', 16)  5.43 us
    pallas_call x1, Pallas kernels, score_grads(): return call(kernel, outs, ins, 0.3, 'score_part', 16, scratch)(*args)  5.37 us
    all_to_all x1, waiting for transfers between devices, group_sum(): lax.all_to_all(blocks, BOTH, 0, 0, axis_index_groups=groups, tiled=True)  4.9 us
    ppermute x5, starting transfers between devices, other_core(): return lax.ppermute(array, BOTH, pairs)  4.33 us
    all_to_all x1, starting transfers between devices, group_sum(): lax.all_to_all(blocks, BOTH, 0, 0, axis_index_groups=groups, tiled=True)  4.22 us
  transfers between devices with their start and end apart: 21, of which 8 were waited for; matrix products, arithmetic and copies ran while one was open for 3% of the time, Pallas kernels for 25%

profile of v4, /device:TPU:1, one launch (start us, length us, event | category | flops | bytes accessed | tf_op | source)
XLA Modules:
  0.0 82.4 jit_solution(7842833264054347062)
XLA Ops:
  0.6 1.1 %slice_bitcast_fusion.4 = (bf16[64,1024]{1,0:T(8,128)(2,1)S(1)}, bf16[64,1024]{1,0:T(8,128)(2,1)S(1)}, bf16[64,1024]{1,0:T(8,128)(2,1)S(1)}, bf16[64,1024]{1,0:T(8,128)(2,1)S(1)}) fusion(bf16[16,16,1024]{2,1,0:T(8,128)(2,1)} %param.6), kind=kLoop, calls=%fused_computation.10 | loop fusion | bytes 1048576 | tf_op jit(solution)/shard_map/reshape | solution.py:340
  1.8 4.6 %collective-permute-start = (bf16[64,1024]{1,0:T(8,128)(2,1)S(1)}, bf16[64,1024]{1,0:T(8,128)(2,1)S(1)}, u32[]{:S(2)}, u32[]{:S(2)}) collective-permute-start(bf16[64,1024]{1,0:T(8,128)(2,1)S(1)} %get-tuple-element.84), channel_id=1, source_target_pairs={{0,7},{1,0},{2,1},{3,2},{4,3},{5,4},{6,5},{7,6},{8,15},{9,8},{10,9... | collective-permute-start | bytes 393224 | tf_op jit(solution)/shard_map/ppermute | solution.py:335
  7.3 7.0 %collective-permute-start.2 = (bf16[64,1024]{1,0:T(8,128)(2,1)S(1)}, bf16[64,1024]{1,0:T(8,128)(2,1)S(1)}, u32[]{:S(2)}, u32[]{:S(2)}) collective-permute-start(bf16[64,1024]{1,0:T(8,128)(2,1)S(1)} %get-tuple-element.83), channel_id=1, source_target_pairs={{0,255},{1,248},{2,249},{3,250},{4,251},{5,252},{6,253},{7,254},{8... | collective-permute-start | bytes 393224 | tf_op jit(solution)/shard_map/ppermute | solution.py:335
  14.3 1.1 %slice_bitcast_fusion = (bf16[64,1024]{1,0:T(8,128)(2,1)S(1)}, bf16[64,1024]{1,0:T(8,128)(2,1)S(1)}, bf16[64,1024]{1,0:T(8,128)(2,1)S(1)}, bf16[64,1024]{1,0:T(8,128)(2,1)S(1)}) fusion(bf16[16,16,1024]{2,1,0:T(8,128)(2,1)} %param.7), kind=kLoop, calls=%fused_computation.6 | loop fusion | bytes 1048576 | tf_op jit(solution)/shard_map/reshape | solution.py:340
  15.4 1.8 %collective-permute-start.3 = (bf16[64,1024]{1,0:T(8,128)(2,1)S(1)}, bf16[64,1024]{1,0:T(8,128)(2,1)S(1)}, u32[]{:S(2)}, u32[]{:S(2)}) collective-permute-start(bf16[64,1024]{1,0:T(8,128)(2,1)S(1)} %get-tuple-element.81), channel_id=1, source_target_pairs={{0,7},{1,0},{2,1},{3,2},{4,3},{5,4},{6,5},{7,6},{8,15},{9,8},{10,9... | collective-permute-start | bytes 393224 | tf_op jit(solution)/shard_map/ppermute | solution.py:335
  17.7 1.1 %collective-permute-start.5 = (bf16[64,1024]{1,0:T(8,128)(2,1)S(1)}, bf16[64,1024]{1,0:T(8,128)(2,1)S(1)}, u32[]{:S(2)}, u32[]{:S(2)}) collective-permute-start(bf16[64,1024]{1,0:T(8,128)(2,1)S(1)} %get-tuple-element.82), channel_id=1, source_target_pairs={{0,255},{1,248},{2,249},{3,250},{4,251},{5,252},{6,253},{7,254},{8... | collective-permute-start | bytes 393224 | tf_op jit(solution)/shard_map/ppermute | solution.py:335
  18.8 4.2 %project_part.1 = (f32[1024,256]{1,0:T(8,128)S(1)}, f32[1024,256]{1,0:T(8,128)S(1)}, bf16[1024,256]{1,0:T(8,128)(2,1)S(1)}, f32[64,256]{1,0:T(8,128)S(1)}, bf16[256,1024]{1,0:T(8,128)(2,1)S(1)}) custom-call(bf16[64,1024]{1,0:T(8,128)(2,1)S(1)} %get-tuple-element.85.x0_ref, bf16[64,1024]{1,0:T(8,128)(2,1)S(1)} %collective-permute-done.x1_ref, ...), custom_call_target="tpu_custom_call" | custom-call | flops 4400000000 | bytes 1048576 | tf_op jit(solution)/shard_map/project_part/pallas_call | solution.py:278
  24.5 5.4 %attention_part.1 = (bf16[1024,256]{1,0:T(8,128)(2,1)S(1)}, f32[32,256,256]{2,1,0:T(8,128)S(1)}) custom-call(f32[1024,256]{1,0:T(8,128)S(1)} %get-tuple-element.41.query_ref, f32[1024,256]{1,0:T(8,128)S(1)} %get-tuple-element.42.key_ref, bf16[1024,256]{1,0:T(8,128)(2,1)S(1)} %get-tuple-element.43.value_ref, f32[32]{0:T(128)S(1)} %copy-done, ...), custom_call_target="tpu_custom_call" | custom-call | flops 6600000000 | bytes 1048576 | tf_op jit(solution)/shard_map/attention_part/pallas_call | solution.py:286
  30.1 1.9 %norm_part.1 = (bf16[256,1024]{1,0:T(8,128)(2,1)S(1)}, bf16[1024,256]{1,0:T(8,128)(2,1)S(1)}) custom-call(bf16[1024,256]{1,0:T(8,128)(2,1)S(1)} %get-tuple-element.44.att_ref, bf16[64,1024]{1,0:T(8,128)(2,1)S(1)} %get-tuple-element.79.g0_ref, bf16[64,1024]{1,0:T(8,128)(2,1)S(1)} %collective-permute-done.3.after_ref.g1_ref, ...), custom_call_target="tpu_custom_call" | custom-call | flops 2200000000 | bytes 1048576 | tf_op jit(solution)/shard_map/norm_part/pallas_call | solution.py:291
  32.0 1.7 %value_part.1.after_ref.grad_value_ref.refs_2_ = bf16[1024,256]{1,0:T(8,128)(2,1)S(1)} custom-call(f32[32,256,256]{2,1,0:T(8,128)S(1)} %get-tuple-element.46.probs_ref, bf16[1024,256]{1,0:T(8,128)(2,1)S(1)} %get-tuple-element.47.grad_att_ref, bf16[1024,256]{1,0:T(8,128)(2,1)S(1)} %collective-permute-done.6.after_ref.att2_ref), custom_call_target="tpu_custom_call" | custom-call | flops 2200000000 | bytes 1048576 | tf_op jit(solution)/shard_map/value_part/pallas_call | solution.py:298
  34.5 1.3 %left_rows.1.left_ref = bf16[1024,512]{1,0:T(8,128)(2,1)S(1)} custom-call(bf16[1024,1024]{1,0:T(8,128)(2,1)S(1)} %fusion.after_ref.order_ref, bf16[1024,256]{1,0:T(8,128)(2,1)S(1)} %get-tuple-element.44.att_ref, bf16[1024,256]{1,0:T(8,128)(2,1)S(1)} %collective-permute-done.6.after_ref.att2_ref, bf16[256,1024]{1,0:T(8,128)(2,1)S(1)} %get-tuple-element.45.x_ref, ...), custom_call_target="tpu_custom_call" | custom-call | flops 1320000000 | bytes 1048576 | tf_op jit(solution)/shard_map/left_rows/pallas_call | solution.py:303
  36.5 1.4 %weight_terms.1 = (bf16[256,1024]{1,0:T(8,128)(2,1)S(1)}, bf16[256,1024]{1,0:T(8,128)(2,1)S(1)}, bf16[256,1024]{1,0:T(8,128)(2,1)S(1)}, bf16[256,1024]{1,0:T(8,128)(2,1)S(1)}) custom-call(bf16[1024,512]{1,0:T(8,128)(2,1)S(1)} %left_rows.1.left_ref, bf16[256,1024]{1,0:T(8,128)(2,1)S(1)} %get-tuple-element.48.grad_mix_ref, ...), custom_call_target="tpu_custom_call" | custom-call | flops 1430000000 | bytes 1048576 | tf_op jit(solution)/shard_map/weight_terms/pallas_call | solution.py:308
  39.1 2.3 %collective-permute-start.12 = (bf16[256,1024]{1,0:T(8,128)(2,1)S(1)}, bf16[256,1024]{1,0:T(8,128)(2,1)S(1)}, u32[]{:S(2)}, u32[]{:S(2)}) collective-permute-start(bf16[256,1024]{1,0:T(8,128)(2,1)S(1)} %get-tuple-element.59), channel_id=1, source_target_pairs={{0,17},{8,14},{32,49},{40,46},{64,81},{72,78},{96,113},{104,110},{... | collective-permute-start | bytes 1572872 | tf_op jit(solution)/shard_map/ppermute | solution.py:368
  41.4 5.4 %score_part.1 = (bf16[1024,256]{1,0:T(8,128)(2,1)S(1)}, bf16[1024,256]{1,0:T(8,128)(2,1)S(1)}) custom-call(f32[32,256,256]{2,1,0:T(8,128)S(1)} %get-tuple-element.46.probs_ref, bf16[1024,256]{1,0:T(8,128)(2,1)S(1)} %get-tuple-element.47.grad_att_ref, f32[1024,256]{1,0:T(8,128)S(1)} %get-tuple-element.41.query_ref, ...), custom_call_target="tpu_custom_call" | custom-call | flops 330000000 | bytes 1048576 | tf_op jit(solution)/shard_map/score_part/pallas_call | solution.py:316
  46.8 1.9 %input_part.1 = (bf16[64,1024]{1,0:T(8,128)(2,1)S(1)}, bf16[64,1024]{1,0:T(8,128)(2,1)S(1)}, bf16[64,1024]{1,0:T(8,128)(2,1)S(1)}, bf16[64,1024]{1,0:T(8,128)(2,1)S(1)}) custom-call(bf16[1024,256]{1,0:T(8,128)(2,1)S(1)} %get-tuple-element.51.refs_0_, bf16[1024,256]{1,0:T(8,128)(2,1)S(1)} %get-tuple-element.52.refs_1_, ...), custom_call_target="tpu_custom_call" | custom-call | flops 220000000 | bytes 1048576 | tf_op jit(solution)/shard_map/input_part/pallas_call | solution.py:326
  48.7 4.7 %collective-permute-done.11.refs_1_ = bf16[256,1024]{1,0:T(8,128)(2,1)S(1)} collective-permute-done((bf16[256,1024]{1,0:T(8,128)(2,1)S(1)}, bf16[256,1024]{1,0:T(8,128)(2,1)S(1)}, u32[]{:S(2)}, u32[]{:S(2)}) %collective-permute-start.11) | collective-permute-done | bytes 524320 | tf_op jit(solution)/shard_map/ppermute | solution.py:368
  53.7 1.7 %collective-permute-start.13 = (bf16[64,1024]{1,0:T(8,128)(2,1)S(1)}, bf16[64,1024]{1,0:T(8,128)(2,1)S(1)}, u32[]{:S(2)}, u32[]{:S(2)}) collective-permute-start(bf16[64,1024]{1,0:T(8,128)(2,1)S(1)} %get-tuple-element.64), channel_id=1, source_target_pairs={{0,4},{8,24},{32,36},{40,56},{64,68},{72,88},{96,100},{104,120},{1... | collective-permute-start | bytes 393224 | tf_op jit(solution)/shard_map/ppermute | solution.py:368
  55.9 2.1 %collective-permute-start.15 = (bf16[64,1024]{1,0:T(8,128)(2,1)S(1)}, bf16[64,1024]{1,0:T(8,128)(2,1)S(1)}, u32[]{:S(2)}, u32[]{:S(2)}) collective-permute-start(bf16[64,1024]{1,0:T(8,128)(2,1)S(1)} %get-tuple-element.66), channel_id=1, source_target_pairs={{0,6},{8,25},{32,38},{40,57},{64,70},{72,89},{96,102},{104,121},{1... | collective-permute-start | bytes 393224 | tf_op jit(solution)/shard_map/ppermute | solution.py:368
  59.1 1.7 %collective-permute-done.14.refs_1_ = bf16[64,1024]{1,0:T(8,128)(2,1)S(1)} collective-permute-done((bf16[64,1024]{1,0:T(8,128)(2,1)S(1)}, bf16[64,1024]{1,0:T(8,128)(2,1)S(1)}, u32[]{:S(2)}, u32[]{:S(2)}) %collective-permute-start.14) | collective-permute-done | bytes 131104 | tf_op jit(solution)/shard_map/ppermute | solution.py:368
  60.8 4.1 %collective-permute-start.17 = (bf16[64,1024]{1,0:T(8,128)(2,1)S(1)}, bf16[64,1024]{1,0:T(8,128)(2,1)S(1)}, u32[]{:S(2)}, u32[]{:S(2)}) collective-permute-start(bf16[64,1024]{1,0:T(8,128)(2,1)S(1)} %get-tuple-element.72), channel_id=1, source_target_pairs={{0,8},{1,9},{2,10},{3,11},{4,12},{5,13},{6,14},{7,15},{8,16},{9,17... | collective-permute-start | bytes 393224 | tf_op jit(solution)/shard_map/ppermute | solution.py:335
  66.4 4.2 %all-to-all-start = ((bf16[8,8,1024]{2,1,0:T(8,128)(2,1)}), bf16[8,8,1024]{2,1,0:T(8,128)(2,1)S(1)}, u32[]{:S(2)}, u32[]{:S(2)}) async-start(bf16[8,8,1024]{2,1,0:T(8,128)(2,1)} %bitcast.16), calls=%async_computation | async-start | bytes 262144 | tf_op jit(solution)/shard_map/all_to_all | solution.py:389
  70.6 2.0 %collective-permute-done.18 = bf16[64,1024]{1,0:T(8,128)(2,1)S(1)} collective-permute-done((bf16[64,1024]{1,0:T(8,128)(2,1)S(1)}, bf16[64,1024]{1,0:T(8,128)(2,1)S(1)}, u32[]{:S(2)}, u32[]{:S(2)}) %collective-permute-start.18) | collective-permute-done | bytes 131104 | tf_op jit(solution)/shard_map/ppermute | solution.py:335
  73.5 4.9 %all-to-all-done = bf16[8,8,1024]{2,1,0:T(8,128)(2,1)S(1)} async-done(((bf16[8,8,1024]{2,1,0:T(8,128)(2,1)}), bf16[8,8,1024]{2,1,0:T(8,128)(2,1)S(1)}, u32[]{:S(2)}, u32[]{:S(2)}) %all-to-all-start) | async-done | bytes 131104 | tf_op jit(solution)/shard_map/all_to_all | solution.py:389
  78.4 2.4 %collective-permute-start.19 = (f32[4,1024]{1,0:T(4,128)S(1)}, f32[4,1024]{1,0:T(4,128)S(1)}, u32[]{:S(2)}, u32[]{:S(2)}) collective-permute-start(f32[4,1024]{1,0:T(4,128)S(1)} %slice.40), channel_id=1, source_target_pairs={{0,8},{8,0},{32,40},{40,32},{64,72},{72,64},{96,104},{104,96},{128... | collective-permute-start | bytes 49160 | tf_op jit(solution)/shard_map/ppermute | solution.py:360
  (52 shorter events, 11.6 us)
Async XLA Ops:
  1.8 15.9 %collective-permute-start = (bf16[64,1024]{1,0:T(8,128)(2,1)S(1)}, bf16[64,1024]{1,0:T(8,128)(2,1)S(1)}, u32[]{:S(2)}, u32[]{:S(2)}) collective-permute-start(bf16[64,1024]{1,0:T(8,128)(2,1)S(1)} %get-tuple-element.84), channel_id=1, source_target_pairs={{0,7},{1,0},{2,1},{3,2},{4,3},{5,4},{6,5},{7,6},{8,15},{9,8},{10,9... | collective-permute-start | bytes 393224 | tf_op jit(solution)/shard_map/ppermute | solution.py:335
  6.3 12.5 %collective-permute-start.1 = (bf16[64,1024]{1,0:T(8,128)(2,1)S(1)}, bf16[64,1024]{1,0:T(8,128)(2,1)S(1)}, u32[]{:S(2)}, u32[]{:S(2)}) collective-permute-start(bf16[64,1024]{1,0:T(8,128)(2,1)S(1)} %get-tuple-element.86), channel_id=1, source_target_pairs={{0,248},{1,249},{2,250},{3,251},{4,252},{5,253},{6,254},{7,255},{8... | collective-permute-start | bytes 393224 | tf_op jit(solution)/shard_map/ppermute | solution.py:335
  7.3 11.5 %collective-permute-start.2 = (bf16[64,1024]{1,0:T(8,128)(2,1)S(1)}, bf16[64,1024]{1,0:T(8,128)(2,1)S(1)}, u32[]{:S(2)}, u32[]{:S(2)}) collective-permute-start(bf16[64,1024]{1,0:T(8,128)(2,1)S(1)} %get-tuple-element.83), channel_id=1, source_target_pairs={{0,255},{1,248},{2,249},{3,250},{4,251},{5,252},{6,253},{7,254},{8... | collective-permute-start | bytes 393224 | tf_op jit(solution)/shard_map/ppermute | solution.py:335
  15.4 8.6 %collective-permute-start.3 = (bf16[64,1024]{1,0:T(8,128)(2,1)S(1)}, bf16[64,1024]{1,0:T(8,128)(2,1)S(1)}, u32[]{:S(2)}, u32[]{:S(2)}) collective-permute-start(bf16[64,1024]{1,0:T(8,128)(2,1)S(1)} %get-tuple-element.81), channel_id=1, source_target_pairs={{0,7},{1,0},{2,1},{3,2},{4,3},{5,4},{6,5},{7,6},{8,15},{9,8},{10,9... | collective-permute-start | bytes 393224 | tf_op jit(solution)/shard_map/ppermute | solution.py:335
  17.2 6.8 %collective-permute-start.4 = (bf16[64,1024]{1,0:T(8,128)(2,1)S(1)}, bf16[64,1024]{1,0:T(8,128)(2,1)S(1)}, u32[]{:S(2)}, u32[]{:S(2)}) collective-permute-start(bf16[64,1024]{1,0:T(8,128)(2,1)S(1)} %get-tuple-element.80), channel_id=1, source_target_pairs={{0,248},{1,249},{2,250},{3,251},{4,252},{5,253},{6,254},{7,255},{8... | collective-permute-start | bytes 393224 | tf_op jit(solution)/shard_map/ppermute | solution.py:335
  17.7 6.8 %collective-permute-start.5 = (bf16[64,1024]{1,0:T(8,128)(2,1)S(1)}, bf16[64,1024]{1,0:T(8,128)(2,1)S(1)}, u32[]{:S(2)}, u32[]{:S(2)}) collective-permute-start(bf16[64,1024]{1,0:T(8,128)(2,1)S(1)} %get-tuple-element.82), channel_id=1, source_target_pairs={{0,255},{1,248},{2,249},{3,250},{4,251},{5,252},{6,253},{7,254},{8... | collective-permute-start | bytes 393224 | tf_op jit(solution)/shard_map/ppermute | solution.py:335
  18.8 5.7 %copy-start = (f32[32]{0:T(128)S(1)}, f32[32]{0:T(128)}, u32[]{:S(2)}) copy-start(f32[32]{0:T(128)} %scale_ref.3) | copy-start | bytes 388
  23.0 7.0 %collective-permute-start.7 = (bf16[256,1024]{1,0:T(8,128)(2,1)S(1)}, bf16[256,1024]{1,0:T(8,128)(2,1)S(1)}, u32[]{:S(2)}, u32[]{:S(2)}) collective-permute-start(bf16[256,1024]{1,0:T(8,128)(2,1)S(1)} %get-tuple-element.45.x_ref), channel_id=1, source_target_pairs={{0,8},{8,0},{32,40},{40,32},{64,72},{72,64},{96,104},{104,96},{128... | collective-permute-start | bytes 1572872 | tf_op jit(solution)/shard_map/ppermute | solution.py:360
  24.5 5.5 %copy-start.2 = (f32[1024]{0:T(1024)S(1)}, f32[1024]{0:T(1024)}, u32[]{:S(2)}) copy-start(f32[1024]{0:T(1024)} %param.10) | copy-start | bytes 12292
  30.0 2.1 %collective-permute-start.6 = (bf16[1024,256]{1,0:T(8,128)(2,1)S(1)}, bf16[1024,256]{1,0:T(8,128)(2,1)S(1)}, u32[]{:S(2)}, u32[]{:S(2)}) collective-permute-start(bf16[1024,256]{1,0:T(8,128)(2,1)S(1)} %get-tuple-element.44.att_ref), channel_id=1, source_target_pairs={{0,8},{8,0},{32,40},{40,32},{64,72},{72,64},{96,104},{104,96},{128... | collective-permute-start | bytes 1572872 | tf_op jit(solution)/shard_map/ppermute | solution.py:360
  33.7 2.1 %collective-permute-start.9 = (bf16[1024,256]{1,0:T(8,128)(2,1)S(1)}, bf16[1024,256]{1,0:T(8,128)(2,1)S(1)}, u32[]{:S(2)}, u32[]{:S(2)}) collective-permute-start(bf16[1024,256]{1,0:T(8,128)(2,1)S(1)} %value_part.1.after_ref.grad_value_ref.refs_2_), channel_id=1, source_target_pairs={{0,8},{8,0},{32,40},{40,32},{64,72},{72,64},{96,104},{104,96},{128... | collective-permute-start | bytes 1572872 | tf_op jit(solution)/shard_map/ppermute | solution.py:360
  34.2 2.3 %collective-permute-start.8 = (bf16[256,1024]{1,0:T(8,128)(2,1)S(1)}, bf16[256,1024]{1,0:T(8,128)(2,1)S(1)}, u32[]{:S(2)}, u32[]{:S(2)}) collective-permute-start(bf16[256,1024]{1,0:T(8,128)(2,1)S(1)} %get-tuple-element.48.grad_mix_ref), channel_id=1, source_target_pairs={{0,8},{8,0},{32,40},{40,32},{64,72},{72,64},{96,104},{104,96},{128... | collective-permute-start | bytes 1572872 | tf_op jit(solution)/shard_map/ppermute | solution.py:360
  37.9 10.8 %collective-permute-start.10 = (bf16[256,1024]{1,0:T(8,128)(2,1)S(1)}, bf16[256,1024]{1,0:T(8,128)(2,1)S(1)}, u32[]{:S(2)}, u32[]{:S(2)}) collective-permute-start(bf16[256,1024]{1,0:T(8,128)(2,1)S(1)} %get-tuple-element.57), channel_id=1, source_target_pairs={{0,16},{8,12},{32,48},{40,44},{64,80},{72,76},{96,112},{104,108},{... | collective-permute-start | bytes 1572872 | tf_op jit(solution)/shard_map/ppermute | solution.py:368
  38.0 15.4 %collective-permute-start.11 = (bf16[256,1024]{1,0:T(8,128)(2,1)S(1)}, bf16[256,1024]{1,0:T(8,128)(2,1)S(1)}, u32[]{:S(2)}, u32[]{:S(2)}) collective-permute-start(bf16[256,1024]{1,0:T(8,128)(2,1)S(1)} %get-tuple-element.58), channel_id=1, source_target_pairs={{0,1},{8,10},{32,33},{40,42},{64,65},{72,74},{96,97},{104,106},{12... | collective-permute-start | bytes 1572872 | tf_op jit(solution)/shard_map/ppermute | solution.py:368
  39.1 14.4 %collective-permute-start.12 = (bf16[256,1024]{1,0:T(8,128)(2,1)S(1)}, bf16[256,1024]{1,0:T(8,128)(2,1)S(1)}, u32[]{:S(2)}, u32[]{:S(2)}) collective-permute-start(bf16[256,1024]{1,0:T(8,128)(2,1)S(1)} %get-tuple-element.59), channel_id=1, source_target_pairs={{0,17},{8,14},{32,49},{40,46},{64,81},{72,78},{96,113},{104,110},{... | collective-permute-start | bytes 1572872 | tf_op jit(solution)/shard_map/ppermute | solution.py:368
  53.4 27.4 %copy-start.3 = (bf16[16,16,1024]{2,1,0:T(8,128)(2,1)S(1)}, bf16[16,16,1024]{2,1,0:T(8,128)(2,1)}, u32[]{:S(2)}) copy-start(bf16[16,16,1024]{2,1,0:T(8,128)(2,1)} %param.7) | copy-start | bytes 1572868
  53.7 5.4 %collective-permute-start.13 = (bf16[64,1024]{1,0:T(8,128)(2,1)S(1)}, bf16[64,1024]{1,0:T(8,128)(2,1)S(1)}, u32[]{:S(2)}, u32[]{:S(2)}) collective-permute-start(bf16[64,1024]{1,0:T(8,128)(2,1)S(1)} %get-tuple-element.64), channel_id=1, source_target_pairs={{0,4},{8,24},{32,36},{40,56},{64,68},{72,88},{96,100},{104,120},{1... | collective-permute-start | bytes 393224 | tf_op jit(solution)/shard_map/ppermute | solution.py:368
  55.4 5.4 %collective-permute-start.14 = (bf16[64,1024]{1,0:T(8,128)(2,1)S(1)}, bf16[64,1024]{1,0:T(8,128)(2,1)S(1)}, u32[]{:S(2)}, u32[]{:S(2)}) collective-permute-start(bf16[64,1024]{1,0:T(8,128)(2,1)S(1)} %get-tuple-element.65), channel_id=1, source_target_pairs={{0,2},{8,9},{32,34},{40,41},{64,66},{72,73},{96,98},{104,105},{128... | collective-permute-start | bytes 393224 | tf_op jit(solution)/shard_map/ppermute | solution.py:368
  55.9 4.9 %collective-permute-start.15 = (bf16[64,1024]{1,0:T(8,128)(2,1)S(1)}, bf16[64,1024]{1,0:T(8,128)(2,1)S(1)}, u32[]{:S(2)}, u32[]{:S(2)}) collective-permute-start(bf16[64,1024]{1,0:T(8,128)(2,1)S(1)} %get-tuple-element.66), channel_id=1, source_target_pairs={{0,6},{8,25},{32,38},{40,57},{64,70},{72,89},{96,102},{104,121},{1... | collective-permute-start | bytes 393224 | tf_op jit(solution)/shard_map/ppermute | solution.py:368
  60.8 9.8 %collective-permute-start.17 = (bf16[64,1024]{1,0:T(8,128)(2,1)S(1)}, bf16[64,1024]{1,0:T(8,128)(2,1)S(1)}, u32[]{:S(2)}, u32[]{:S(2)}) collective-permute-start(bf16[64,1024]{1,0:T(8,128)(2,1)S(1)} %get-tuple-element.72), channel_id=1, source_target_pairs={{0,8},{1,9},{2,10},{3,11},{4,12},{5,13},{6,14},{7,15},{8,16},{9,17... | collective-permute-start | bytes 393224 | tf_op jit(solution)/shard_map/ppermute | solution.py:335
  64.9 7.7 %collective-permute-start.18 = (bf16[64,1024]{1,0:T(8,128)(2,1)S(1)}, bf16[64,1024]{1,0:T(8,128)(2,1)S(1)}, u32[]{:S(2)}, u32[]{:S(2)}) collective-permute-start(bf16[64,1024]{1,0:T(8,128)(2,1)S(1)} %get-tuple-element.73), channel_id=1, source_target_pairs={{0,1},{1,2},{2,3},{3,4},{4,5},{5,6},{6,7},{7,0},{8,9},{9,10},{10,1... | collective-permute-start | bytes 393224 | tf_op jit(solution)/shard_map/ppermute | solution.py:335
  64.9 8.3 %collective-permute-start.16 = (bf16[64,1024]{1,0:T(8,128)(2,1)S(1)}, bf16[64,1024]{1,0:T(8,128)(2,1)S(1)}, u32[]{:S(2)}, u32[]{:S(2)}) collective-permute-start(bf16[64,1024]{1,0:T(8,128)(2,1)S(1)} %get-tuple-element.71), channel_id=1, source_target_pairs={{0,9},{1,10},{2,11},{3,12},{4,13},{5,14},{6,15},{7,8},{8,17},{9,18... | collective-permute-start | bytes 393224 | tf_op jit(solution)/shard_map/ppermute | solution.py:335
  66.4 12.0 %all-to-all-start = ((bf16[8,8,1024]{2,1,0:T(8,128)(2,1)}), bf16[8,8,1024]{2,1,0:T(8,128)(2,1)S(1)}, u32[]{:S(2)}, u32[]{:S(2)}) async-start(bf16[8,8,1024]{2,1,0:T(8,128)(2,1)} %bitcast.16), calls=%async_computation | async-start | bytes 262144 | tf_op jit(solution)/shard_map/all_to_all | solution.py:389
  78.4 3.3 %collective-permute-start.19 = (f32[4,1024]{1,0:T(4,128)S(1)}, f32[4,1024]{1,0:T(4,128)S(1)}, u32[]{:S(2)}, u32[]{:S(2)}) collective-permute-start(f32[4,1024]{1,0:T(4,128)S(1)} %slice.40), channel_id=1, source_target_pairs={{0,8},{8,0},{32,40},{40,32},{64,72},{72,64},{96,104},{104,96},{128... | collective-permute-start | bytes 49160 | tf_op jit(solution)/shard_map/ppermute | solution.py:360
  (3 other events, 16.3 us)

commit v5 on v4

--- a/solution.py
+++ b/solution.py
@@ -115,7 +115,7 @@
         att_ref[rows, :] = dot(probs.astype(BF), value_ref[rows, :], TT).T.astype(BF)
         return carry
 
-    lax.fori_loop(0, HEADS, head, 0, unroll=8)
+    lax.fori_loop(0, HEADS, head, 0, unroll=HEADS)
 
 
 def norm_kernel(
@@ -149,7 +149,7 @@
         ).astype(BF)
         return carry
 
-    lax.fori_loop(0, HEADS, head, 0, unroll=8)
+    lax.fori_loop(0, HEADS, head, 0, unroll=HEADS)
 
 
 def left_kernel(order_ref, att_ref, att2_ref, x_ref, x2_ref, after_ref, left_ref):
@@ -165,13 +165,13 @@
 
 
 def term_kernel(
-    left_ref, grad_mix_ref, grad_mix2_ref, grad_value_ref, grad_value2_ref, *out_refs
+    spans, left_ref, grad_mix_ref, grad_mix2_ref, grad_value_ref, grad_value2_ref, *out_refs
 ):
     def write(col, term):
         for n, out_ref in enumerate(out_refs):
             out_ref[:, col : col + TOK] = term[n * TOK : n * TOK + TOK].astype(BF)
 
-    left = left_ref[...]
+    left = jnp.concatenate([left_ref[a:b, :] for a, b in spans], axis=0)
 
     @pl.when(core_index() == 0)
     def _():
@@ -304,8 +304,14 @@
 
 
 def weight_terms(*args):
-    outs = (shape((TOK, C), BF),) * 4
-    return call(term_kernel, outs, [VM] * 5, 1.3, "weight_terms", 24)(*args)
+    def part(*spans):
+        outs = (shape((TOK, C), BF),) * (sum(b - a for a, b in spans) // TOK)
+        kernel = functools.partial(term_kernel, spans)
+        return call(kernel, outs, [VM] * 5, 0.6, "weight_terms", 24)(*args)
+
+    (far,) = part((2 * TOK, 3 * TOK))
+    own, one, three = part((0, 2 * TOK), (3 * TOK, 4 * TOK))
+    return own, one, far, three
 
 
 def score_grads(first, count, *args):
@@ -421,9 +427,9 @@
     grad_input = input_grad(parts, w_qkv)
     grad_input, others = lax.optimization_barrier((grad_input, others))
     blocks = block_sums(4, blocks[0], *others)
+    blocks, grad_input = lax.optimization_barrier((blocks, grad_input))
     others = gathered(blocks, 1)
-    terms, grad_input = lax.optimization_barrier(((blocks[0], *others), grad_input))
-    (terms,) = block_sums(1, *terms)
+    (terms,) = block_sums(1, blocks[0], *others)
     terms = z_sum(terms.reshape(8, 8, C))
     kept, got = terms[:4], other_core(terms[4:])
     first = lax.axis_index("row") % 2 == 0

time: 82.6 us -> 77.9 us (0.943)
  waiting for transfers between devices: 16.2 us -> 12.4 us
  Pallas kernels: 24.1 us -> 22.8 us
    ppermute x6, waiting for transfers between devices: 7.51 us -> 3.27 us  [moved(): return lax.ppermute(array, BOTH, pairs)]
    all_to_all x1, waiting for transfers between devices: 4.9 us -> 6.72 us  [group_sum(): lax.all_to_all(blocks, BOTH, 0, 0, axis_index_groups=groups, tiled=True)]
    ppermute x9, waiting for transfers between devices: 3.07 us -> 1.51 us  [passed(): return lax.ppermute(array, ('row', 'col'), pairs)]
    pallas_call x1, Pallas kernels: 5.43 us -> 4.29 us  [attention(): call(kernel, outs, [VM] * 3 + [SM] + [ANY] * 3, 6, 'attention_part', 16)]
  transfers between devices with their start and end apart: 21 -> 21, of which waited for: 8 -> 7; matrix products, arithmetic and copies ran while one was open for 3% -> 4% of each run, Pallas kernels for 25% -> 27%
where the time goes in v5:
time: 77.9 us; the launch traced here: 77.7 us
  starting transfers between devices  37 us (47%)
  Pallas kernels  22.8 us (29%)
  waiting for transfers between devices  12.4 us (16%)
  local copies, waits for them, and re-layouts  2.36 us (3%)
  other arithmetic  2.2 us (3%)
  between operations  0.84 us (1%)
    ppermute x9, starting transfers between devices, passed(): return lax.ppermute(array, ('row', 'col'), pairs)  20.2 us
    ppermute x6, starting transfers between devices, moved(): return lax.ppermute(array, BOTH, pairs)  8.21 us
    all_to_all x1, waiting for transfers between devices, group_sum(): lax.all_to_all(blocks, BOTH, 0, 0, axis_index_groups=groups, tiled=True)  6.72 us
    pallas_call x1, Pallas kernels, score_grads(): return call(kernel, outs, ins, 0.3, 'score_part', 16, scratch)(*args)  5.39 us
    ppermute x5, starting transfers between devices, other_core(): return lax.ppermute(array, BOTH, pairs)  4.55 us
    pallas_call x1, Pallas kernels, attention(): call(kernel, outs, [VM] * 3 + [SM] + [ANY] * 3, 6, 'attention_part', 16)  4.29 us
    pallas_call x1, Pallas kernels, project(): call(project_kernel, outs, ins, 4, 'project_part', 24, scratch)  4.18 us
    all_to_all x1, starting transfers between devices, group_sum(): lax.all_to_all(blocks, BOTH, 0, 0, axis_index_groups=groups, tiled=True)  4.12 us
  transfers between devices with their start and end apart: 21, of which 7 were waited for; matrix products, arithmetic and copies ran while one was open for 4% of the time, Pallas kernels for 27%

profile of v5, /device:TPU:1, one launch (start us, length us, event | category | flops | bytes accessed | tf_op | source)
XLA Modules:
  0.0 77.7 jit_solution(728813203506843683)
XLA Ops:
  0.6 1.1 %slice_bitcast_fusion.4 = (bf16[64,1024]{1,0:T(8,128)(2,1)S(1)}, bf16[64,1024]{1,0:T(8,128)(2,1)S(1)}, bf16[64,1024]{1,0:T(8,128)(2,1)S(1)}, bf16[64,1024]{1,0:T(8,128)(2,1)S(1)}) fusion(bf16[16,16,1024]{2,1,0:T(8,128)(2,1)} %param.6), kind=kLoop, calls=%fused_computation.10 | loop fusion | bytes 1048576 | tf_op jit(solution)/shard_map/reshape | solution.py:346
  1.8 4.6 %collective-permute-start = (bf16[64,1024]{1,0:T(8,128)(2,1)S(1)}, bf16[64,1024]{1,0:T(8,128)(2,1)S(1)}, u32[]{:S(2)}, u32[]{:S(2)}) collective-permute-start(bf16[64,1024]{1,0:T(8,128)(2,1)S(1)} %get-tuple-element.82), channel_id=1, source_target_pairs={{0,7},{1,0},{2,1},{3,2},{4,3},{5,4},{6,5},{7,6},{8,15},{9,8},{10,9... | collective-permute-start | bytes 393224 | tf_op jit(solution)/shard_map/ppermute | solution.py:341
  7.3 7.0 %collective-permute-start.2 = (bf16[64,1024]{1,0:T(8,128)(2,1)S(1)}, bf16[64,1024]{1,0:T(8,128)(2,1)S(1)}, u32[]{:S(2)}, u32[]{:S(2)}) collective-permute-start(bf16[64,1024]{1,0:T(8,128)(2,1)S(1)} %get-tuple-element.81), channel_id=1, source_target_pairs={{0,255},{1,248},{2,249},{3,250},{4,251},{5,252},{6,253},{7,254},{8... | collective-permute-start | bytes 393224 | tf_op jit(solution)/shard_map/ppermute | solution.py:341
  14.3 1.1 %slice_bitcast_fusion = (bf16[64,1024]{1,0:T(8,128)(2,1)S(1)}, bf16[64,1024]{1,0:T(8,128)(2,1)S(1)}, bf16[64,1024]{1,0:T(8,128)(2,1)S(1)}, bf16[64,1024]{1,0:T(8,128)(2,1)S(1)}) fusion(bf16[16,16,1024]{2,1,0:T(8,128)(2,1)} %param.7), kind=kLoop, calls=%fused_computation.6 | loop fusion | bytes 1048576 | tf_op jit(solution)/shard_map/reshape | solution.py:346
  15.4 1.8 %collective-permute-start.3 = (bf16[64,1024]{1,0:T(8,128)(2,1)S(1)}, bf16[64,1024]{1,0:T(8,128)(2,1)S(1)}, u32[]{:S(2)}, u32[]{:S(2)}) collective-permute-start(bf16[64,1024]{1,0:T(8,128)(2,1)S(1)} %get-tuple-element.79), channel_id=1, source_target_pairs={{0,7},{1,0},{2,1},{3,2},{4,3},{5,4},{6,5},{7,6},{8,15},{9,8},{10,9... | collective-permute-start | bytes 393224 | tf_op jit(solution)/shard_map/ppermute | solution.py:341
  17.7 1.1 %collective-permute-start.5 = (bf16[64,1024]{1,0:T(8,128)(2,1)S(1)}, bf16[64,1024]{1,0:T(8,128)(2,1)S(1)}, u32[]{:S(2)}, u32[]{:S(2)}) collective-permute-start(bf16[64,1024]{1,0:T(8,128)(2,1)S(1)} %get-tuple-element.80), channel_id=1, source_target_pairs={{0,255},{1,248},{2,249},{3,250},{4,251},{5,252},{6,253},{7,254},{8... | collective-permute-start | bytes 393224 | tf_op jit(solution)/shard_map/ppermute | solution.py:341
  18.8 4.2 %project_part.1 = (f32[1024,256]{1,0:T(8,128)S(1)}, f32[1024,256]{1,0:T(8,128)S(1)}, bf16[1024,256]{1,0:T(8,128)(2,1)S(1)}, f32[64,256]{1,0:T(8,128)S(1)}, bf16[256,1024]{1,0:T(8,128)(2,1)S(1)}) custom-call(bf16[64,1024]{1,0:T(8,128)(2,1)S(1)} %get-tuple-element.83.x0_ref, bf16[64,1024]{1,0:T(8,128)(2,1)S(1)} %collective-permute-done.x1_ref, ...), custom_call_target="tpu_custom_call" | custom-call | flops 4400000000 | bytes 1048576 | tf_op jit(solution)/shard_map/project_part/pallas_call | solution.py:278
  23.0 1.1 %collective-permute-start.7 = (bf16[256,1024]{1,0:T(8,128)(2,1)S(1)}, bf16[256,1024]{1,0:T(8,128)(2,1)S(1)}, u32[]{:S(2)}, u32[]{:S(2)}) collective-permute-start(bf16[256,1024]{1,0:T(8,128)(2,1)S(1)} %get-tuple-element.44.x_ref), channel_id=1, source_target_pairs={{0,8},{8,0},{32,40},{40,32},{64,72},{72,64},{96,104},{104,96},{128... | collective-permute-start | bytes 1572872 | tf_op jit(solution)/shard_map/ppermute | solution.py:366
  24.5 4.3 %attention_part.1 = (bf16[1024,256]{1,0:T(8,128)(2,1)S(1)}, f32[32,256,256]{2,1,0:T(8,128)S(1)}) custom-call(f32[1024,256]{1,0:T(8,128)S(1)} %get-tuple-element.40.query_ref, f32[1024,256]{1,0:T(8,128)S(1)} %get-tuple-element.41.key_ref, bf16[1024,256]{1,0:T(8,128)(2,1)S(1)} %get-tuple-element.42.value_ref, f32[32]{0:T(128)S(1)} %copy-done, ...), custom_call_target="tpu_custom_call" | custom-call | flops 6600000000 | bytes 1048576 | tf_op jit(solution)/shard_map/attention_part/pallas_call | solution.py:286
  29.1 1.9 %norm_part.1 = (bf16[256,1024]{1,0:T(8,128)(2,1)S(1)}, bf16[1024,256]{1,0:T(8,128)(2,1)S(1)}) custom-call(bf16[1024,256]{1,0:T(8,128)(2,1)S(1)} %get-tuple-element.43.att_ref, bf16[64,1024]{1,0:T(8,128)(2,1)S(1)} %get-tuple-element.77.g0_ref, bf16[64,1024]{1,0:T(8,128)(2,1)S(1)} %collective-permute-done.3.after_ref.g1_ref, ...), custom_call_target="tpu_custom_call" | custom-call | flops 2200000000 | bytes 1048576 | tf_op jit(solution)/shard_map/norm_part/pallas_call | solution.py:291
  31.1 1.3 %value_part.1.after_ref.grad_value_ref.refs_2_ = bf16[1024,256]{1,0:T(8,128)(2,1)S(1)} custom-call(f32[32,256,256]{2,1,0:T(8,128)S(1)} %get-tuple-element.45.probs_ref, bf16[1024,256]{1,0:T(8,128)(2,1)S(1)} %get-tuple-element.46.grad_att_ref, bf16[1024,256]{1,0:T(8,128)(2,1)S(1)} %collective-permute-done.6.after_ref.att2_ref), custom_call_target="tpu_custom_call" | custom-call | flops 2200000000 | bytes 1048576 | tf_op jit(solution)/shard_map/value_part/pallas_call | solution.py:298
  33.0 1.3 %left_rows.1.left_ref = bf16[1024,512]{1,0:T(8,128)(2,1)S(1)} custom-call(bf16[1024,1024]{1,0:T(8,128)(2,1)S(1)} %fusion.after_ref.order_ref, bf16[1024,256]{1,0:T(8,128)(2,1)S(1)} %get-tuple-element.43.att_ref, bf16[1024,256]{1,0:T(8,128)(2,1)S(1)} %collective-permute-done.6.after_ref.att2_ref, bf16[256,1024]{1,0:T(8,128)(2,1)S(1)} %get-tuple-element.44.x_ref, ...), custom_call_target="tpu_custom_call" | custom-call | flops 1320000000 | bytes 1048576 | tf_op jit(solution)/shard_map/left_rows/pallas_call | solution.py:303
  35.8 1.1 %weight_terms.2 = (bf16[256,1024]{1,0:T(8,128)(2,1)S(1)}, bf16[256,1024]{1,0:T(8,128)(2,1)S(1)}, bf16[256,1024]{1,0:T(8,128)(2,1)S(1)}) custom-call(bf16[1024,512]{1,0:T(8,128)(2,1)S(1)} %left_rows.1.left_ref, bf16[256,1024]{1,0:T(8,128)(2,1)S(1)} %get-tuple-element.47.grad_mix_ref, bf16[256,1024]{1,0:T(8,128)(2,1)S(1)} %collective-permute-done.8.grad_mix2_ref, ...), custom_call_target="tpu_custom_call" | custom-call | flops 660000000 | bytes 1048576 | tf_op jit(solution)/shard_map/weight_terms/pallas_call | solution.py:310
  38.0 2.7 %collective-permute-start.12 = (bf16[256,1024]{1,0:T(8,128)(2,1)S(1)}, bf16[256,1024]{1,0:T(8,128)(2,1)S(1)}, u32[]{:S(2)}, u32[]{:S(2)}) collective-permute-start(bf16[256,1024]{1,0:T(8,128)(2,1)S(1)} %get-tuple-element.57), channel_id=1, source_target_pairs={{0,17},{8,14},{32,49},{40,46},{64,81},{72,78},{96,113},{104,110},{... | collective-permute-start | bytes 1572872 | tf_op jit(solution)/shard_map/ppermute | solution.py:374
  40.6 5.4 %score_part.1 = (bf16[1024,256]{1,0:T(8,128)(2,1)S(1)}, bf16[1024,256]{1,0:T(8,128)(2,1)S(1)}) custom-call(f32[32,256,256]{2,1,0:T(8,128)S(1)} %get-tuple-element.45.probs_ref, bf16[1024,256]{1,0:T(8,128)(2,1)S(1)} %get-tuple-element.46.grad_att_ref, f32[1024,256]{1,0:T(8,128)S(1)} %get-tuple-element.40.query_ref, ...), custom_call_target="tpu_custom_call" | custom-call | flops 330000000 | bytes 1048576 | tf_op jit(solution)/shard_map/score_part/pallas_call | solution.py:322
  46.1 1.9 %input_part.1 = (bf16[64,1024]{1,0:T(8,128)(2,1)S(1)}, bf16[64,1024]{1,0:T(8,128)(2,1)S(1)}, bf16[64,1024]{1,0:T(8,128)(2,1)S(1)}, bf16[64,1024]{1,0:T(8,128)(2,1)S(1)}) custom-call(bf16[1024,256]{1,0:T(8,128)(2,1)S(1)} %get-tuple-element.50.refs_0_, bf16[1024,256]{1,0:T(8,128)(2,1)S(1)} %get-tuple-element.51.refs_1_, ...), custom_call_target="tpu_custom_call" | custom-call | flops 220000000 | bytes 1048576 | tf_op jit(solution)/shard_map/input_part/pallas_call | solution.py:332
  48.0 3.3 %collective-permute-done.11.refs_1_ = bf16[256,1024]{1,0:T(8,128)(2,1)S(1)} collective-permute-done((bf16[256,1024]{1,0:T(8,128)(2,1)S(1)}, bf16[256,1024]{1,0:T(8,128)(2,1)S(1)}, u32[]{:S(2)}, u32[]{:S(2)}) %collective-permute-start.11) | collective-permute-done | bytes 524320 | tf_op jit(solution)/shard_map/ppermute | solution.py:374
  51.5 1.7 %collective-permute-start.16 = (bf16[64,1024]{1,0:T(8,128)(2,1)S(1)}, bf16[64,1024]{1,0:T(8,128)(2,1)S(1)}, u32[]{:S(2)}, u32[]{:S(2)}) collective-permute-start(bf16[64,1024]{1,0:T(8,128)(2,1)S(1)} %get-tuple-element.74), channel_id=1, source_target_pairs={{0,4},{8,24},{32,36},{40,56},{64,68},{72,88},{96,100},{104,120},{1... | collective-permute-start | bytes 393224 | tf_op jit(solution)/shard_map/ppermute | solution.py:374
  53.7 2.1 %collective-permute-start.18 = (bf16[64,1024]{1,0:T(8,128)(2,1)S(1)}, bf16[64,1024]{1,0:T(8,128)(2,1)S(1)}, u32[]{:S(2)}, u32[]{:S(2)}) collective-permute-start(bf16[64,1024]{1,0:T(8,128)(2,1)S(1)} %get-tuple-element.76), channel_id=1, source_target_pairs={{0,6},{8,25},{32,38},{40,57},{64,70},{72,89},{96,102},{104,121},{1... | collective-permute-start | bytes 393224 | tf_op jit(solution)/shard_map/ppermute | solution.py:374
  55.8 2.5 %collective-permute-start.14 = (bf16[64,1024]{1,0:T(8,128)(2,1)S(1)}, bf16[64,1024]{1,0:T(8,128)(2,1)S(1)}, u32[]{:S(2)}, u32[]{:S(2)}) collective-permute-start(bf16[64,1024]{1,0:T(8,128)(2,1)S(1)} %get-tuple-element.70), channel_id=1, source_target_pairs={{0,8},{1,9},{2,10},{3,11},{4,12},{5,13},{6,14},{7,15},{8,16},{9,17... | collective-permute-start | bytes 393224 | tf_op jit(solution)/shard_map/ppermute | solution.py:341
  58.4 2.1 %collective-permute-start.13 = (bf16[64,1024]{1,0:T(8,128)(2,1)S(1)}, bf16[64,1024]{1,0:T(8,128)(2,1)S(1)}, u32[]{:S(2)}, u32[]{:S(2)}) collective-permute-start(bf16[64,1024]{1,0:T(8,128)(2,1)S(1)} %get-tuple-element.69), channel_id=1, source_target_pairs={{0,9},{1,10},{2,11},{3,12},{4,13},{5,14},{6,15},{7,8},{8,17},{9,18... | collective-permute-start | bytes 393224 | tf_op jit(solution)/shard_map/ppermute | solution.py:341
  61.3 4.1 %all-to-all-start = ((bf16[8,8,1024]{2,1,0:T(8,128)(2,1)}), bf16[8,8,1024]{2,1,0:T(8,128)(2,1)S(1)}, u32[]{:S(2)}, u32[]{:S(2)}) async-start(bf16[8,8,1024]{2,1,0:T(8,128)(2,1)} %bitcast.16), calls=%async_computation | async-start | bytes 262144 | tf_op jit(solution)/shard_map/all_to_all | solution.py:395
  66.7 6.7 %all-to-all-done = bf16[8,8,1024]{2,1,0:T(8,128)(2,1)S(1)} async-done(((bf16[8,8,1024]{2,1,0:T(8,128)(2,1)}), bf16[8,8,1024]{2,1,0:T(8,128)(2,1)S(1)}, u32[]{:S(2)}, u32[]{:S(2)}) %all-to-all-start) | async-done | bytes 131104 | tf_op jit(solution)/shard_map/all_to_all | solution.py:395
  73.5 2.6 %collective-permute-start.19 = (f32[4,1024]{1,0:T(4,128)S(1)}, f32[4,1024]{1,0:T(4,128)S(1)}, u32[]{:S(2)}, u32[]{:S(2)}) collective-permute-start(f32[4,1024]{1,0:T(4,128)S(1)} %slice.40), channel_id=1, source_target_pairs={{0,8},{8,0},{32,40},{40,32},{64,72},{72,64},{96,104},{104,96},{128... | collective-permute-start | bytes 49160 | tf_op jit(solution)/shard_map/ppermute | solution.py:366
  (53 shorter events, 9.8 us)
Async XLA Ops:
  1.8 15.9 %collective-permute-start = (bf16[64,1024]{1,0:T(8,128)(2,1)S(1)}, bf16[64,1024]{1,0:T(8,128)(2,1)S(1)}, u32[]{:S(2)}, u32[]{:S(2)}) collective-permute-start(bf16[64,1024]{1,0:T(8,128)(2,1)S(1)} %get-tuple-element.82), channel_id=1, source_target_pairs={{0,7},{1,0},{2,1},{3,2},{4,3},{5,4},{6,5},{7,6},{8,15},{9,8},{10,9... | collective-permute-start | bytes 393224 | tf_op jit(solution)/shard_map/ppermute | solution.py:341
  6.3 12.5 %collective-permute-start.1 = (bf16[64,1024]{1,0:T(8,128)(2,1)S(1)}, bf16[64,1024]{1,0:T(8,128)(2,1)S(1)}, u32[]{:S(2)}, u32[]{:S(2)}) collective-permute-start(bf16[64,1024]{1,0:T(8,128)(2,1)S(1)} %get-tuple-element.84), channel_id=1, source_target_pairs={{0,248},{1,249},{2,250},{3,251},{4,252},{5,253},{6,254},{7,255},{8... | collective-permute-start | bytes 393224 | tf_op jit(solution)/shard_map/ppermute | solution.py:341
  7.3 11.5 %collective-permute-start.2 = (bf16[64,1024]{1,0:T(8,128)(2,1)S(1)}, bf16[64,1024]{1,0:T(8,128)(2,1)S(1)}, u32[]{:S(2)}, u32[]{:S(2)}) collective-permute-start(bf16[64,1024]{1,0:T(8,128)(2,1)S(1)} %get-tuple-element.81), channel_id=1, source_target_pairs={{0,255},{1,248},{2,249},{3,250},{4,251},{5,252},{6,253},{7,254},{8... | collective-permute-start | bytes 393224 | tf_op jit(solution)/shard_map/ppermute | solution.py:341
  15.4 8.6 %collective-permute-start.3 = (bf16[64,1024]{1,0:T(8,128)(2,1)S(1)}, bf16[64,1024]{1,0:T(8,128)(2,1)S(1)}, u32[]{:S(2)}, u32[]{:S(2)}) collective-permute-start(bf16[64,1024]{1,0:T(8,128)(2,1)S(1)} %get-tuple-element.79), channel_id=1, source_target_pairs={{0,7},{1,0},{2,1},{3,2},{4,3},{5,4},{6,5},{7,6},{8,15},{9,8},{10,9... | collective-permute-start | bytes 393224 | tf_op jit(solution)/shard_map/ppermute | solution.py:341
  17.2 6.8 %collective-permute-start.4 = (bf16[64,1024]{1,0:T(8,128)(2,1)S(1)}, bf16[64,1024]{1,0:T(8,128)(2,1)S(1)}, u32[]{:S(2)}, u32[]{:S(2)}) collective-permute-start(bf16[64,1024]{1,0:T(8,128)(2,1)S(1)} %get-tuple-element.78), channel_id=1, source_target_pairs={{0,248},{1,249},{2,250},{3,251},{4,252},{5,253},{6,254},{7,255},{8... | collective-permute-start | bytes 393224 | tf_op jit(solution)/shard_map/ppermute | solution.py:341
  17.7 6.8 %collective-permute-start.5 = (bf16[64,1024]{1,0:T(8,128)(2,1)S(1)}, bf16[64,1024]{1,0:T(8,128)(2,1)S(1)}, u32[]{:S(2)}, u32[]{:S(2)}) collective-permute-start(bf16[64,1024]{1,0:T(8,128)(2,1)S(1)} %get-tuple-element.80), channel_id=1, source_target_pairs={{0,255},{1,248},{2,249},{3,250},{4,251},{5,252},{6,253},{7,254},{8... | collective-permute-start | bytes 393224 | tf_op jit(solution)/shard_map/ppermute | solution.py:341
  18.8 5.7 %copy-start = (f32[32]{0:T(128)S(1)}, f32[32]{0:T(128)}, u32[]{:S(2)}) copy-start(f32[32]{0:T(128)} %scale_ref.3) | copy-start | bytes 388
  23.0 6.1 %collective-permute-start.7 = (bf16[256,1024]{1,0:T(8,128)(2,1)S(1)}, bf16[256,1024]{1,0:T(8,128)(2,1)S(1)}, u32[]{:S(2)}, u32[]{:S(2)}) collective-permute-start(bf16[256,1024]{1,0:T(8,128)(2,1)S(1)} %get-tuple-element.44.x_ref), channel_id=1, source_target_pairs={{0,8},{8,0},{32,40},{40,32},{64,72},{72,64},{96,104},{104,96},{128... | collective-permute-start | bytes 1572872 | tf_op jit(solution)/shard_map/ppermute | solution.py:366
  28.8 2.2 %collective-permute-start.6 = (bf16[1024,256]{1,0:T(8,128)(2,1)S(1)}, bf16[1024,256]{1,0:T(8,128)(2,1)S(1)}, u32[]{:S(2)}, u32[]{:S(2)}) collective-permute-start(bf16[1024,256]{1,0:T(8,128)(2,1)S(1)} %get-tuple-element.43.att_ref), channel_id=1, source_target_pairs={{0,8},{8,0},{32,40},{40,32},{64,72},{72,64},{96,104},{104,96},{128... | collective-permute-start | bytes 1572872 | tf_op jit(solution)/shard_map/ppermute | solution.py:366
  32.4 2.1 %collective-permute-start.9 = (bf16[1024,256]{1,0:T(8,128)(2,1)S(1)}, bf16[1024,256]{1,0:T(8,128)(2,1)S(1)}, u32[]{:S(2)}, u32[]{:S(2)}) collective-permute-start(bf16[1024,256]{1,0:T(8,128)(2,1)S(1)} %value_part.1.after_ref.grad_value_ref.refs_2_), channel_id=1, source_target_pairs={{0,8},{8,0},{32,40},{40,32},{64,72},{72,64},{96,104},{104,96},{128... | collective-permute-start | bytes 1572872 | tf_op jit(solution)/shard_map/ppermute | solution.py:366
  32.9 2.3 %collective-permute-start.8 = (bf16[256,1024]{1,0:T(8,128)(2,1)S(1)}, bf16[256,1024]{1,0:T(8,128)(2,1)S(1)}, u32[]{:S(2)}, u32[]{:S(2)}) collective-permute-start(bf16[256,1024]{1,0:T(8,128)(2,1)S(1)} %get-tuple-element.47.grad_mix_ref), channel_id=1, source_target_pairs={{0,8},{8,0},{32,40},{40,32},{64,72},{72,64},{96,104},{104,96},{128... | collective-permute-start | bytes 1572872 | tf_op jit(solution)/shard_map/ppermute | solution.py:366
  35.7 12.3 %collective-permute-start.10 = (bf16[256,1024]{1,0:T(8,128)(2,1)S(1)}, bf16[256,1024]{1,0:T(8,128)(2,1)S(1)}, u32[]{:S(2)}, u32[]{:S(2)}) collective-permute-start(bf16[256,1024]{1,0:T(8,128)(2,1)S(1)} %weight_terms.3), channel_id=1, source_target_pairs={{0,16},{8,12},{32,48},{40,44},{64,80},{72,76},{96,112},{104,108},{... | collective-permute-start | bytes 1572872 | tf_op jit(solution)/shard_map/ppermute | solution.py:374
  36.9 14.3 %collective-permute-start.11 = (bf16[256,1024]{1,0:T(8,128)(2,1)S(1)}, bf16[256,1024]{1,0:T(8,128)(2,1)S(1)}, u32[]{:S(2)}, u32[]{:S(2)}) collective-permute-start(bf16[256,1024]{1,0:T(8,128)(2,1)S(1)} %get-tuple-element.56), channel_id=1, source_target_pairs={{0,1},{8,10},{32,33},{40,42},{64,65},{72,74},{96,97},{104,106},{12... | collective-permute-start | bytes 1572872 | tf_op jit(solution)/shard_map/ppermute | solution.py:374
  38.0 13.3 %collective-permute-start.12 = (bf16[256,1024]{1,0:T(8,128)(2,1)S(1)}, bf16[256,1024]{1,0:T(8,128)(2,1)S(1)}, u32[]{:S(2)}, u32[]{:S(2)}) collective-permute-start(bf16[256,1024]{1,0:T(8,128)(2,1)S(1)} %get-tuple-element.57), channel_id=1, source_target_pairs={{0,17},{8,14},{32,49},{40,46},{64,81},{72,78},{96,113},{104,110},{... | collective-permute-start | bytes 1572872 | tf_op jit(solution)/shard_map/ppermute | solution.py:374
  40.6 5.4 %slice-start.1 = ((s8[6291456]{0:T(1024)(128)(4,1)}), s8[2097152]{0:T(1024)(128)(4,1)S(1)}, s32[]{:S(2)}) async-start(s8[6291456]{0:T(1024)(128)(4,1)} %bitcast.27), calls=%async_computation.2 | async-start | bytes 4194304
  51.2 24.9 %copy-start.3 = (bf16[16,16,1024]{2,1,0:T(8,128)(2,1)S(1)}, bf16[16,16,1024]{2,1,0:T(8,128)(2,1)}, u32[]{:S(2)}) copy-start(bf16[16,16,1024]{2,1,0:T(8,128)(2,1)} %param.7) | copy-start | bytes 1572868
  51.5 6.9 %collective-permute-start.16 = (bf16[64,1024]{1,0:T(8,128)(2,1)S(1)}, bf16[64,1024]{1,0:T(8,128)(2,1)S(1)}, u32[]{:S(2)}, u32[]{:S(2)}) collective-permute-start(bf16[64,1024]{1,0:T(8,128)(2,1)S(1)} %get-tuple-element.74), channel_id=1, source_target_pairs={{0,4},{8,24},{32,36},{40,56},{64,68},{72,88},{96,100},{104,120},{1... | collective-permute-start | bytes 393224 | tf_op jit(solution)/shard_map/ppermute | solution.py:374
  53.2 7.4 %collective-permute-start.17 = (bf16[64,1024]{1,0:T(8,128)(2,1)S(1)}, bf16[64,1024]{1,0:T(8,128)(2,1)S(1)}, u32[]{:S(2)}, u32[]{:S(2)}) collective-permute-start(bf16[64,1024]{1,0:T(8,128)(2,1)S(1)} %get-tuple-element.75), channel_id=1, source_target_pairs={{0,2},{8,9},{32,34},{40,41},{64,66},{72,73},{96,98},{104,105},{128... | collective-permute-start | bytes 393224 | tf_op jit(solution)/shard_map/ppermute | solution.py:374
  53.7 6.8 %collective-permute-start.18 = (bf16[64,1024]{1,0:T(8,128)(2,1)S(1)}, bf16[64,1024]{1,0:T(8,128)(2,1)S(1)}, u32[]{:S(2)}, u32[]{:S(2)}) collective-permute-start(bf16[64,1024]{1,0:T(8,128)(2,1)S(1)} %get-tuple-element.76), channel_id=1, source_target_pairs={{0,6},{8,25},{32,38},{40,57},{64,70},{72,89},{96,102},{104,121},{1... | collective-permute-start | bytes 393224 | tf_op jit(solution)/shard_map/ppermute | solution.py:374
  55.8 9.6 %collective-permute-start.14 = (bf16[64,1024]{1,0:T(8,128)(2,1)S(1)}, bf16[64,1024]{1,0:T(8,128)(2,1)S(1)}, u32[]{:S(2)}, u32[]{:S(2)}) collective-permute-start(bf16[64,1024]{1,0:T(8,128)(2,1)S(1)} %get-tuple-element.70), channel_id=1, source_target_pairs={{0,8},{1,9},{2,10},{3,11},{4,12},{5,13},{6,14},{7,15},{8,16},{9,17... | collective-permute-start | bytes 393224 | tf_op jit(solution)/shard_map/ppermute | solution.py:341
  58.4 7.4 %collective-permute-start.15 = (bf16[64,1024]{1,0:T(8,128)(2,1)S(1)}, bf16[64,1024]{1,0:T(8,128)(2,1)S(1)}, u32[]{:S(2)}, u32[]{:S(2)}) collective-permute-start(bf16[64,1024]{1,0:T(8,128)(2,1)S(1)} %get-tuple-element.71), channel_id=1, source_target_pairs={{0,1},{1,2},{2,3},{3,4},{4,5},{5,6},{6,7},{7,0},{8,9},{9,10},{10,1... | collective-permute-start | bytes 393224 | tf_op jit(solution)/shard_map/ppermute | solution.py:341
  58.4 8.0 %collective-permute-start.13 = (bf16[64,1024]{1,0:T(8,128)(2,1)S(1)}, bf16[64,1024]{1,0:T(8,128)(2,1)S(1)}, u32[]{:S(2)}, u32[]{:S(2)}) collective-permute-start(bf16[64,1024]{1,0:T(8,128)(2,1)S(1)} %get-tuple-element.69), channel_id=1, source_target_pairs={{0,9},{1,10},{2,11},{3,12},{4,13},{5,14},{6,15},{7,8},{8,17},{9,18... | collective-permute-start | bytes 393224 | tf_op jit(solution)/shard_map/ppermute | solution.py:341
  61.3 12.2 %all-to-all-start = ((bf16[8,8,1024]{2,1,0:T(8,128)(2,1)}), bf16[8,8,1024]{2,1,0:T(8,128)(2,1)S(1)}, u32[]{:S(2)}, u32[]{:S(2)}) async-start(bf16[8,8,1024]{2,1,0:T(8,128)(2,1)} %bitcast.16), calls=%async_computation | async-start | bytes 262144 | tf_op jit(solution)/shard_map/all_to_all | solution.py:395
  73.5 3.6 %collective-permute-start.19 = (f32[4,1024]{1,0:T(4,128)S(1)}, f32[4,1024]{1,0:T(4,128)S(1)}, u32[]{:S(2)}, u32[]{:S(2)}) collective-permute-start(f32[4,1024]{1,0:T(4,128)S(1)} %slice.40), channel_id=1, source_target_pairs={{0,8},{8,0},{32,40},{40,32},{64,72},{72,64},{96,104},{104,96},{128... | collective-permute-start | bytes 49160 | tf_op jit(solution)/shard_map/ppermute | solution.py:366
  (3 other events, 14.5 us)

commit v6 on v5

--- a/solution.py
+++ b/solution.py
@@ -387,7 +387,7 @@
     dx, dy = jnp.where(core == 0, a, b), jnp.where(core == 0, b, a)
     x = (r // 2 % 2 * 2 + c % 2 + dx) % 4
     y = (c // 2 + dy) % 4
-    source = z * 128 + x // 2 * 64 + (core + far) % 2 * 32 + y * 8 + x % 2 * 4 + row
+    source = z * 128 + x // 2 * 64 + far * 32 + y * 8 + x % 2 * 4 + row
     return (source[:, None] == jnp.arange(C, dtype=jnp.int32)[None, :]).astype(BF)
 
 
@@ -396,14 +396,15 @@
     return jnp.sum(got.astype(F32), axis=0)
 
 
-def z_sum(blocks):
+def chip_column_sum(blocks):
     groups = [
-        [line(x, y, z, core) for z in range(8)]
+        [line(x, y, z, core) for z in range(8) for core in range(2)]
         for x in range(4)
         for y in range(4)
-        for core in range(2)
     ]
-    return group_sum(blocks, groups)
+    got = lax.all_to_all(blocks, BOTH, 0, 0, axis_index_groups=groups, tiled=True)
+    got = jnp.sum(got.reshape(8, 2, 4, C).astype(F32), axis=0)
+    return got[0], got[1]
 
 
 def per_device(tokens, grad_out, w_qkv, w_proj, norm_gain, logit_scale):
@@ -430,10 +431,7 @@
     blocks, grad_input = lax.optimization_barrier((blocks, grad_input))
     others = gathered(blocks, 1)
     (terms,) = block_sums(1, blocks[0], *others)
-    terms = z_sum(terms.reshape(8, 8, C))
-    kept, got = terms[:4], other_core(terms[4:])
-    first = lax.axis_index("row") % 2 == 0
-    proj_part, value_part = jnp.where(first, kept, got), jnp.where(first, got, kept)
+    proj_part, value_part = chip_column_sum(terms.reshape(16, 4, C))
     back = jnp.stack(
         [
             passed(grad_input[3], 1, 1, rows, cols),

time: 77.9 us -> 77 us (0.988)
  local copies, waits for them, and re-layouts: 2.36 us -> 3.67 us
  starting transfers between devices: 37 us -> 35.9 us
    ppermute x5 -> x4, starting transfers between devices: 4.55 us -> 1.95 us  [other_core(): return lax.ppermute(array, BOTH, pairs)]
    all_to_all x1, starting transfers between devices: 4.12 us -> 5.6 us  [chip_column_sum(): lax.all_to_all(blocks, BOTH, 0, 0, axis_index_groups=groups, tiled=True)]
    all_to_all x1, waiting for transfers between devices: 6.72 us -> 7.91 us  [chip_column_sum(): lax.all_to_all(blocks, BOTH, 0, 0, axis_index_groups=groups, tiled=True)]
    ppermute x9, waiting for transfers between devices: 1.51 us -> 0.48 us  [passed(): return lax.ppermute(array, ('row', 'col'), pairs)]
  transfers between devices with their start and end apart: 21 -> 20, of which waited for: 7 -> 5; matrix products, arithmetic and copies ran while one was open for 4% -> 5% of each run, Pallas kernels for 27% -> 26%
where the time goes in v6:
time: 77 us; the launch traced here: 76.8 us
  starting transfers between devices  35.9 us (47%)
  Pallas kernels  22.2 us (29%)
  waiting for transfers between devices  12.6 us (16%)
  local copies, waits for them, and re-layouts  3.67 us (5%)
  other arithmetic  1.62 us (2%)
  between operations  0.86 us (1%)
    ppermute x9, starting transfers between devices, passed(): return lax.ppermute(array, ('row', 'col'), pairs)  20.2 us
    ppermute x6, starting transfers between devices, moved(): return lax.ppermute(array, BOTH, pairs)  8.21 us
    all_to_all x1, waiting for transfers between devices, chip_column_sum(): lax.all_to_all(blocks, BOTH, 0, 0, axis_index_groups=groups, tiled=True)  7.91 us
    all_to_all x1, starting transfers between devices, chip_column_sum(): lax.all_to_all(blocks, BOTH, 0, 0, axis_index_groups=groups, tiled=True)  5.6 us
    pallas_call x1, Pallas kernels, score_grads(): return call(kernel, outs, ins, 0.3, 'score_part', 16, scratch)(*args)  5.39 us
    pallas_call x1, Pallas kernels, attention(): call(kernel, outs, [VM] * 3 + [SM] + [ANY] * 3, 6, 'attention_part', 16)  4.29 us
    pallas_call x1, Pallas kernels, project(): call(project_kernel, outs, ins, 4, 'project_part', 24, scratch)  4.18 us
    ppermute x6, waiting for transfers between devices, moved(): return lax.ppermute(array, BOTH, pairs)  3.27 us
  transfers between devices with their start and end apart: 20, of which 5 were waited for; matrix products, arithmetic and copies ran while one was open for 5% of the time, Pallas kernels for 26%

profile of v6, /device:TPU:1, one launch (start us, length us, event | category | flops | bytes accessed | tf_op | source)
XLA Modules:
  0.0 76.8 jit_solution(13363954123031439983)
XLA Ops:
  0.6 1.1 %slice_bitcast_fusion.4 = (bf16[64,1024]{1,0:T(8,128)(2,1)S(1)}, bf16[64,1024]{1,0:T(8,128)(2,1)S(1)}, bf16[64,1024]{1,0:T(8,128)(2,1)S(1)}, bf16[64,1024]{1,0:T(8,128)(2,1)S(1)}) fusion(bf16[16,16,1024]{2,1,0:T(8,128)(2,1)} %param.6), kind=kLoop, calls=%fused_computation.10 | loop fusion | bytes 1048576 | tf_op jit(solution)/shard_map/reshape | solution.py:346
  1.8 4.6 %collective-permute-start = (bf16[64,1024]{1,0:T(8,128)(2,1)S(1)}, bf16[64,1024]{1,0:T(8,128)(2,1)S(1)}, u32[]{:S(2)}, u32[]{:S(2)}) collective-permute-start(bf16[64,1024]{1,0:T(8,128)(2,1)S(1)} %get-tuple-element.82), channel_id=1, source_target_pairs={{0,7},{1,0},{2,1},{3,2},{4,3},{5,4},{6,5},{7,6},{8,15},{9,8},{10,9... | collective-permute-start | bytes 393224 | tf_op jit(solution)/shard_map/ppermute | solution.py:341
  7.3 7.0 %collective-permute-start.2 = (bf16[64,1024]{1,0:T(8,128)(2,1)S(1)}, bf16[64,1024]{1,0:T(8,128)(2,1)S(1)}, u32[]{:S(2)}, u32[]{:S(2)}) collective-permute-start(bf16[64,1024]{1,0:T(8,128)(2,1)S(1)} %get-tuple-element.81), channel_id=1, source_target_pairs={{0,255},{1,248},{2,249},{3,250},{4,251},{5,252},{6,253},{7,254},{8... | collective-permute-start | bytes 393224 | tf_op jit(solution)/shard_map/ppermute | solution.py:341
  14.3 1.1 %slice_bitcast_fusion = (bf16[64,1024]{1,0:T(8,128)(2,1)S(1)}, bf16[64,1024]{1,0:T(8,128)(2,1)S(1)}, bf16[64,1024]{1,0:T(8,128)(2,1)S(1)}, bf16[64,1024]{1,0:T(8,128)(2,1)S(1)}) fusion(bf16[16,16,1024]{2,1,0:T(8,128)(2,1)} %param.7), kind=kLoop, calls=%fused_computation.6 | loop fusion | bytes 1048576 | tf_op jit(solution)/shard_map/reshape | solution.py:346
  15.4 1.8 %collective-permute-start.3 = (bf16[64,1024]{1,0:T(8,128)(2,1)S(1)}, bf16[64,1024]{1,0:T(8,128)(2,1)S(1)}, u32[]{:S(2)}, u32[]{:S(2)}) collective-permute-start(bf16[64,1024]{1,0:T(8,128)(2,1)S(1)} %get-tuple-element.79), channel_id=1, source_target_pairs={{0,7},{1,0},{2,1},{3,2},{4,3},{5,4},{6,5},{7,6},{8,15},{9,8},{10,9... | collective-permute-start | bytes 393224 | tf_op jit(solution)/shard_map/ppermute | solution.py:341
  17.7 1.1 %collective-permute-start.5 = (bf16[64,1024]{1,0:T(8,128)(2,1)S(1)}, bf16[64,1024]{1,0:T(8,128)(2,1)S(1)}, u32[]{:S(2)}, u32[]{:S(2)}) collective-permute-start(bf16[64,1024]{1,0:T(8,128)(2,1)S(1)} %get-tuple-element.80), channel_id=1, source_target_pairs={{0,255},{1,248},{2,249},{3,250},{4,251},{5,252},{6,253},{7,254},{8... | collective-permute-start | bytes 393224 | tf_op jit(solution)/shard_map/ppermute | solution.py:341
  18.8 4.2 %project_part.1 = (f32[1024,256]{1,0:T(8,128)S(1)}, f32[1024,256]{1,0:T(8,128)S(1)}, bf16[1024,256]{1,0:T(8,128)(2,1)S(1)}, f32[64,256]{1,0:T(8,128)S(1)}, bf16[256,1024]{1,0:T(8,128)(2,1)S(1)}) custom-call(bf16[64,1024]{1,0:T(8,128)(2,1)S(1)} %get-tuple-element.83.x0_ref, bf16[64,1024]{1,0:T(8,128)(2,1)S(1)} %collective-permute-done.x1_ref, ...), custom_call_target="tpu_custom_call" | custom-call | flops 4400000000 | bytes 1048576 | tf_op jit(solution)/shard_map/project_part/pallas_call | solution.py:278
  23.0 1.1 %collective-permute-start.7 = (bf16[256,1024]{1,0:T(8,128)(2,1)S(1)}, bf16[256,1024]{1,0:T(8,128)(2,1)S(1)}, u32[]{:S(2)}, u32[]{:S(2)}) collective-permute-start(bf16[256,1024]{1,0:T(8,128)(2,1)S(1)} %get-tuple-element.44.x_ref), channel_id=1, source_target_pairs={{0,8},{8,0},{32,40},{40,32},{64,72},{72,64},{96,104},{104,96},{128... | collective-permute-start | bytes 1572872 | tf_op jit(solution)/shard_map/ppermute | solution.py:366
  24.5 4.3 %attention_part.1 = (bf16[1024,256]{1,0:T(8,128)(2,1)S(1)}, f32[32,256,256]{2,1,0:T(8,128)S(1)}) custom-call(f32[1024,256]{1,0:T(8,128)S(1)} %get-tuple-element.40.query_ref, f32[1024,256]{1,0:T(8,128)S(1)} %get-tuple-element.41.key_ref, bf16[1024,256]{1,0:T(8,128)(2,1)S(1)} %get-tuple-element.42.value_ref, f32[32]{0:T(128)S(1)} %copy-done, ...), custom_call_target="tpu_custom_call" | custom-call | flops 6600000000 | bytes 1048576 | tf_op jit(solution)/shard_map/attention_part/pallas_call | solution.py:286
  29.1 1.9 %norm_part.1 = (bf16[256,1024]{1,0:T(8,128)(2,1)S(1)}, bf16[1024,256]{1,0:T(8,128)(2,1)S(1)}) custom-call(bf16[1024,256]{1,0:T(8,128)(2,1)S(1)} %get-tuple-element.43.att_ref, bf16[64,1024]{1,0:T(8,128)(2,1)S(1)} %get-tuple-element.77.g0_ref, bf16[64,1024]{1,0:T(8,128)(2,1)S(1)} %collective-permute-done.3.after_ref.g1_ref, ...), custom_call_target="tpu_custom_call" | custom-call | flops 2200000000 | bytes 1048576 | tf_op jit(solution)/shard_map/norm_part/pallas_call | solution.py:291
  31.1 1.3 %value_part.1.after_ref.grad_value_ref.refs_2_ = bf16[1024,256]{1,0:T(8,128)(2,1)S(1)} custom-call(f32[32,256,256]{2,1,0:T(8,128)S(1)} %get-tuple-element.45.probs_ref, bf16[1024,256]{1,0:T(8,128)(2,1)S(1)} %get-tuple-element.46.grad_att_ref, bf16[1024,256]{1,0:T(8,128)(2,1)S(1)} %collective-permute-done.6.after_ref.att2_ref), custom_call_target="tpu_custom_call" | custom-call | flops 2200000000 | bytes 1048576 | tf_op jit(solution)/shard_map/value_part/pallas_call | solution.py:298
  33.0 1.3 %left_rows.1.left_ref = bf16[1024,512]{1,0:T(8,128)(2,1)S(1)} custom-call(bf16[1024,1024]{1,0:T(8,128)(2,1)S(1)} %fusion.after_ref.order_ref, bf16[1024,256]{1,0:T(8,128)(2,1)S(1)} %get-tuple-element.43.att_ref, bf16[1024,256]{1,0:T(8,128)(2,1)S(1)} %collective-permute-done.6.after_ref.att2_ref, bf16[256,1024]{1,0:T(8,128)(2,1)S(1)} %get-tuple-element.44.x_ref, ...), custom_call_target="tpu_custom_call" | custom-call | flops 1320000000 | bytes 1048576 | tf_op jit(solution)/shard_map/left_rows/pallas_call | solution.py:303
  35.8 1.1 %weight_terms.2 = (bf16[256,1024]{1,0:T(8,128)(2,1)S(1)}, bf16[256,1024]{1,0:T(8,128)(2,1)S(1)}, bf16[256,1024]{1,0:T(8,128)(2,1)S(1)}) custom-call(bf16[1024,512]{1,0:T(8,128)(2,1)S(1)} %left_rows.1.left_ref, bf16[256,1024]{1,0:T(8,128)(2,1)S(1)} %get-tuple-element.47.grad_mix_ref, bf16[256,1024]{1,0:T(8,128)(2,1)S(1)} %collective-permute-done.8.grad_mix2_ref, ...), custom_call_target="tpu_custom_call" | custom-call | flops 660000000 | bytes 1048576 | tf_op jit(solution)/shard_map/weight_terms/pallas_call | solution.py:310
  36.9 1.0 %collective-permute-start.11 = (bf16[256,1024]{1,0:T(8,128)(2,1)S(1)}, bf16[256,1024]{1,0:T(8,128)(2,1)S(1)}, u32[]{:S(2)}, u32[]{:S(2)}) collective-permute-start(bf16[256,1024]{1,0:T(8,128)(2,1)S(1)} %get-tuple-element.56), channel_id=1, source_target_pairs={{0,1},{8,10},{32,33},{40,42},{64,65},{72,74},{96,97},{104,106},{12... | collective-permute-start | bytes 1572872 | tf_op jit(solution)/shard_map/ppermute | solution.py:374
  38.0 2.7 %collective-permute-start.12 = (bf16[256,1024]{1,0:T(8,128)(2,1)S(1)}, bf16[256,1024]{1,0:T(8,128)(2,1)S(1)}, u32[]{:S(2)}, u32[]{:S(2)}) collective-permute-start(bf16[256,1024]{1,0:T(8,128)(2,1)S(1)} %get-tuple-element.57), channel_id=1, source_target_pairs={{0,17},{8,14},{32,49},{40,46},{64,81},{72,78},{96,113},{104,110},{... | collective-permute-start | bytes 1572872 | tf_op jit(solution)/shard_map/ppermute | solution.py:374
  40.6 5.4 %score_part.1 = (bf16[1024,256]{1,0:T(8,128)(2,1)S(1)}, bf16[1024,256]{1,0:T(8,128)(2,1)S(1)}) custom-call(f32[32,256,256]{2,1,0:T(8,128)S(1)} %get-tuple-element.45.probs_ref, bf16[1024,256]{1,0:T(8,128)(2,1)S(1)} %get-tuple-element.46.grad_att_ref, f32[1024,256]{1,0:T(8,128)S(1)} %get-tuple-element.40.query_ref, ...), custom_call_target="tpu_custom_call" | custom-call | flops 330000000 | bytes 1048576 | tf_op jit(solution)/shard_map/score_part/pallas_call | solution.py:322
  46.1 1.9 %input_part.1 = (bf16[64,1024]{1,0:T(8,128)(2,1)S(1)}, bf16[64,1024]{1,0:T(8,128)(2,1)S(1)}, bf16[64,1024]{1,0:T(8,128)(2,1)S(1)}, bf16[64,1024]{1,0:T(8,128)(2,1)S(1)}) custom-call(bf16[1024,256]{1,0:T(8,128)(2,1)S(1)} %get-tuple-element.50.refs_0_, bf16[1024,256]{1,0:T(8,128)(2,1)S(1)} %get-tuple-element.51.refs_1_, ...), custom_call_target="tpu_custom_call" | custom-call | flops 220000000 | bytes 1048576 | tf_op jit(solution)/shard_map/input_part/pallas_call | solution.py:332
  48.0 3.3 %collective-permute-done.11.refs_1_ = bf16[256,1024]{1,0:T(8,128)(2,1)S(1)} collective-permute-done((bf16[256,1024]{1,0:T(8,128)(2,1)S(1)}, bf16[256,1024]{1,0:T(8,128)(2,1)S(1)}, u32[]{:S(2)}, u32[]{:S(2)}) %collective-permute-start.11) | collective-permute-done | bytes 524320 | tf_op jit(solution)/shard_map/ppermute | solution.py:374
  51.5 1.7 %collective-permute-start.16 = (bf16[64,1024]{1,0:T(8,128)(2,1)S(1)}, bf16[64,1024]{1,0:T(8,128)(2,1)S(1)}, u32[]{:S(2)}, u32[]{:S(2)}) collective-permute-start(bf16[64,1024]{1,0:T(8,128)(2,1)S(1)} %get-tuple-element.74), channel_id=1, source_target_pairs={{0,4},{8,24},{32,36},{40,56},{64,68},{72,88},{96,100},{104,120},{1... | collective-permute-start | bytes 393224 | tf_op jit(solution)/shard_map/ppermute | solution.py:374
  53.7 2.1 %collective-permute-start.18 = (bf16[64,1024]{1,0:T(8,128)(2,1)S(1)}, bf16[64,1024]{1,0:T(8,128)(2,1)S(1)}, u32[]{:S(2)}, u32[]{:S(2)}) collective-permute-start(bf16[64,1024]{1,0:T(8,128)(2,1)S(1)} %get-tuple-element.76), channel_id=1, source_target_pairs={{0,6},{8,25},{32,38},{40,57},{64,70},{72,89},{96,102},{104,121},{1... | collective-permute-start | bytes 393224 | tf_op jit(solution)/shard_map/ppermute | solution.py:374
  55.8 2.5 %collective-permute-start.14 = (bf16[64,1024]{1,0:T(8,128)(2,1)S(1)}, bf16[64,1024]{1,0:T(8,128)(2,1)S(1)}, u32[]{:S(2)}, u32[]{:S(2)}) collective-permute-start(bf16[64,1024]{1,0:T(8,128)(2,1)S(1)} %get-tuple-element.70), channel_id=1, source_target_pairs={{0,8},{1,9},{2,10},{3,11},{4,12},{5,13},{6,14},{7,15},{8,16},{9,17... | collective-permute-start | bytes 393224 | tf_op jit(solution)/shard_map/ppermute | solution.py:341
  58.4 2.1 %collective-permute-start.13 = (bf16[64,1024]{1,0:T(8,128)(2,1)S(1)}, bf16[64,1024]{1,0:T(8,128)(2,1)S(1)}, u32[]{:S(2)}, u32[]{:S(2)}) collective-permute-start(bf16[64,1024]{1,0:T(8,128)(2,1)S(1)} %get-tuple-element.69), channel_id=1, source_target_pairs={{0,9},{1,10},{2,11},{3,12},{4,13},{5,14},{6,15},{7,8},{8,17},{9,18... | collective-permute-start | bytes 393224 | tf_op jit(solution)/shard_map/ppermute | solution.py:341
  61.4 5.6 %all-to-all-start = ((bf16[16,4,1024]{2,1,0:T(4,128)(2,1)}), bf16[16,4,1024]{2,1,0:T(4,128)(2,1)S(1)}, u32[]{:S(2)}, u32[]{:S(2)}) async-start(bf16[16,4,1024]{2,1,0:T(4,128)(2,1)} %reshape.193), calls=%async_computation | async-start | bytes 262144 | tf_op jit(solution)/shard_map/all_to_all | solution.py:405
  68.2 7.9 %all-to-all-done = bf16[16,4,1024]{2,1,0:T(4,128)(2,1)S(1)} async-done(((bf16[16,4,1024]{2,1,0:T(4,128)(2,1)}), bf16[16,4,1024]{2,1,0:T(4,128)(2,1)S(1)}, u32[]{:S(2)}, u32[]{:S(2)}) %all-to-all-start) | async-done | bytes 131104 | tf_op jit(solution)/shard_map/all_to_all | solution.py:405
  (51 shorter events, 7.8 us)
Async XLA Ops:
  1.8 15.9 %collective-permute-start = (bf16[64,1024]{1,0:T(8,128)(2,1)S(1)}, bf16[64,1024]{1,0:T(8,128)(2,1)S(1)}, u32[]{:S(2)}, u32[]{:S(2)}) collective-permute-start(bf16[64,1024]{1,0:T(8,128)(2,1)S(1)} %get-tuple-element.82), channel_id=1, source_target_pairs={{0,7},{1,0},{2,1},{3,2},{4,3},{5,4},{6,5},{7,6},{8,15},{9,8},{10,9... | collective-permute-start | bytes 393224 | tf_op jit(solution)/shard_map/ppermute | solution.py:341
  6.3 12.5 %collective-permute-start.1 = (bf16[64,1024]{1,0:T(8,128)(2,1)S(1)}, bf16[64,1024]{1,0:T(8,128)(2,1)S(1)}, u32[]{:S(2)}, u32[]{:S(2)}) collective-permute-start(bf16[64,1024]{1,0:T(8,128)(2,1)S(1)} %get-tuple-element.84), channel_id=1, source_target_pairs={{0,248},{1,249},{2,250},{3,251},{4,252},{5,253},{6,254},{7,255},{8... | collective-permute-start | bytes 393224 | tf_op jit(solution)/shard_map/ppermute | solution.py:341
  7.3 11.5 %collective-permute-start.2 = (bf16[64,1024]{1,0:T(8,128)(2,1)S(1)}, bf16[64,1024]{1,0:T(8,128)(2,1)S(1)}, u32[]{:S(2)}, u32[]{:S(2)}) collective-permute-start(bf16[64,1024]{1,0:T(8,128)(2,1)S(1)} %get-tuple-element.81), channel_id=1, source_target_pairs={{0,255},{1,248},{2,249},{3,250},{4,251},{5,252},{6,253},{7,254},{8... | collective-permute-start | bytes 393224 | tf_op jit(solution)/shard_map/ppermute | solution.py:341
  15.4 8.6 %collective-permute-start.3 = (bf16[64,1024]{1,0:T(8,128)(2,1)S(1)}, bf16[64,1024]{1,0:T(8,128)(2,1)S(1)}, u32[]{:S(2)}, u32[]{:S(2)}) collective-permute-start(bf16[64,1024]{1,0:T(8,128)(2,1)S(1)} %get-tuple-element.79), channel_id=1, source_target_pairs={{0,7},{1,0},{2,1},{3,2},{4,3},{5,4},{6,5},{7,6},{8,15},{9,8},{10,9... | collective-permute-start | bytes 393224 | tf_op jit(solution)/shard_map/ppermute | solution.py:341
  17.2 6.8 %collective-permute-start.4 = (bf16[64,1024]{1,0:T(8,128)(2,1)S(1)}, bf16[64,1024]{1,0:T(8,128)(2,1)S(1)}, u32[]{:S(2)}, u32[]{:S(2)}) collective-permute-start(bf16[64,1024]{1,0:T(8,128)(2,1)S(1)} %get-tuple-element.78), channel_id=1, source_target_pairs={{0,248},{1,249},{2,250},{3,251},{4,252},{5,253},{6,254},{7,255},{8... | collective-permute-start | bytes 393224 | tf_op jit(solution)/shard_map/ppermute | solution.py:341
  17.7 6.8 %collective-permute-start.5 = (bf16[64,1024]{1,0:T(8,128)(2,1)S(1)}, bf16[64,1024]{1,0:T(8,128)(2,1)S(1)}, u32[]{:S(2)}, u32[]{:S(2)}) collective-permute-start(bf16[64,1024]{1,0:T(8,128)(2,1)S(1)} %get-tuple-element.80), channel_id=1, source_target_pairs={{0,255},{1,248},{2,249},{3,250},{4,251},{5,252},{6,253},{7,254},{8... | collective-permute-start | bytes 393224 | tf_op jit(solution)/shard_map/ppermute | solution.py:341
  18.8 5.7 %copy-start = (f32[32]{0:T(128)S(1)}, f32[32]{0:T(128)}, u32[]{:S(2)}) copy-start(f32[32]{0:T(128)} %scale_ref.3) | copy-start | bytes 388
  23.0 6.1 %collective-permute-start.7 = (bf16[256,1024]{1,0:T(8,128)(2,1)S(1)}, bf16[256,1024]{1,0:T(8,128)(2,1)S(1)}, u32[]{:S(2)}, u32[]{:S(2)}) collective-permute-start(bf16[256,1024]{1,0:T(8,128)(2,1)S(1)} %get-tuple-element.44.x_ref), channel_id=1, source_target_pairs={{0,8},{8,0},{32,40},{40,32},{64,72},{72,64},{96,104},{104,96},{128... | collective-permute-start | bytes 1572872 | tf_op jit(solution)/shard_map/ppermute | solution.py:366
  28.8 2.2 %collective-permute-start.6 = (bf16[1024,256]{1,0:T(8,128)(2,1)S(1)}, bf16[1024,256]{1,0:T(8,128)(2,1)S(1)}, u32[]{:S(2)}, u32[]{:S(2)}) collective-permute-start(bf16[1024,256]{1,0:T(8,128)(2,1)S(1)} %get-tuple-element.43.att_ref), channel_id=1, source_target_pairs={{0,8},{8,0},{32,40},{40,32},{64,72},{72,64},{96,104},{104,96},{128... | collective-permute-start | bytes 1572872 | tf_op jit(solution)/shard_map/ppermute | solution.py:366
  32.4 2.1 %collective-permute-start.9 = (bf16[1024,256]{1,0:T(8,128)(2,1)S(1)}, bf16[1024,256]{1,0:T(8,128)(2,1)S(1)}, u32[]{:S(2)}, u32[]{:S(2)}) collective-permute-start(bf16[1024,256]{1,0:T(8,128)(2,1)S(1)} %value_part.1.after_ref.grad_value_ref.refs_2_), channel_id=1, source_target_pairs={{0,8},{8,0},{32,40},{40,32},{64,72},{72,64},{96,104},{104,96},{128... | collective-permute-start | bytes 1572872 | tf_op jit(solution)/shard_map/ppermute | solution.py:366
  32.9 2.3 %collective-permute-start.8 = (bf16[256,1024]{1,0:T(8,128)(2,1)S(1)}, bf16[256,1024]{1,0:T(8,128)(2,1)S(1)}, u32[]{:S(2)}, u32[]{:S(2)}) collective-permute-start(bf16[256,1024]{1,0:T(8,128)(2,1)S(1)} %get-tuple-element.47.grad_mix_ref), channel_id=1, source_target_pairs={{0,8},{8,0},{32,40},{40,32},{64,72},{72,64},{96,104},{104,96},{128... | collective-permute-start | bytes 1572872 | tf_op jit(solution)/shard_map/ppermute | solution.py:366
  35.7 12.3 %collective-permute-start.10 = (bf16[256,1024]{1,0:T(8,128)(2,1)S(1)}, bf16[256,1024]{1,0:T(8,128)(2,1)S(1)}, u32[]{:S(2)}, u32[]{:S(2)}) collective-permute-start(bf16[256,1024]{1,0:T(8,128)(2,1)S(1)} %weight_terms.3), channel_id=1, source_target_pairs={{0,16},{8,12},{32,48},{40,44},{64,80},{72,76},{96,112},{104,108},{... | collective-permute-start | bytes 1572872 | tf_op jit(solution)/shard_map/ppermute | solution.py:374
  36.9 14.3 %collective-permute-start.11 = (bf16[256,1024]{1,0:T(8,128)(2,1)S(1)}, bf16[256,1024]{1,0:T(8,128)(2,1)S(1)}, u32[]{:S(2)}, u32[]{:S(2)}) collective-permute-start(bf16[256,1024]{1,0:T(8,128)(2,1)S(1)} %get-tuple-element.56), channel_id=1, source_target_pairs={{0,1},{8,10},{32,33},{40,42},{64,65},{72,74},{96,97},{104,106},{12... | collective-permute-start | bytes 1572872 | tf_op jit(solution)/shard_map/ppermute | solution.py:374
  38.0 13.3 %collective-permute-start.12 = (bf16[256,1024]{1,0:T(8,128)(2,1)S(1)}, bf16[256,1024]{1,0:T(8,128)(2,1)S(1)}, u32[]{:S(2)}, u32[]{:S(2)}) collective-permute-start(bf16[256,1024]{1,0:T(8,128)(2,1)S(1)} %get-tuple-element.57), channel_id=1, source_target_pairs={{0,17},{8,14},{32,49},{40,46},{64,81},{72,78},{96,113},{104,110},{... | collective-permute-start | bytes 1572872 | tf_op jit(solution)/shard_map/ppermute | solution.py:374
  40.6 5.4 %slice-start = ((s8[6291456]{0:T(1024)(128)(4,1)}), s8[4194304]{0:T(1024)(128)(4,1)S(1)}, s32[]{:S(2)}) async-start(s8[6291456]{0:T(1024)(128)(4,1)} %bitcast.32), calls=%async_computation.1 | async-start | bytes 8388608
  40.6 5.4 %slice-start.1 = ((s8[6291456]{0:T(1024)(128)(4,1)}), s8[2097152]{0:T(1024)(128)(4,1)S(1)}, s32[]{:S(2)}) async-start(s8[6291456]{0:T(1024)(128)(4,1)} %bitcast.32), calls=%async_computation.2 | async-start | bytes 4194304
  51.2 16.0 %copy-start.3 = (bf16[16,16,1024]{2,1,0:T(8,128)(2,1)S(1)}, bf16[16,16,1024]{2,1,0:T(8,128)(2,1)}, u32[]{:S(2)}) copy-start(bf16[16,16,1024]{2,1,0:T(8,128)(2,1)} %param.7) | copy-start | bytes 1572868
  51.5 6.9 %collective-permute-start.16 = (bf16[64,1024]{1,0:T(8,128)(2,1)S(1)}, bf16[64,1024]{1,0:T(8,128)(2,1)S(1)}, u32[]{:S(2)}, u32[]{:S(2)}) collective-permute-start(bf16[64,1024]{1,0:T(8,128)(2,1)S(1)} %get-tuple-element.74), channel_id=1, source_target_pairs={{0,4},{8,24},{32,36},{40,56},{64,68},{72,88},{96,100},{104,120},{1... | collective-permute-start | bytes 393224 | tf_op jit(solution)/shard_map/ppermute | solution.py:374
  53.2 7.4 %collective-permute-start.17 = (bf16[64,1024]{1,0:T(8,128)(2,1)S(1)}, bf16[64,1024]{1,0:T(8,128)(2,1)S(1)}, u32[]{:S(2)}, u32[]{:S(2)}) collective-permute-start(bf16[64,1024]{1,0:T(8,128)(2,1)S(1)} %get-tuple-element.75), channel_id=1, source_target_pairs={{0,2},{8,9},{32,34},{40,41},{64,66},{72,73},{96,98},{104,105},{128... | collective-permute-start | bytes 393224 | tf_op jit(solution)/shard_map/ppermute | solution.py:374
  53.7 6.8 %collective-permute-start.18 = (bf16[64,1024]{1,0:T(8,128)(2,1)S(1)}, bf16[64,1024]{1,0:T(8,128)(2,1)S(1)}, u32[]{:S(2)}, u32[]{:S(2)}) collective-permute-start(bf16[64,1024]{1,0:T(8,128)(2,1)S(1)} %get-tuple-element.76), channel_id=1, source_target_pairs={{0,6},{8,25},{32,38},{40,57},{64,70},{72,89},{96,102},{104,121},{1... | collective-permute-start | bytes 393224 | tf_op jit(solution)/shard_map/ppermute | solution.py:374
  55.8 11.1 %collective-permute-start.14 = (bf16[64,1024]{1,0:T(8,128)(2,1)S(1)}, bf16[64,1024]{1,0:T(8,128)(2,1)S(1)}, u32[]{:S(2)}, u32[]{:S(2)}) collective-permute-start(bf16[64,1024]{1,0:T(8,128)(2,1)S(1)} %get-tuple-element.70), channel_id=1, source_target_pairs={{0,8},{1,9},{2,10},{3,11},{4,12},{5,13},{6,14},{7,15},{8,16},{9,17... | collective-permute-start | bytes 393224 | tf_op jit(solution)/shard_map/ppermute | solution.py:341
  58.4 8.6 %collective-permute-start.15 = (bf16[64,1024]{1,0:T(8,128)(2,1)S(1)}, bf16[64,1024]{1,0:T(8,128)(2,1)S(1)}, u32[]{:S(2)}, u32[]{:S(2)}) collective-permute-start(bf16[64,1024]{1,0:T(8,128)(2,1)S(1)} %get-tuple-element.71), channel_id=1, source_target_pairs={{0,1},{1,2},{2,3},{3,4},{4,5},{5,6},{6,7},{7,0},{8,9},{9,10},{10,1... | collective-permute-start | bytes 393224 | tf_op jit(solution)/shard_map/ppermute | solution.py:341
  58.4 8.5 %collective-permute-start.13 = (bf16[64,1024]{1,0:T(8,128)(2,1)S(1)}, bf16[64,1024]{1,0:T(8,128)(2,1)S(1)}, u32[]{:S(2)}, u32[]{:S(2)}) collective-permute-start(bf16[64,1024]{1,0:T(8,128)(2,1)S(1)} %get-tuple-element.69), channel_id=1, source_target_pairs={{0,9},{1,10},{2,11},{3,12},{4,13},{5,14},{6,15},{7,8},{8,17},{9,18... | collective-permute-start | bytes 393224 | tf_op jit(solution)/shard_map/ppermute | solution.py:341
  61.4 14.8 %all-to-all-start = ((bf16[16,4,1024]{2,1,0:T(4,128)(2,1)}), bf16[16,4,1024]{2,1,0:T(4,128)(2,1)S(1)}, u32[]{:S(2)}, u32[]{:S(2)}) async-start(bf16[16,4,1024]{2,1,0:T(4,128)(2,1)} %reshape.193), calls=%async_computation | async-start | bytes 262144 | tf_op jit(solution)/shard_map/all_to_all | solution.py:405
  (2 other events, 9.1 us)

commit v7 on v6

--- a/solution.py
+++ b/solution.py
@@ -141,7 +141,7 @@
         ).astype(BF)
 
 
-def value_kernel(probs_ref, grad_att_ref, after_ref, grad_value_ref):
+def value_kernel(probs_ref, grad_att_ref, after_ref, after2_ref, grad_value_ref):
     def head(h, carry):
         rows = head_rows(h)
         grad_value_ref[rows, :] = dot(
@@ -294,7 +294,7 @@
 
 
 def value_grads(*args):
-    ins = [VM] * 2 + [ANY]
+    ins = [VM] * 2 + [ANY] * 2
     return call(value_kernel, shape((C, TOK), BF), ins, 2, "value_part", 16)(*args)
 
 
@@ -415,8 +415,8 @@
     query, key, value, unit_scale, tokens_win = project(x, w_qkv, order)
     att, probs = attention(rows, cols, query, key, value, logit_scale, *g[1:])
     tokens_win2, att2 = other_core(tokens_win), other_core(att)
-    grad_mix, grad_att = output_norm(att, g, w_proj, norm_gain.reshape(1, C), tokens_win2)
-    grad_value = value_grads(probs, grad_att, att2)
+    grad_mix, grad_att = output_norm(att, g, w_proj, norm_gain.reshape(1, C), tokens_win)
+    grad_value = value_grads(probs, grad_att, att2, tokens_win2)
     grad_mix2, grad_value2 = other_core(grad_mix), other_core(grad_value)
     left = left_rows(order, att, att2, tokens_win, tokens_win2, grad_value)
     blocks = weight_terms(left, grad_mix, grad_mix2, grad_value, grad_value2)

time: 77 us -> 76.7 us (level)
  starting transfers between devices: 35.9 us -> 35.1 us
    ppermute x9, waiting for transfers between devices: 0.48 us -> 1.52 us  [passed(): return lax.ppermute(array, ('row', 'col'), pairs)]
  transfers between devices with their start and end apart: 20 -> 20, of which waited for: 5 -> 5; matrix products, arithmetic and copies ran while one was open for 5% -> 5% of each run, Pallas kernels for 26% -> 22%
where the time goes in v7:
time: 76.7 us; the launch traced here: 76.5 us
  starting transfers between devices  35.1 us (46%)
  Pallas kernels  22.1 us (29%)
  waiting for transfers between devices  13.1 us (17%)
  local copies, waits for them, and re-layouts  3.67 us (5%)
  other arithmetic  1.62 us (2%)
  between operations  0.85 us (1%)
    ppermute x9, starting transfers between devices, passed(): return lax.ppermute(array, ('row', 'col'), pairs)  20.6 us
    all_to_all x1, waiting for transfers between devices, chip_column_sum(): lax.all_to_all(blocks, BOTH, 0, 0, axis_index_groups=groups, tiled=True)  7.91 us
    ppermute x6, starting transfers between devices, moved(): return lax.ppermute(array, BOTH, pairs)  7.78 us
    all_to_all x1, starting transfers between devices, chip_column_sum(): lax.all_to_all(blocks, BOTH, 0, 0, axis_index_groups=groups, tiled=True)  5.46 us
    pallas_call x1, Pallas kernels, score_grads(): return call(kernel, outs, ins, 0.3, 'score_part', 16, scratch)(*args)  5.39 us
    pallas_call x1, Pallas kernels, attention(): call(kernel, outs, [VM] * 3 + [SM] + [ANY] * 3, 6, 'attention_part', 16)  4.29 us
    pallas_call x1, Pallas kernels, project(): call(project_kernel, outs, ins, 4, 'project_part', 24, scratch)  4.18 us
    ppermute x6, waiting for transfers between devices, moved(): return lax.ppermute(array, BOTH, pairs)  3.28 us
  transfers between devices with their start and end apart: 20, of which 5 were waited for; matrix products, arithmetic and copies ran while one was open for 5% of the time, Pallas kernels for 22%

profile of v7, /device:TPU:1, one launch (start us, length us, event | category | flops | bytes accessed | tf_op | source)
XLA Modules:
  0.0 76.5 jit_solution(6484439007192135892)
XLA Ops:
  0.6 1.1 %slice_bitcast_fusion.4 = (bf16[64,1024]{1,0:T(8,128)(2,1)S(1)}, bf16[64,1024]{1,0:T(8,128)(2,1)S(1)}, bf16[64,1024]{1,0:T(8,128)(2,1)S(1)}, bf16[64,1024]{1,0:T(8,128)(2,1)S(1)}) fusion(bf16[16,16,1024]{2,1,0:T(8,128)(2,1)} %param.6), kind=kLoop, calls=%fused_computation.10 | loop fusion | bytes 1048576 | tf_op jit(solution)/shard_map/reshape | solution.py:346
  1.8 4.6 %collective-permute-start = (bf16[64,1024]{1,0:T(8,128)(2,1)S(1)}, bf16[64,1024]{1,0:T(8,128)(2,1)S(1)}, u32[]{:S(2)}, u32[]{:S(2)}) collective-permute-start(bf16[64,1024]{1,0:T(8,128)(2,1)S(1)} %get-tuple-element.82), channel_id=1, source_target_pairs={{0,7},{1,0},{2,1},{3,2},{4,3},{5,4},{6,5},{7,6},{8,15},{9,8},{10,9... | collective-permute-start | bytes 393224 | tf_op jit(solution)/shard_map/ppermute | solution.py:341
  6.3 1.0 %collective-permute-start.1 = (bf16[64,1024]{1,0:T(8,128)(2,1)S(1)}, bf16[64,1024]{1,0:T(8,128)(2,1)S(1)}, u32[]{:S(2)}, u32[]{:S(2)}) collective-permute-start(bf16[64,1024]{1,0:T(8,128)(2,1)S(1)} %get-tuple-element.84), channel_id=1, source_target_pairs={{0,248},{1,249},{2,250},{3,251},{4,252},{5,253},{6,254},{7,255},{8... | collective-permute-start | bytes 393224 | tf_op jit(solution)/shard_map/ppermute | solution.py:341
  7.3 7.0 %collective-permute-start.2 = (bf16[64,1024]{1,0:T(8,128)(2,1)S(1)}, bf16[64,1024]{1,0:T(8,128)(2,1)S(1)}, u32[]{:S(2)}, u32[]{:S(2)}) collective-permute-start(bf16[64,1024]{1,0:T(8,128)(2,1)S(1)} %get-tuple-element.81), channel_id=1, source_target_pairs={{0,255},{1,248},{2,249},{3,250},{4,251},{5,252},{6,253},{7,254},{8... | collective-permute-start | bytes 393224 | tf_op jit(solution)/shard_map/ppermute | solution.py:341
  14.3 1.1 %slice_bitcast_fusion = (bf16[64,1024]{1,0:T(8,128)(2,1)S(1)}, bf16[64,1024]{1,0:T(8,128)(2,1)S(1)}, bf16[64,1024]{1,0:T(8,128)(2,1)S(1)}, bf16[64,1024]{1,0:T(8,128)(2,1)S(1)}) fusion(bf16[16,16,1024]{2,1,0:T(8,128)(2,1)} %param.7), kind=kLoop, calls=%fused_computation.6 | loop fusion | bytes 1048576 | tf_op jit(solution)/shard_map/reshape | solution.py:346
  15.4 1.8 %collective-permute-start.3 = (bf16[64,1024]{1,0:T(8,128)(2,1)S(1)}, bf16[64,1024]{1,0:T(8,128)(2,1)S(1)}, u32[]{:S(2)}, u32[]{:S(2)}) collective-permute-start(bf16[64,1024]{1,0:T(8,128)(2,1)S(1)} %get-tuple-element.79), channel_id=1, source_target_pairs={{0,7},{1,0},{2,1},{3,2},{4,3},{5,4},{6,5},{7,6},{8,15},{9,8},{10,9... | collective-permute-start | bytes 393224 | tf_op jit(solution)/shard_map/ppermute | solution.py:341
  17.7 1.1 %collective-permute-start.5 = (bf16[64,1024]{1,0:T(8,128)(2,1)S(1)}, bf16[64,1024]{1,0:T(8,128)(2,1)S(1)}, u32[]{:S(2)}, u32[]{:S(2)}) collective-permute-start(bf16[64,1024]{1,0:T(8,128)(2,1)S(1)} %get-tuple-element.80), channel_id=1, source_target_pairs={{0,255},{1,248},{2,249},{3,250},{4,251},{5,252},{6,253},{7,254},{8... | collective-permute-start | bytes 393224 | tf_op jit(solution)/shard_map/ppermute | solution.py:341
  18.8 4.2 %project_part.1 = (f32[1024,256]{1,0:T(8,128)S(1)}, f32[1024,256]{1,0:T(8,128)S(1)}, bf16[1024,256]{1,0:T(8,128)(2,1)S(1)}, f32[64,256]{1,0:T(8,128)S(1)}, bf16[256,1024]{1,0:T(8,128)(2,1)S(1)}) custom-call(bf16[64,1024]{1,0:T(8,128)(2,1)S(1)} %get-tuple-element.83.x0_ref, bf16[64,1024]{1,0:T(8,128)(2,1)S(1)} %collective-permute-done.x1_ref, ...), custom_call_target="tpu_custom_call" | custom-call | flops 4400000000 | bytes 1048576 | tf_op jit(solution)/shard_map/project_part/pallas_call | solution.py:278
  24.5 4.3 %attention_part.1 = (bf16[1024,256]{1,0:T(8,128)(2,1)S(1)}, f32[32,256,256]{2,1,0:T(8,128)S(1)}) custom-call(f32[1024,256]{1,0:T(8,128)S(1)} %get-tuple-element.40.query_ref, f32[1024,256]{1,0:T(8,128)S(1)} %get-tuple-element.41.key_ref, bf16[1024,256]{1,0:T(8,128)(2,1)S(1)} %get-tuple-element.42.value_ref, f32[32]{0:T(128)S(1)} %copy-done, ...), custom_call_target="tpu_custom_call" | custom-call | flops 6600000000 | bytes 1048576 | tf_op jit(solution)/shard_map/attention_part/pallas_call | solution.py:286
  29.4 1.9 %norm_part.1 = (bf16[256,1024]{1,0:T(8,128)(2,1)S(1)}, bf16[1024,256]{1,0:T(8,128)(2,1)S(1)}) custom-call(bf16[1024,256]{1,0:T(8,128)(2,1)S(1)} %get-tuple-element.43.att_ref, bf16[64,1024]{1,0:T(8,128)(2,1)S(1)} %get-tuple-element.77.g0_ref, bf16[64,1024]{1,0:T(8,128)(2,1)S(1)} %collective-permute-done.3.after_ref.g1_ref, ...), custom_call_target="tpu_custom_call" | custom-call | flops 2200000000 | bytes 1048576 | tf_op jit(solution)/shard_map/norm_part/pallas_call | solution.py:291
  31.7 1.3 %value_part.1.after_ref.grad_value_ref.refs_2_ = bf16[1024,256]{1,0:T(8,128)(2,1)S(1)} custom-call(f32[32,256,256]{2,1,0:T(8,128)S(1)} %get-tuple-element.45.probs_ref, bf16[1024,256]{1,0:T(8,128)(2,1)S(1)} %get-tuple-element.46.grad_att_ref, bf16[1024,256]{1,0:T(8,128)(2,1)S(1)} %collective-permute-done.6.after_ref.att2_ref, ...), custom_call_target="tpu_custom_call" | custom-call | flops 2200000000 | bytes 1048576 | tf_op jit(solution)/shard_map/value_part/pallas_call | solution.py:298
  33.3 1.3 %left_rows.1.left_ref = bf16[1024,512]{1,0:T(8,128)(2,1)S(1)} custom-call(bf16[1024,1024]{1,0:T(8,128)(2,1)S(1)} %fusion.after_ref.order_ref, bf16[1024,256]{1,0:T(8,128)(2,1)S(1)} %get-tuple-element.43.att_ref, bf16[1024,256]{1,0:T(8,128)(2,1)S(1)} %collective-permute-done.6.after_ref.att2_ref, bf16[256,1024]{1,0:T(8,128)(2,1)S(1)} %get-tuple-element.44.after_ref.x_ref, ...), custom_call_target="tpu_custom_call" | custom-call | flops 1320000000 | bytes 1048576 | tf_op jit(solution)/shard_map/left_rows/pallas_call | solution.py:303
  35.6 1.1 %weight_terms.2 = (bf16[256,1024]{1,0:T(8,128)(2,1)S(1)}, bf16[256,1024]{1,0:T(8,128)(2,1)S(1)}, bf16[256,1024]{1,0:T(8,128)(2,1)S(1)}) custom-call(bf16[1024,512]{1,0:T(8,128)(2,1)S(1)} %left_rows.1.left_ref, bf16[256,1024]{1,0:T(8,128)(2,1)S(1)} %get-tuple-element.47.grad_mix_ref, bf16[256,1024]{1,0:T(8,128)(2,1)S(1)} %collective-permute-done.8.grad_mix2_ref, ...), custom_call_target="tpu_custom_call" | custom-call | flops 660000000 | bytes 1048576 | tf_op jit(solution)/shard_map/weight_terms/pallas_call | solution.py:310
  36.7 1.0 %collective-permute-start.11 = (bf16[256,1024]{1,0:T(8,128)(2,1)S(1)}, bf16[256,1024]{1,0:T(8,128)(2,1)S(1)}, u32[]{:S(2)}, u32[]{:S(2)}) collective-permute-start(bf16[256,1024]{1,0:T(8,128)(2,1)S(1)} %get-tuple-element.56), channel_id=1, source_target_pairs={{0,1},{8,10},{32,33},{40,42},{64,65},{72,74},{96,97},{104,106},{12... | collective-permute-start | bytes 1572872 | tf_op jit(solution)/shard_map/ppermute | solution.py:374
  37.7 2.7 %collective-permute-start.12 = (bf16[256,1024]{1,0:T(8,128)(2,1)S(1)}, bf16[256,1024]{1,0:T(8,128)(2,1)S(1)}, u32[]{:S(2)}, u32[]{:S(2)}) collective-permute-start(bf16[256,1024]{1,0:T(8,128)(2,1)S(1)} %get-tuple-element.57), channel_id=1, source_target_pairs={{0,17},{8,14},{32,49},{40,46},{64,81},{72,78},{96,113},{104,110},{... | collective-permute-start | bytes 1572872 | tf_op jit(solution)/shard_map/ppermute | solution.py:374
  40.4 5.4 %score_part.1 = (bf16[1024,256]{1,0:T(8,128)(2,1)S(1)}, bf16[1024,256]{1,0:T(8,128)(2,1)S(1)}) custom-call(f32[32,256,256]{2,1,0:T(8,128)S(1)} %get-tuple-element.45.probs_ref, bf16[1024,256]{1,0:T(8,128)(2,1)S(1)} %get-tuple-element.46.grad_att_ref, f32[1024,256]{1,0:T(8,128)S(1)} %get-tuple-element.40.query_ref, ...), custom_call_target="tpu_custom_call" | custom-call | flops 330000000 | bytes 1048576 | tf_op jit(solution)/shard_map/score_part/pallas_call | solution.py:322
  45.9 1.9 %input_part.1 = (bf16[64,1024]{1,0:T(8,128)(2,1)S(1)}, bf16[64,1024]{1,0:T(8,128)(2,1)S(1)}, bf16[64,1024]{1,0:T(8,128)(2,1)S(1)}, bf16[64,1024]{1,0:T(8,128)(2,1)S(1)}) custom-call(bf16[1024,256]{1,0:T(8,128)(2,1)S(1)} %get-tuple-element.50.refs_0_, bf16[1024,256]{1,0:T(8,128)(2,1)S(1)} %get-tuple-element.51.refs_1_, ...), custom_call_target="tpu_custom_call" | custom-call | flops 220000000 | bytes 1048576 | tf_op jit(solution)/shard_map/input_part/pallas_call | solution.py:332
  47.8 3.3 %collective-permute-done.11.refs_1_ = bf16[256,1024]{1,0:T(8,128)(2,1)S(1)} collective-permute-done((bf16[256,1024]{1,0:T(8,128)(2,1)S(1)}, bf16[256,1024]{1,0:T(8,128)(2,1)S(1)}, u32[]{:S(2)}, u32[]{:S(2)}) %collective-permute-start.11) | collective-permute-done | bytes 524320 | tf_op jit(solution)/shard_map/ppermute | solution.py:374
  51.3 1.2 %collective-permute-start.16 = (bf16[64,1024]{1,0:T(8,128)(2,1)S(1)}, bf16[64,1024]{1,0:T(8,128)(2,1)S(1)}, u32[]{:S(2)}, u32[]{:S(2)}) collective-permute-start(bf16[64,1024]{1,0:T(8,128)(2,1)S(1)} %get-tuple-element.74), channel_id=1, source_target_pairs={{0,4},{8,24},{32,36},{40,56},{64,68},{72,88},{96,100},{104,120},{1... | collective-permute-start | bytes 393224 | tf_op jit(solution)/shard_map/ppermute | solution.py:374
  53.4 1.8 %collective-permute-start.18 = (bf16[64,1024]{1,0:T(8,128)(2,1)S(1)}, bf16[64,1024]{1,0:T(8,128)(2,1)S(1)}, u32[]{:S(2)}, u32[]{:S(2)}) collective-permute-start(bf16[64,1024]{1,0:T(8,128)(2,1)S(1)} %get-tuple-element.76), channel_id=1, source_target_pairs={{0,6},{8,25},{32,38},{40,57},{64,70},{72,89},{96,102},{104,121},{1... | collective-permute-start | bytes 393224 | tf_op jit(solution)/shard_map/ppermute | solution.py:374
  55.2 2.8 %collective-permute-start.14 = (bf16[64,1024]{1,0:T(8,128)(2,1)S(1)}, bf16[64,1024]{1,0:T(8,128)(2,1)S(1)}, u32[]{:S(2)}, u32[]{:S(2)}) collective-permute-start(bf16[64,1024]{1,0:T(8,128)(2,1)S(1)} %get-tuple-element.70), channel_id=1, source_target_pairs={{0,8},{1,9},{2,10},{3,11},{4,12},{5,13},{6,14},{7,15},{8,16},{9,17... | collective-permute-start | bytes 393224 | tf_op jit(solution)/shard_map/ppermute | solution.py:341
  58.2 2.1 %collective-permute-start.13 = (bf16[64,1024]{1,0:T(8,128)(2,1)S(1)}, bf16[64,1024]{1,0:T(8,128)(2,1)S(1)}, u32[]{:S(2)}, u32[]{:S(2)}) collective-permute-start(bf16[64,1024]{1,0:T(8,128)(2,1)S(1)} %get-tuple-element.69), channel_id=1, source_target_pairs={{0,9},{1,10},{2,11},{3,12},{4,13},{5,14},{6,15},{7,8},{8,17},{9,18... | collective-permute-start | bytes 393224 | tf_op jit(solution)/shard_map/ppermute | solution.py:341
  61.1 5.5 %all-to-all-start = ((bf16[16,4,1024]{2,1,0:T(4,128)(2,1)}), bf16[16,4,1024]{2,1,0:T(4,128)(2,1)S(1)}, u32[]{:S(2)}, u32[]{:S(2)}) async-start(bf16[16,4,1024]{2,1,0:T(4,128)(2,1)} %reshape.193), calls=%async_computation | async-start | bytes 262144 | tf_op jit(solution)/shard_map/all_to_all | solution.py:405
  67.9 7.9 %all-to-all-done = bf16[16,4,1024]{2,1,0:T(4,128)(2,1)S(1)} async-done(((bf16[16,4,1024]{2,1,0:T(4,128)(2,1)}), bf16[16,4,1024]{2,1,0:T(4,128)(2,1)S(1)}, u32[]{:S(2)}, u32[]{:S(2)}) %all-to-all-start) | async-done | bytes 131104 | tf_op jit(solution)/shard_map/all_to_all | solution.py:405
  (51 shorter events, 8.2 us)
Async XLA Ops:
  1.8 15.9 %collective-permute-start = (bf16[64,1024]{1,0:T(8,128)(2,1)S(1)}, bf16[64,1024]{1,0:T(8,128)(2,1)S(1)}, u32[]{:S(2)}, u32[]{:S(2)}) collective-permute-start(bf16[64,1024]{1,0:T(8,128)(2,1)S(1)} %get-tuple-element.82), channel_id=1, source_target_pairs={{0,7},{1,0},{2,1},{3,2},{4,3},{5,4},{6,5},{7,6},{8,15},{9,8},{10,9... | collective-permute-start | bytes 393224 | tf_op jit(solution)/shard_map/ppermute | solution.py:341
  6.3 12.5 %collective-permute-start.1 = (bf16[64,1024]{1,0:T(8,128)(2,1)S(1)}, bf16[64,1024]{1,0:T(8,128)(2,1)S(1)}, u32[]{:S(2)}, u32[]{:S(2)}) collective-permute-start(bf16[64,1024]{1,0:T(8,128)(2,1)S(1)} %get-tuple-element.84), channel_id=1, source_target_pairs={{0,248},{1,249},{2,250},{3,251},{4,252},{5,253},{6,254},{7,255},{8... | collective-permute-start | bytes 393224 | tf_op jit(solution)/shard_map/ppermute | solution.py:341
  7.3 11.5 %collective-permute-start.2 = (bf16[64,1024]{1,0:T(8,128)(2,1)S(1)}, bf16[64,1024]{1,0:T(8,128)(2,1)S(1)}, u32[]{:S(2)}, u32[]{:S(2)}) collective-permute-start(bf16[64,1024]{1,0:T(8,128)(2,1)S(1)} %get-tuple-element.81), channel_id=1, source_target_pairs={{0,255},{1,248},{2,249},{3,250},{4,251},{5,252},{6,253},{7,254},{8... | collective-permute-start | bytes 393224 | tf_op jit(solution)/shard_map/ppermute | solution.py:341
  15.4 7.6 %collective-permute-start.3 = (bf16[64,1024]{1,0:T(8,128)(2,1)S(1)}, bf16[64,1024]{1,0:T(8,128)(2,1)S(1)}, u32[]{:S(2)}, u32[]{:S(2)}) collective-permute-start(bf16[64,1024]{1,0:T(8,128)(2,1)S(1)} %get-tuple-element.79), channel_id=1, source_target_pairs={{0,7},{1,0},{2,1},{3,2},{4,3},{5,4},{6,5},{7,6},{8,15},{9,8},{10,9... | collective-permute-start | bytes 393224 | tf_op jit(solution)/shard_map/ppermute | solution.py:341
  17.2 6.4 %collective-permute-start.4 = (bf16[64,1024]{1,0:T(8,128)(2,1)S(1)}, bf16[64,1024]{1,0:T(8,128)(2,1)S(1)}, u32[]{:S(2)}, u32[]{:S(2)}) collective-permute-start(bf16[64,1024]{1,0:T(8,128)(2,1)S(1)} %get-tuple-element.78), channel_id=1, source_target_pairs={{0,248},{1,249},{2,250},{3,251},{4,252},{5,253},{6,254},{7,255},{8... | collective-permute-start | bytes 393224 | tf_op jit(solution)/shard_map/ppermute | solution.py:341
  17.7 6.8 %collective-permute-start.5 = (bf16[64,1024]{1,0:T(8,128)(2,1)S(1)}, bf16[64,1024]{1,0:T(8,128)(2,1)S(1)}, u32[]{:S(2)}, u32[]{:S(2)}) collective-permute-start(bf16[64,1024]{1,0:T(8,128)(2,1)S(1)} %get-tuple-element.80), channel_id=1, source_target_pairs={{0,255},{1,248},{2,249},{3,250},{4,251},{5,252},{6,253},{7,254},{8... | collective-permute-start | bytes 393224 | tf_op jit(solution)/shard_map/ppermute | solution.py:341
  18.8 5.7 %copy-start = (f32[32]{0:T(128)S(1)}, f32[32]{0:T(128)}, u32[]{:S(2)}) copy-start(f32[32]{0:T(128)} %scale_ref.3) | copy-start | bytes 388
  28.8 2.9 %collective-permute-start.6 = (bf16[1024,256]{1,0:T(8,128)(2,1)S(1)}, bf16[1024,256]{1,0:T(8,128)(2,1)S(1)}, u32[]{:S(2)}, u32[]{:S(2)}) collective-permute-start(bf16[1024,256]{1,0:T(8,128)(2,1)S(1)} %get-tuple-element.43.att_ref), channel_id=1, source_target_pairs={{0,8},{8,0},{32,40},{40,32},{64,72},{72,64},{96,104},{104,96},{128... | collective-permute-start | bytes 1572872 | tf_op jit(solution)/shard_map/ppermute | solution.py:366
  28.9 2.8 %collective-permute-start.7 = (bf16[256,1024]{1,0:T(8,128)(2,1)S(1)}, bf16[256,1024]{1,0:T(8,128)(2,1)S(1)}, u32[]{:S(2)}, u32[]{:S(2)}) collective-permute-start(bf16[256,1024]{1,0:T(8,128)(2,1)S(1)} %get-tuple-element.44.after_ref.x_ref), channel_id=1, source_target_pairs={{0,8},{8,0},{32,40},{40,32},{64,72},{72,64},{96,104},{104,96},{128... | collective-permute-start | bytes 1572872 | tf_op jit(solution)/shard_map/ppermute | solution.py:366
  31.3 3.3 %collective-permute-start.8 = (bf16[256,1024]{1,0:T(8,128)(2,1)S(1)}, bf16[256,1024]{1,0:T(8,128)(2,1)S(1)}, u32[]{:S(2)}, u32[]{:S(2)}) collective-permute-start(bf16[256,1024]{1,0:T(8,128)(2,1)S(1)} %get-tuple-element.47.grad_mix_ref), channel_id=1, source_target_pairs={{0,8},{8,0},{32,40},{40,32},{64,72},{72,64},{96,104},{104,96},{128... | collective-permute-start | bytes 1572872 | tf_op jit(solution)/shard_map/ppermute | solution.py:366
  33.0 2.0 %collective-permute-start.9 = (bf16[1024,256]{1,0:T(8,128)(2,1)S(1)}, bf16[1024,256]{1,0:T(8,128)(2,1)S(1)}, u32[]{:S(2)}, u32[]{:S(2)}) collective-permute-start(bf16[1024,256]{1,0:T(8,128)(2,1)S(1)} %value_part.1.after_ref.grad_value_ref.refs_2_), channel_id=1, source_target_pairs={{0,8},{8,0},{32,40},{40,32},{64,72},{72,64},{96,104},{104,96},{128... | collective-permute-start | bytes 1572872 | tf_op jit(solution)/shard_map/ppermute | solution.py:366
  35.5 12.3 %collective-permute-start.10 = (bf16[256,1024]{1,0:T(8,128)(2,1)S(1)}, bf16[256,1024]{1,0:T(8,128)(2,1)S(1)}, u32[]{:S(2)}, u32[]{:S(2)}) collective-permute-start(bf16[256,1024]{1,0:T(8,128)(2,1)S(1)} %weight_terms.3), channel_id=1, source_target_pairs={{0,16},{8,12},{32,48},{40,44},{64,80},{72,76},{96,112},{104,108},{... | collective-permute-start | bytes 1572872 | tf_op jit(solution)/shard_map/ppermute | solution.py:374
  36.7 14.3 %collective-permute-start.11 = (bf16[256,1024]{1,0:T(8,128)(2,1)S(1)}, bf16[256,1024]{1,0:T(8,128)(2,1)S(1)}, u32[]{:S(2)}, u32[]{:S(2)}) collective-permute-start(bf16[256,1024]{1,0:T(8,128)(2,1)S(1)} %get-tuple-element.56), channel_id=1, source_target_pairs={{0,1},{8,10},{32,33},{40,42},{64,65},{72,74},{96,97},{104,106},{12... | collective-permute-start | bytes 1572872 | tf_op jit(solution)/shard_map/ppermute | solution.py:374
  37.7 13.3 %collective-permute-start.12 = (bf16[256,1024]{1,0:T(8,128)(2,1)S(1)}, bf16[256,1024]{1,0:T(8,128)(2,1)S(1)}, u32[]{:S(2)}, u32[]{:S(2)}) collective-permute-start(bf16[256,1024]{1,0:T(8,128)(2,1)S(1)} %get-tuple-element.57), channel_id=1, source_target_pairs={{0,17},{8,14},{32,49},{40,46},{64,81},{72,78},{96,113},{104,110},{... | collective-permute-start | bytes 1572872 | tf_op jit(solution)/shard_map/ppermute | solution.py:374
  40.4 5.4 %slice-start = ((s8[6291456]{0:T(1024)(128)(4,1)}), s8[4194304]{0:T(1024)(128)(4,1)S(1)}, s32[]{:S(2)}) async-start(s8[6291456]{0:T(1024)(128)(4,1)} %bitcast.32), calls=%async_computation.1 | async-start | bytes 8388608
  40.4 5.4 %slice-start.1 = ((s8[6291456]{0:T(1024)(128)(4,1)}), s8[2097152]{0:T(1024)(128)(4,1)S(1)}, s32[]{:S(2)}) async-start(s8[6291456]{0:T(1024)(128)(4,1)} %bitcast.32), calls=%async_computation.2 | async-start | bytes 4194304
  51.0 15.9 %copy-start.3 = (bf16[16,16,1024]{2,1,0:T(8,128)(2,1)S(1)}, bf16[16,16,1024]{2,1,0:T(8,128)(2,1)}, u32[]{:S(2)}) copy-start(bf16[16,16,1024]{2,1,0:T(8,128)(2,1)} %param.7) | copy-start | bytes 1572868
  51.3 6.9 %collective-permute-start.16 = (bf16[64,1024]{1,0:T(8,128)(2,1)S(1)}, bf16[64,1024]{1,0:T(8,128)(2,1)S(1)}, u32[]{:S(2)}, u32[]{:S(2)}) collective-permute-start(bf16[64,1024]{1,0:T(8,128)(2,1)S(1)} %get-tuple-element.74), channel_id=1, source_target_pairs={{0,4},{8,24},{32,36},{40,56},{64,68},{72,88},{96,100},{104,120},{1... | collective-permute-start | bytes 393224 | tf_op jit(solution)/shard_map/ppermute | solution.py:374
  52.5 7.8 %collective-permute-start.17 = (bf16[64,1024]{1,0:T(8,128)(2,1)S(1)}, bf16[64,1024]{1,0:T(8,128)(2,1)S(1)}, u32[]{:S(2)}, u32[]{:S(2)}) collective-permute-start(bf16[64,1024]{1,0:T(8,128)(2,1)S(1)} %get-tuple-element.75), channel_id=1, source_target_pairs={{0,2},{8,9},{32,34},{40,41},{64,66},{72,73},{96,98},{104,105},{128... | collective-permute-start | bytes 393224 | tf_op jit(solution)/shard_map/ppermute | solution.py:374
  53.4 7.0 %collective-permute-start.18 = (bf16[64,1024]{1,0:T(8,128)(2,1)S(1)}, bf16[64,1024]{1,0:T(8,128)(2,1)S(1)}, u32[]{:S(2)}, u32[]{:S(2)}) collective-permute-start(bf16[64,1024]{1,0:T(8,128)(2,1)S(1)} %get-tuple-element.76), channel_id=1, source_target_pairs={{0,6},{8,25},{32,38},{40,57},{64,70},{72,89},{96,102},{104,121},{1... | collective-permute-start | bytes 393224 | tf_op jit(solution)/shard_map/ppermute | solution.py:374
  55.2 11.4 %collective-permute-start.14 = (bf16[64,1024]{1,0:T(8,128)(2,1)S(1)}, bf16[64,1024]{1,0:T(8,128)(2,1)S(1)}, u32[]{:S(2)}, u32[]{:S(2)}) collective-permute-start(bf16[64,1024]{1,0:T(8,128)(2,1)S(1)} %get-tuple-element.70), channel_id=1, source_target_pairs={{0,8},{1,9},{2,10},{3,11},{4,12},{5,13},{6,14},{7,15},{8,16},{9,17... | collective-permute-start | bytes 393224 | tf_op jit(solution)/shard_map/ppermute | solution.py:341
  58.0 8.6 %collective-permute-start.15 = (bf16[64,1024]{1,0:T(8,128)(2,1)S(1)}, bf16[64,1024]{1,0:T(8,128)(2,1)S(1)}, u32[]{:S(2)}, u32[]{:S(2)}) collective-permute-start(bf16[64,1024]{1,0:T(8,128)(2,1)S(1)} %get-tuple-element.71), channel_id=1, source_target_pairs={{0,1},{1,2},{2,3},{3,4},{4,5},{5,6},{6,7},{7,0},{8,9},{9,10},{10,1... | collective-permute-start | bytes 393224 | tf_op jit(solution)/shard_map/ppermute | solution.py:341
  58.2 8.4 %collective-permute-start.13 = (bf16[64,1024]{1,0:T(8,128)(2,1)S(1)}, bf16[64,1024]{1,0:T(8,128)(2,1)S(1)}, u32[]{:S(2)}, u32[]{:S(2)}) collective-permute-start(bf16[64,1024]{1,0:T(8,128)(2,1)S(1)} %get-tuple-element.69), channel_id=1, source_target_pairs={{0,9},{1,10},{2,11},{3,12},{4,13},{5,14},{6,15},{7,8},{8,17},{9,18... | collective-permute-start | bytes 393224 | tf_op jit(solution)/shard_map/ppermute | solution.py:341
  61.1 14.6 %all-to-all-start = ((bf16[16,4,1024]{2,1,0:T(4,128)(2,1)}), bf16[16,4,1024]{2,1,0:T(4,128)(2,1)S(1)}, u32[]{:S(2)}, u32[]{:S(2)}) async-start(bf16[16,4,1024]{2,1,0:T(4,128)(2,1)} %reshape.193), calls=%async_computation | async-start | bytes 262144 | tf_op jit(solution)/shard_map/all_to_all | solution.py:405
  (2 other events, 9.7 us)
